TPU v7x, 256 devices: a whole 4x4x8 slice. The times are simulated.
256 devices in a mesh: dp: 4 (over y), space: 64 (over z, x, core).
Axes of the slice: x: 4, y: 4, z: 8, core: 2. Of those that a mesh axis runs over, the one named last changes fastest.
Arguments:
- features: bfloat16 [4, 16384, 256], P('dp', 'space'), may hold values from -6 to 6
- neighbours: int32 [4, 27, 16384], P('dp', None, 'space'), may hold values from -1 to 16383, as said below
- parents: int32 [4, 16384], P('dp', 'space'), may hold values from 0 to 4095, as said below
- conv_first: bfloat16 [27, 256, 256], replicated, may hold values from -0.078125 to 0.078125
- conv_second: bfloat16 [27, 256, 256], replicated, may hold values from -0.078125 to 0.078125
- gain_first: float32 [256], replicated, may hold values from 0.1 to 1.9
- gain_second: float32 [256], replicated, may hold values from 0.1 to 1.9
- down_weight: bfloat16 [256, 512], replicated, may hold values from -0.375 to 0.375
- cotangent: bfloat16 [4, 4096, 512], P('dp', 'space'), may hold values from -6 to 6
Outputs:
- fine_out: bfloat16 [4, 16384, 256], P('dp', 'space')
- coarse: bfloat16 [4, 4096, 512], P('dp', 'space')
- down_grad: float32 [256, 512], replicated
Inputs may be any that keep to these rules, and one draw needn't show every extreme that they name: `neighbours`: for a site s of the block [d * 256, (d + 1) * 256), every entry is -1 or lies in [(d - 1) * 256, (d + 2) * 256); entry 13 is s itself. The parents of the sites of the block [d * 256, (d + 1) * 256) never decrease along the block and lie in [d * 64, (d + 2) * 64).
All inputs are finite; a program needn't handle non-finite values.
Results may differ from a plain program's by a relative error of at most 0.0057.
Values may be sent and summed in bfloat16 or wider, within the bound.
No kernel may reach another device: no remote copies, remote signals or barrier semaphores. Data moves between devices by JAX's collectives and lax.ppermute only.
A program may use at most 64 MiB of HBM per device.

v0:
```python
import math

import jax
import jax.numpy as jnp
from jax import lax
from jax.sharding import PartitionSpec as P


def extended(cells, sides, width):
    for axis, dim in sides:
        count = lax.axis_size(axis)
        ends = count - 1
        head = lax.slice_in_dim(cells, 0, width, axis=dim)
        tail = lax.slice_in_dim(cells, cells.shape[dim] - width, cells.shape[dim], axis=dim)
        cells = jnp.concatenate(
            [
                lax.ppermute(tail, axis, [(i, (i + 1) % count) for i in range(ends)]),
                cells,
                lax.ppermute(head, axis, [((i + 1) % count, i) for i in range(ends)]),
            ],
            axis=dim,
        )
    return cells


def from_behind(array, axis, by):
    length = lax.axis_size(axis)
    pairs = [(i, i + by) for i in range(length) if 0 <= i + by < length]
    return lax.ppermute(array, axis, pairs)


def convolve(field, tap_lists, weights):
    site_rows = field.shape[1]
    nearby = extended(field, (("space", 1),), site_rows)
    lowest = (lax.axis_index("space") - 1) * site_rows
    lookup = jnp.where(tap_lists < 0, 3 * site_rows, tap_lists - lowest)
    window_ids = jnp.arange(3 * site_rows, dtype=jnp.int32)

    def one_tap(running, inputs):
        rows_now, weight = inputs
        selector = (rows_now[:, :, None] == window_ids[None, None, :]).astype(jnp.bfloat16)
        picked = jnp.einsum(
            "wsr,wrc->wsc", selector, nearby, preferred_element_type=jnp.float32
        ).astype(jnp.bfloat16)
        return (
            running + jnp.einsum("wsc,cd->wsd", picked, weight, preferred_element_type=jnp.float32),
            None,
        )

    start = jnp.zeros((field.shape[0], site_rows, weights.shape[2]), jnp.float32)
    running, _ = lax.scan(one_tap, start, (jnp.moveaxis(lookup, 1, 0), weights))
    return running


def settle(running, gain):
    inverse = lax.rsqrt(jnp.mean(running * running, axis=-1, keepdims=True) + 1e-05)
    return jax.nn.silu(running * inverse * gain)


def body(
    features,
    neighbours,
    parents,
    conv_first,
    conv_second,
    gain_first,
    gain_second,
    down_weight,
    cotangent,
):
    middle = settle(convolve(features, neighbours, conv_first), gain_first).astype(jnp.bfloat16)
    fine_out = (
        features.astype(jnp.float32)
        + settle(convolve(middle, neighbours, conv_second), gain_second)
    ).astype(jnp.bfloat16)
    par_rows = cotangent.shape[1]
    owner_id = lax.axis_index("space")
    world_rows = features.shape[0]
    parent_ids = owner_id * par_rows + jnp.arange(2 * par_rows, dtype=jnp.int32)
    onehot = (parents[:, None, :] == parent_ids[None, :, None]).astype(jnp.bfloat16)
    partial_value = jnp.einsum("wps,wsc->wpc", onehot, fine_out, preferred_element_type=jnp.float32)
    tallies = jnp.sum(onehot.astype(jnp.float32), axis=2)
    moved = from_behind((partial_value[:, par_rows:], tallies[:, par_rows:]), "space", 1)
    parent_sums = partial_value[:, :par_rows] + moved[0]
    counts = tallies[:, :par_rows] + moved[1]
    pooled = (parent_sums / jnp.maximum(counts, 1.0)[:, :, None]).astype(jnp.bfloat16)
    coarse = jnp.einsum(
        "wpc,cd->wpd", pooled, down_weight, preferred_element_type=jnp.float32
    ).astype(jnp.bfloat16)
    local_grad = jnp.einsum("wpc,wpd->cd", pooled, cotangent, preferred_element_type=jnp.float32)
    worlds_all = world_rows * lax.axis_size("dp")
    parents_all = par_rows * lax.axis_size("space")
    down_grad = lax.psum(local_grad, ("dp", "space")) * (1.0 / math.sqrt(worlds_all * parents_all))
    return (fine_out, coarse, down_grad)


def solution(mesh):
    return jax.shard_map(
        body,
        mesh=mesh,
        in_specs=(
            P("dp", "space", None),
            P("dp", None, "space"),
            P("dp", "space"),
            P(),
            P(),
            P(),
            P(),
            P(),
            P("dp", "space", None),
        ),
        out_specs=(P("dp", "space", None), P("dp", "space", None), P()),
        check_vma=False,
    )
```

profile of v0, /device:TPU:1, one launch (start us, length us, event | category | flops | bytes accessed | tf_op | source)
XLA Modules:
  0.0 382.0 jit_solution(2045092295294285536)
XLA Ops:
  7.2 4.6 %collective-permute-start = (bf16[1,256,256]{2,1,0:T(8,128)(2,1)}, bf16[1,256,256]{2,1,0:T(8,128)(2,1)S(1)}, u32[]{:S(2)}, u32[]{:S(2)}) collective-permute-start(bf16[1,256,256]{2,1,0:T(8,128)(2,1)} %param.13), channel_id=1, source_target_pairs={{0,1},{1,2},{2,3},{3,4},{4,5},{5,6},{6,7},{7,8},{8,9},{9,10},{10,1... | collective-permute-start | bytes 393224 | tf_op jit(solution)/shard_map/ppermute | solution.py:17
  11.9 1.9 collective-permute-start.1
  14.7 3.7 collective-permute-done.1
  19.3 39.3 %while.22 = (s32[]{:T(128)}, f32[1,256,256]{2,1,0:T(8,128)S(1)}, s32[27,1,256]{2,1,0:T(1,128)S(1)}, bf16[1,768,256]{2,1,0:T(8,128)(2,1)S(1)}, bf16[27,256,256]{2,1,0:T(8,128)(2,1)}, /*index=5*/s32[]{:T(128)}, s32[]{:T(128)}) while((s32[]{:T(128)}, f32[1,256,256]{2,1,0:T(8,128)S(1)}, s32[27,1,256]{2,1,0:T(1,128)S(1)}, ...), condition=%wide.region_1.2_spmd.clone, body=%wide.region_0.1_spmd.clone.sunk | while | flops 134610944 | bytes 1052251 | solution.py:51
  19.4 1.4 fusion.50
  20.8 1.4 fusion.50
  22.3 1.4 fusion.50
  23.7 1.4 fusion.50
  25.2 1.4 fusion.50
  29.6 1.4 fusion.50
  31.0 1.4 fusion.50
  32.5 1.4 fusion.50
  33.9 1.4 fusion.50
  35.4 1.4 fusion.50
  59.0 1.9 collective-permute-start.2
  60.9 2.4 collective-permute-start.3
  63.6 3.2 collective-permute-start.5
  67.2 39.3 %while.23 = (s32[]{:T(128)}, f32[1,256,256]{2,1,0:T(8,128)S(1)}, s32[27,1,256]{2,1,0:T(1,128)S(1)}, bf16[1,768,256]{2,1,0:T(8,128)(2,1)S(1)}, bf16[27,256,256]{2,1,0:T(8,128)(2,1)}, /*index=5*/s32[]{:T(128)}, s32[]{:T(128)}) while((s32[]{:T(128)}, f32[1,256,256]{2,1,0:T(8,128)S(1)}, s32[27,1,256]{2,1,0:T(1,128)S(1)}, ...), condition=%wide.region_4.5_spmd.clone, body=%wide.region_3.4_spmd.clone.sunk | while | flops 134610944 | bytes 1052251 | solution.py:51
  67.3 1.4 fusion.54
  68.7 1.4 fusion.54
  70.2 1.4 fusion.54
  107.1 1.9 collective-permute-start.4
  112.3 260.9 %all-reduce.2.cloned.1.call-done = f32[256,512]{1,0:T(8,128)} async-done(((f32[256,512]{1,0:T(8,128)}), f32[256,512]{1,0:T(8,128)}) %all-reduce.2.cloned.1.call-update) | async-done | bytes 524304 | tf_op jit(solution)/shard_map/psum | solution.py:93
  373.2 1.9 broadcast_multiply_fusion
  (136 shorter events, 64.9 us)
Async XLA Ops:
  7.2 104.4 %copy-start = (bf16[256,512]{1,0:T(8,128)(2,1)S(1)}, bf16[256,512]{1,0:T(8,128)(2,1)}, u32[]{:S(2)}) copy-start(bf16[256,512]{1,0:T(8,128)(2,1)} %param.20) | copy-start | bytes 786436
  7.2 51.6 %copy-start.5 = (f32[256]{0:T(256)S(1)}, f32[256]{0:T(256)}, u32[]{:S(2)}) copy-start(f32[256]{0:T(256)} %param.18) | copy-start | bytes 3076
  7.2 56.2 %copy-start.4 = (s32[1,256]{1,0:T(1,128)S(1)}, s32[1,256]{1,0:T(1,128)}, u32[]{:S(2)}) copy-start(s32[1,256]{1,0:T(1,128)} %param.15) | copy-start | bytes 3076
  7.2 366.0 %all-reduce.2.cloned.1.call-start = ((), (), s32[]{:S(2)}) async-start(), calls=%async_computation | async-start | bytes 1048576 | tf_op jit(solution)/shard_map/psum | solution.py:93
  7.2 7.4 %collective-permute-start = (bf16[1,256,256]{2,1,0:T(8,128)(2,1)}, bf16[1,256,256]{2,1,0:T(8,128)(2,1)S(1)}, u32[]{:S(2)}, u32[]{:S(2)}) collective-permute-start(bf16[1,256,256]{2,1,0:T(8,128)(2,1)} %param.13), channel_id=1, source_target_pairs={{0,1},{1,2},{2,3},{3,4},{4,5},{5,6},{6,7},{7,8},{8,9},{9,10},{10,1... | collective-permute-start | bytes 393224 | tf_op jit(solution)/shard_map/ppermute | solution.py:17
  11.9 6.5 %collective-permute-start.1 = (bf16[1,256,256]{2,1,0:T(8,128)(2,1)}, bf16[1,256,256]{2,1,0:T(8,128)(2,1)S(1)}, u32[]{:S(2)}, u32[]{:S(2)}) collective-permute-start(bf16[1,256,256]{2,1,0:T(8,128)(2,1)} %param.13), channel_id=1, source_target_pairs={{1,0},{2,1},{3,2},{4,3},{5,4},{6,5},{7,6},{8,7},{9,8},{10,9},{11,1... | collective-permute-start | bytes 393224 | tf_op jit(solution)/shard_map/ppermute | solution.py:19
  58.7 48.0 %copy-start.2 = (bf16[1,256,256]{2,1,0:T(8,128)(2,1)S(1)}, bf16[1,256,256]{2,1,0:T(8,128)(2,1)}, u32[]{:S(2)}) copy-start(bf16[1,256,256]{2,1,0:T(8,128)(2,1)} %param.13) | copy-start | bytes 393220
  58.7 48.0 %copy-start.6 = (f32[256]{0:T(256)S(1)}, f32[256]{0:T(256)}, u32[]{:S(2)}) copy-start(f32[256]{0:T(256)} %param.19) | copy-start | bytes 3076
  59.0 7.8 %collective-permute-start.2 = (bf16[1,256,256]{2,1,0:T(8,128)(2,1)S(1)}, bf16[1,256,256]{2,1,0:T(8,128)(2,1)S(1)}, u32[]{:S(2)}, u32[]{:S(2)}) collective-permute-start(bf16[1,256,256]{2,1,0:T(8,128)(2,1)S(1)} %multiply_convert_fusion), channel_id=1, source_target_pairs={{0,1},{1,2},{2,3},{3,4},{4,5},{5,6},{6,7},{7,8},{8,9},{9,10},{10,1... | collective-permute-start | bytes 393224 | tf_op jit(solution)/shard_map/ppermute | solution.py:17
  60.9 6.3 %collective-permute-start.3 = (bf16[1,256,256]{2,1,0:T(8,128)(2,1)S(1)}, bf16[1,256,256]{2,1,0:T(8,128)(2,1)S(1)}, u32[]{:S(2)}, u32[]{:S(2)}) collective-permute-start(bf16[1,256,256]{2,1,0:T(8,128)(2,1)S(1)} %multiply_convert_fusion), channel_id=1, source_target_pairs={{1,0},{2,1},{3,2},{4,3},{5,4},{6,5},{7,6},{8,7},{9,8},{10,9},{11,1... | collective-permute-start | bytes 393224 | tf_op jit(solution)/shard_map/ppermute | solution.py:19
  63.6 45.5 %collective-permute-start.5 = (f32[1,64]{1,0:T(1,128)S(1)}, f32[1,64]{1,0:T(1,128)S(1)}, u32[]{:S(2)}, u32[]{:S(2)}) collective-permute-start(f32[1,64]{1,0:T(1,128)S(1)} %slice.15), channel_id=1, source_target_pairs={{0,1},{1,2},{2,3},{3,4},{4,5},{5,6},{6,7},{7,8},{8,9},{9,10},{10,1... | collective-permute-start | bytes 776 | tf_op jit(solution)/shard_map/ppermute | solution.py:29
  67.2 43.2 %copy-start.3 = (bf16[1,64,512]{2,1,0:T(8,128)(2,1)S(1)}, bf16[1,64,512]{2,1,0:T(8,128)(2,1)}, u32[]{:S(2)}) copy-start(bf16[1,64,512]{2,1,0:T(8,128)(2,1)} %param.21) | copy-start | bytes 196612
  106.9 268.2 %copy-start.1 = (bf16[1,256,256]{2,1,0:T(8,128)(2,1)}, bf16[1,256,256]{2,1,0:T(8,128)(2,1)S(1)}, u32[]{:S(2)}) copy-start(bf16[1,256,256]{2,1,0:T(8,128)(2,1)S(1)} %add_convert_fusion) | copy-start | bytes 393220
  107.1 3.2 collective-permute-start.4
Sparse Core Ops, SparseCore 0:
  111.7 261.5 all-reduce.1
where the time goes:
time: 384 us; the launch traced here: 382 us
  waiting for transfers between devices  266 us (69%)
  matrix products  78.4 us (20%)
  starting transfers between devices  16 us (4%)
  between operations  14.3 us (4%)
  other arithmetic  4.42 us (1%)
    psum x1, waiting for transfers between devices, body(): lax.psum(local_grad, ('dp', 'space'))  261 us
    dot_general x54, matrix products, one_tap(): jnp.einsum('wsc,cd->wsd', picked, weight, preferred_element_type=jnp.floa...  76.4 us
  transfers between devices with their start and end apart: 7, of which 4 were waited for; matrix products, arithmetic and copies ran while one was open for 11% of the time, Pallas kernels for 0%

commit v1 on v0

--- a/solution.py
+++ b/solution.py
@@ -3,7 +3,18 @@
 import jax
 import jax.numpy as jnp
 from jax import lax
+from jax.sharding import Mesh
 from jax.sharding import PartitionSpec as P
+
+
+DP = "y"
+SPACE = ("z", "x", "core")
+PLANE = ("y", "x", "core")
+
+
+def split_mesh(mesh):
+    dp, space = mesh.devices.shape
+    return Mesh(mesh.devices.reshape(dp, space // 8, 4, 2), (DP,) + SPACE)
 
 
 def extended(cells, sides, width):
@@ -31,8 +42,8 @@
 
 def convolve(field, tap_lists, weights):
     site_rows = field.shape[1]
-    nearby = extended(field, (("space", 1),), site_rows)
-    lowest = (lax.axis_index("space") - 1) * site_rows
+    nearby = extended(field, ((SPACE, 1),), site_rows)
+    lowest = (lax.axis_index(SPACE) - 1) * site_rows
     lookup = jnp.where(tap_lists < 0, 3 * site_rows, tap_lists - lowest)
     window_ids = jnp.arange(3 * site_rows, dtype=jnp.int32)
 
@@ -57,6 +68,21 @@
     return jax.nn.silu(running * inverse * gain)
 
 
+def exchanged(pieces, axes):
+    return lax.all_to_all(pieces, axes, 0, 0, tiled=True)
+
+
+def reduced(local_grad, scale):
+    rows, cols = local_grad.shape
+    plane = lax.axis_size(PLANE)
+    parts = local_grad.astype(jnp.bfloat16).reshape(plane, rows // plane, cols)
+    part = jnp.sum(exchanged(parts, PLANE).astype(jnp.float32), axis=0)
+    copies = jnp.broadcast_to(part[None], (lax.axis_size("z"),) + part.shape)
+    part = jnp.sum(exchanged(copies, "z"), axis=0) * scale
+    copies = jnp.broadcast_to(part.astype(jnp.bfloat16)[None], (plane,) + part.shape)
+    return exchanged(copies, PLANE).astype(jnp.float32).reshape(rows, cols)
+
+
 def body(
     features,
     neighbours,
@@ -74,13 +100,13 @@
         + settle(convolve(middle, neighbours, conv_second), gain_second)
     ).astype(jnp.bfloat16)
     par_rows = cotangent.shape[1]
-    owner_id = lax.axis_index("space")
+    owner_id = lax.axis_index(SPACE)
     world_rows = features.shape[0]
     parent_ids = owner_id * par_rows + jnp.arange(2 * par_rows, dtype=jnp.int32)
     onehot = (parents[:, None, :] == parent_ids[None, :, None]).astype(jnp.bfloat16)
     partial_value = jnp.einsum("wps,wsc->wpc", onehot, fine_out, preferred_element_type=jnp.float32)
     tallies = jnp.sum(onehot.astype(jnp.float32), axis=2)
-    moved = from_behind((partial_value[:, par_rows:], tallies[:, par_rows:]), "space", 1)
+    moved = from_behind((partial_value[:, par_rows:], tallies[:, par_rows:]), SPACE, 1)
     parent_sums = partial_value[:, :par_rows] + moved[0]
     counts = tallies[:, :par_rows] + moved[1]
     pooled = (parent_sums / jnp.maximum(counts, 1.0)[:, :, None]).astype(jnp.bfloat16)
@@ -88,27 +114,27 @@
         "wpc,cd->wpd", pooled, down_weight, preferred_element_type=jnp.float32
     ).astype(jnp.bfloat16)
     local_grad = jnp.einsum("wpc,wpd->cd", pooled, cotangent, preferred_element_type=jnp.float32)
-    worlds_all = world_rows * lax.axis_size("dp")
-    parents_all = par_rows * lax.axis_size("space")
-    down_grad = lax.psum(local_grad, ("dp", "space")) * (1.0 / math.sqrt(worlds_all * parents_all))
+    worlds_all = world_rows * lax.axis_size(DP)
+    parents_all = par_rows * lax.axis_size(SPACE)
+    down_grad = reduced(local_grad, 1.0 / math.sqrt(worlds_all * parents_all))
     return (fine_out, coarse, down_grad)
 
 
 def solution(mesh):
     return jax.shard_map(
         body,
-        mesh=mesh,
+        mesh=split_mesh(mesh),
         in_specs=(
-            P("dp", "space", None),
-            P("dp", None, "space"),
-            P("dp", "space"),
+            P(DP, SPACE, None),
+            P(DP, None, SPACE),
+            P(DP, SPACE),
             P(),
             P(),
             P(),
             P(),
             P(),
-            P("dp", "space", None),
+            P(DP, SPACE, None),
         ),
-        out_specs=(P("dp", "space", None), P("dp", "space", None), P()),
+        out_specs=(P(DP, SPACE, None), P(DP, SPACE, None), P()),
         check_vma=False,
     )

time: 384 us -> 162 us (0.42)
  waiting for transfers between devices: 266 us -> 13.7 us
  blocking collectives: 0 us -> 40.7 us
  between operations: 14.3 us -> 0.96 us
  starting transfers between devices: 16 us -> 21.3 us
    psum x1 -> x0, waiting for transfers between devices: 261 us -> none  [body(): lax.psum(local_grad, ('dp', 'space'))]
    all_to_all x0 -> x2, blocking collectives: none -> 40.7 us  [exchanged(): return lax.all_to_all(pieces, axes, 0, 0, tiled=True)]
    all_to_all x0 -> x1, waiting for transfers between devices: none -> 8.2 us  [exchanged(): return lax.all_to_all(pieces, axes, 0, 0, tiled=True)]
    all_to_all x0 -> x1, starting transfers between devices: none -> 5.35 us  [exchanged(): return lax.all_to_all(pieces, axes, 0, 0, tiled=True)]
  transfers between devices with their start and end apart: 7 -> 7, of which waited for: 4 -> 4; matrix products, arithmetic and copies ran while one was open for 11% -> 25% of each run, Pallas kernels for 0% -> 0%
where the time goes in v1:
time: 162 us; the launch traced here: 161 us
  matrix products  77.7 us (48%)
  blocking collectives  40.7 us (25%)
  starting transfers between devices  21.3 us (13%)
  waiting for transfers between devices  13.7 us (8%)
  other arithmetic  3.47 us (2%)
  loops' own time  1.87 us (1%)
    dot_general x54, matrix products, one_tap(): jnp.einsum('wsc,cd->wsd', picked, weight, preferred_element_type=jnp.floa...  76.4 us
    all_to_all x2, blocking collectives, exchanged(): return lax.all_to_all(pieces, axes, 0, 0, tiled=True)  40.7 us
    all_to_all x1, waiting for transfers between devices, exchanged(): return lax.all_to_all(pieces, axes, 0, 0, tiled=True)  8.2 us
    ppermute x2, starting transfers between devices, extended(): lax.ppermute(tail, axis, [(i, (i + 1) % count) for i in range(ends)])  6.56 us
    all_to_all x1, starting transfers between devices, exchanged(): return lax.all_to_all(pieces, axes, 0, 0, tiled=True)  5.35 us
    ppermute x2, starting transfers between devices, from_behind(): return lax.ppermute(array, axis, pairs)  5.07 us
    ppermute x2, starting transfers between devices, extended(): lax.ppermute(head, axis, [((i + 1) % count, i) for i in range(ends)])  4.35 us
    ppermute x2, waiting for transfers between devices, extended(): lax.ppermute(head, axis, [((i + 1) % count, i) for i in range(ends)])  4.15 us
  transfers between devices with their start and end apart: 7, of which 4 were waited for; matrix products, arithmetic and copies ran while one was open for 25% of the time, Pallas kernels for 0%

profile of v1, /device:TPU:1, one launch (start us, length us, event | category | flops | bytes accessed | tf_op | source)
XLA Modules:
  0.0 160.9 jit_solution(5228621938075770547)
XLA Ops:
  0.7 4.6 %collective-permute-start = (bf16[1,256,256]{2,1,0:T(8,128)(2,1)}, bf16[1,256,256]{2,1,0:T(8,128)(2,1)S(1)}, u32[]{:S(2)}, u32[]{:S(2)}) collective-permute-start(bf16[1,256,256]{2,1,0:T(8,128)(2,1)} %param.13), channel_id=1, source_target_pairs={{0,1},{1,2},{2,3},{3,4},{4,5},{5,6},{6,7},{7,8},{8,9},{9,10},{10,1... | collective-permute-start | bytes 393224 | tf_op jit(solution)/shard_map/ppermute | solution.py:28
  5.3 1.9 %collective-permute-start.1 = (bf16[1,256,256]{2,1,0:T(8,128)(2,1)}, bf16[1,256,256]{2,1,0:T(8,128)(2,1)S(1)}, u32[]{:S(2)}, u32[]{:S(2)}) collective-permute-start(bf16[1,256,256]{2,1,0:T(8,128)(2,1)} %param.13), channel_id=1, source_target_pairs={{1,0},{2,1},{3,2},{4,3},{5,4},{6,5},{7,6},{8,7},{9,8},{10,9},{11,1... | collective-permute-start | bytes 393224 | tf_op jit(solution)/shard_map/ppermute | solution.py:30
  8.1 3.7 %collective-permute-done.1 = bf16[1,256,256]{2,1,0:T(8,128)(2,1)S(1)} collective-permute-done((bf16[1,256,256]{2,1,0:T(8,128)(2,1)}, bf16[1,256,256]{2,1,0:T(8,128)(2,1)S(1)}, u32[]{:S(2)}, u32[]{:S(2)}) %collective-permute-start.1) | collective-permute-done | bytes 131104 | tf_op jit(solution)/shard_map/ppermute | solution.py:30
  12.8 39.3 %while.22 = (s32[]{:T(128)}, f32[1,256,256]{2,1,0:T(8,128)S(1)}, s32[27,1,256]{2,1,0:T(1,128)S(1)}, bf16[1,768,256]{2,1,0:T(8,128)(2,1)S(1)}, bf16[27,256,256]{2,1,0:T(8,128)(2,1)}, /*index=5*/s32[]{:T(128)}, s32[]{:T(128)}) while((s32[]{:T(128)}, f32[1,256,256]{2,1,0:T(8,128)S(1)}, s32[27,1,256]{2,1,0:T(1,128)S(1)}, ...), condition=%wide.region_1.2_spmd.clone, body=%wide.region_0.1_spmd.clone.sunk | while | flops 134610944 | bytes 1052251 | solution.py:62
  12.8 1.4 fusion.50
  14.2 1.4 fusion.50
  15.7 1.4 fusion.50
  17.2 1.4 fusion.50
  20.1 1.4 fusion.50
  21.5 1.4 fusion.50
  23.0 1.4 fusion.50
  24.4 1.4 fusion.50
  25.9 1.4 fusion.50
  52.4 1.9 %collective-permute-start.2 = (bf16[1,256,256]{2,1,0:T(8,128)(2,1)S(1)}, bf16[1,256,256]{2,1,0:T(8,128)(2,1)S(1)}, u32[]{:S(2)}, u32[]{:S(2)}) collective-permute-start(bf16[1,256,256]{2,1,0:T(8,128)(2,1)S(1)} %multiply_convert_fusion), channel_id=1, source_target_pairs={{0,1},{1,2},{2,3},{3,4},{4,5},{5,6},{6,7},{7,8},{8,9},{9,10},{10,1... | collective-permute-start | bytes 393224 | tf_op jit(solution)/shard_map/ppermute | solution.py:28
  54.3 2.4 %collective-permute-start.3 = (bf16[1,256,256]{2,1,0:T(8,128)(2,1)S(1)}, bf16[1,256,256]{2,1,0:T(8,128)(2,1)S(1)}, u32[]{:S(2)}, u32[]{:S(2)}) collective-permute-start(bf16[1,256,256]{2,1,0:T(8,128)(2,1)S(1)} %multiply_convert_fusion), channel_id=1, source_target_pairs={{1,0},{2,1},{3,2},{4,3},{5,4},{6,5},{7,6},{8,7},{9,8},{10,9},{11,1... | collective-permute-start | bytes 393224 | tf_op jit(solution)/shard_map/ppermute | solution.py:30
  57.0 3.2 %collective-permute-start.5 = (f32[1,64]{1,0:T(1,128)S(1)}, f32[1,64]{1,0:T(1,128)S(1)}, u32[]{:S(2)}, u32[]{:S(2)}) collective-permute-start(f32[1,64]{1,0:T(1,128)S(1)} %slice.15), channel_id=1, source_target_pairs={{0,1},{1,2},{2,3},{3,4},{4,5},{5,6},{6,7},{7,8},{8,9},{9,10},{10,1... | collective-permute-start | bytes 776 | tf_op jit(solution)/shard_map/ppermute | solution.py:40
  60.7 39.3 %while.23 = (s32[]{:T(128)}, f32[1,256,256]{2,1,0:T(8,128)S(1)}, s32[27,1,256]{2,1,0:T(1,128)S(1)}, bf16[1,768,256]{2,1,0:T(8,128)(2,1)S(1)}, bf16[27,256,256]{2,1,0:T(8,128)(2,1)}, /*index=5*/s32[]{:T(128)}, s32[]{:T(128)}) while((s32[]{:T(128)}, f32[1,256,256]{2,1,0:T(8,128)S(1)}, s32[27,1,256]{2,1,0:T(1,128)S(1)}, ...), condition=%wide.region_4.5_spmd.clone, body=%wide.region_3.4_spmd.clone.sunk | while | flops 134610944 | bytes 1052251 | solution.py:62
  60.7 1.4 fusion.54
  62.2 1.4 fusion.54
  100.6 1.9 %collective-permute-start.4 = (f32[1,64,256]{2,1,0:T(8,128)S(1)}, f32[1,64,256]{2,1,0:T(8,128)S(1)}, u32[]{:S(2)}, u32[]{:S(2)}) collective-permute-start(f32[1,64,256]{2,1,0:T(8,128)S(1)} %slice.17), channel_id=1, source_target_pairs={{0,1},{1,2},{2,3},{3,4},{4,5},{5,6},{6,7},{7,8},{8,9},{9,10},{10,1... | collective-permute-start | bytes 196616 | tf_op jit(solution)/shard_map/ppermute | solution.py:40
  104.1 20.2 %all_to_all.15 = bf16[32,8,512]{2,1,0:T(8,128)(2,1)S(1)} all-to-all(bf16[32,8,512]{2,1,0:T(8,128)(2,1)S(1)} %fusion.26), channel_id=1, replica_groups=mesh['y'=4,'z'=8,'x'=4,'core'=2] {'y','x','core'}, dimensions={0} | all-to-all | bytes 524288 | tf_op jit(solution)/shard_map/all_to_all | solution.py:72
  124.4 20.5 %all_to_all.16 = f32[8,8,512]{2,1,0:T(8,128)S(1)} all-to-all(f32[8,8,512]{2,1,0:T(8,128)S(1)} %broadcast_in_dim.14), channel_id=1, replica_groups=mesh['y'=4,'z'=8,'x'=4,'core'=2] {'z'}, dimensions={0} | all-to-all | bytes 262144 | tf_op jit(solution)/shard_map/all_to_all | solution.py:72
  145.7 5.4 %all-to-all-start.2 = ((bf16[32,8,512]{2,1,0:T(8,128)(2,1)}), bf16[32,8,512]{2,1,0:T(8,128)(2,1)S(1)}, u32[]{:S(2)}, u32[]{:S(2)}) async-start(bf16[32,8,512]{2,1,0:T(8,128)(2,1)} %broadcast_in_dim.15), calls=%async_computation.2 | async-start | bytes 524288 | tf_op jit(solution)/shard_map/all_to_all | solution.py:72
  151.9 8.2 %all-to-all-done.2 = bf16[32,8,512]{2,1,0:T(8,128)(2,1)S(1)} async-done(((bf16[32,8,512]{2,1,0:T(8,128)(2,1)}), bf16[32,8,512]{2,1,0:T(8,128)(2,1)S(1)}, u32[]{:S(2)}, u32[]{:S(2)}) %all-to-all-start.2) | async-done | bytes 262176 | tf_op jit(solution)/shard_map/all_to_all | solution.py:72
  (142 shorter events, 68.5 us)
Async XLA Ops:
  0.6 150.4 %copy-start = (bf16[256,512]{1,0:T(8,128)(2,1)S(1)}, bf16[256,512]{1,0:T(8,128)(2,1)}, u32[]{:S(2)}) copy-start(bf16[256,512]{1,0:T(8,128)(2,1)} %param.20) | copy-start | bytes 786436
  0.6 51.6 %copy-start.5 = (f32[256]{0:T(256)S(1)}, f32[256]{0:T(256)}, u32[]{:S(2)}) copy-start(f32[256]{0:T(256)} %param.18) | copy-start | bytes 3076
  0.7 56.1 %copy-start.4 = (s32[1,256]{1,0:T(1,128)S(1)}, s32[1,256]{1,0:T(1,128)}, u32[]{:S(2)}) copy-start(s32[1,256]{1,0:T(1,128)} %param.15) | copy-start | bytes 3076
  0.7 7.4 %collective-permute-start = (bf16[1,256,256]{2,1,0:T(8,128)(2,1)}, bf16[1,256,256]{2,1,0:T(8,128)(2,1)S(1)}, u32[]{:S(2)}, u32[]{:S(2)}) collective-permute-start(bf16[1,256,256]{2,1,0:T(8,128)(2,1)} %param.13), channel_id=1, source_target_pairs={{0,1},{1,2},{2,3},{3,4},{4,5},{5,6},{6,7},{7,8},{8,9},{9,10},{10,1... | collective-permute-start | bytes 393224 | tf_op jit(solution)/shard_map/ppermute | solution.py:28
  5.3 6.5 %collective-permute-start.1 = (bf16[1,256,256]{2,1,0:T(8,128)(2,1)}, bf16[1,256,256]{2,1,0:T(8,128)(2,1)S(1)}, u32[]{:S(2)}, u32[]{:S(2)}) collective-permute-start(bf16[1,256,256]{2,1,0:T(8,128)(2,1)} %param.13), channel_id=1, source_target_pairs={{1,0},{2,1},{3,2},{4,3},{5,4},{6,5},{7,6},{8,7},{9,8},{10,9},{11,1... | collective-permute-start | bytes 393224 | tf_op jit(solution)/shard_map/ppermute | solution.py:30
  52.1 48.0 %copy-start.2 = (bf16[1,256,256]{2,1,0:T(8,128)(2,1)S(1)}, bf16[1,256,256]{2,1,0:T(8,128)(2,1)}, u32[]{:S(2)}) copy-start(bf16[1,256,256]{2,1,0:T(8,128)(2,1)} %param.13) | copy-start | bytes 393220
  52.1 48.0 %copy-start.6 = (f32[256]{0:T(256)S(1)}, f32[256]{0:T(256)}, u32[]{:S(2)}) copy-start(f32[256]{0:T(256)} %param.19) | copy-start | bytes 3076
  52.4 7.8 %collective-permute-start.2 = (bf16[1,256,256]{2,1,0:T(8,128)(2,1)S(1)}, bf16[1,256,256]{2,1,0:T(8,128)(2,1)S(1)}, u32[]{:S(2)}, u32[]{:S(2)}) collective-permute-start(bf16[1,256,256]{2,1,0:T(8,128)(2,1)S(1)} %multiply_convert_fusion), channel_id=1, source_target_pairs={{0,1},{1,2},{2,3},{3,4},{4,5},{5,6},{6,7},{7,8},{8,9},{9,10},{10,1... | collective-permute-start | bytes 393224 | tf_op jit(solution)/shard_map/ppermute | solution.py:28
  54.3 6.3 %collective-permute-start.3 = (bf16[1,256,256]{2,1,0:T(8,128)(2,1)S(1)}, bf16[1,256,256]{2,1,0:T(8,128)(2,1)S(1)}, u32[]{:S(2)}, u32[]{:S(2)}) collective-permute-start(bf16[1,256,256]{2,1,0:T(8,128)(2,1)S(1)} %multiply_convert_fusion), channel_id=1, source_target_pairs={{1,0},{2,1},{3,2},{4,3},{5,4},{6,5},{7,6},{8,7},{9,8},{10,9},{11,1... | collective-permute-start | bytes 393224 | tf_op jit(solution)/shard_map/ppermute | solution.py:30
  57.0 45.5 %collective-permute-start.5 = (f32[1,64]{1,0:T(1,128)S(1)}, f32[1,64]{1,0:T(1,128)S(1)}, u32[]{:S(2)}, u32[]{:S(2)}) collective-permute-start(f32[1,64]{1,0:T(1,128)S(1)} %slice.15), channel_id=1, source_target_pairs={{0,1},{1,2},{2,3},{3,4},{4,5},{5,6},{6,7},{7,8},{8,9},{9,10},{10,1... | collective-permute-start | bytes 776 | tf_op jit(solution)/shard_map/ppermute | solution.py:40
  60.7 43.2 %copy-start.3 = (bf16[1,64,512]{2,1,0:T(8,128)(2,1)S(1)}, bf16[1,64,512]{2,1,0:T(8,128)(2,1)}, u32[]{:S(2)}) copy-start(bf16[1,64,512]{2,1,0:T(8,128)(2,1)} %param.21) | copy-start | bytes 196612
  100.3 60.6 %copy-start.1 = (bf16[1,256,256]{2,1,0:T(8,128)(2,1)}, bf16[1,256,256]{2,1,0:T(8,128)(2,1)S(1)}, u32[]{:S(2)}) copy-start(bf16[1,256,256]{2,1,0:T(8,128)(2,1)S(1)} %add_convert_fusion) | copy-start | bytes 393220
  100.6 3.2 %collective-permute-start.4 = (f32[1,64,256]{2,1,0:T(8,128)S(1)}, f32[1,64,256]{2,1,0:T(8,128)S(1)}, u32[]{:S(2)}, u32[]{:S(2)}) collective-permute-start(f32[1,64,256]{2,1,0:T(8,128)S(1)} %slice.17), channel_id=1, source_target_pairs={{0,1},{1,2},{2,3},{3,4},{4,5},{5,6},{6,7},{7,8},{8,9},{9,10},{10,1... | collective-permute-start | bytes 196616 | tf_op jit(solution)/shard_map/ppermute | solution.py:40
  145.7 14.4 %all-to-all-start.2 = ((bf16[32,8,512]{2,1,0:T(8,128)(2,1)}), bf16[32,8,512]{2,1,0:T(8,128)(2,1)S(1)}, u32[]{:S(2)}, u32[]{:S(2)}) async-start(bf16[32,8,512]{2,1,0:T(8,128)(2,1)} %broadcast_in_dim.15), calls=%async_computation.2 | async-start | bytes 524288 | tf_op jit(solution)/shard_map/all_to_all | solution.py:72

commit v2 on v1

v2 whole, which is shorter than its diff:
```python
import functools
import math

import jax
import jax.numpy as jnp
from jax import lax
from jax.experimental import pallas as pl
from jax.experimental.pallas import tpu as pltpu
from jax.sharding import Mesh
from jax.sharding import PartitionSpec as P


DP = "y"
SPACE = ("z", "x", "core")
PLANE = ("y", "x", "core")
GROUP = 3
VMEM_BYTES = 40 << 20


def split_mesh(mesh):
    dp, space = mesh.devices.shape
    return Mesh(mesh.devices.reshape(dp, space // 8, 4, 2), (DP,) + SPACE)


def shifted(array, by):
    length = lax.axis_size(SPACE)
    return lax.ppermute(array, SPACE, [(i, (i + by) % length) for i in range(length)])


def settled(running, gain):
    inverse = lax.rsqrt(jnp.mean(running * running, axis=-1, keepdims=True) + 1e-05)
    scaled = running * inverse * gain
    return scaled / (1.0 + jnp.exp(-scaled))


def convolved(taps_ref, blocks, weight_ref, select_ref, picked_ref):
    taps, rows = taps_ref.shape
    chans = picked_ref.shape[1] // taps
    window = 3 * rows
    lowest = (lax.axis_index(SPACE) - 1) * rows
    ids = taps_ref[...]
    local = jnp.where(ids < 0, -1, ids - lowest)
    local = jnp.concatenate([local, jnp.full((-taps % 8, rows), -1, jnp.int32)], axis=0).T
    places = lax.broadcasted_iota(jnp.int16, (rows, window), 1)
    for tap in range(taps):
        wanted = jnp.broadcast_to(local[:, tap : tap + 1], (rows, 128)).astype(jnp.int16)
        wanted = jnp.concatenate([wanted] * (window // 128), axis=1)
        select_ref[tap * rows : (tap + 1) * rows] = jnp.where(
            wanted == places, jnp.ones((), jnp.bfloat16), jnp.zeros((), jnp.bfloat16)
        )
    for first in range(0, taps, GROUP):
        part = select_ref[first * rows : (first + GROUP) * rows]
        picked = sum(
            jnp.dot(
                part[:, b * rows : (b + 1) * rows], block[...], preferred_element_type=jnp.float32
            )
            for b, block in enumerate(blocks)
        ).astype(jnp.bfloat16)
        for j in range(GROUP):
            picked_ref[:, (first + j) * chans : (first + j + 1) * chans] = picked[j * rows : (j + 1) * rows]
    return jnp.dot(
        picked_ref[...],
        weight_ref[...].reshape(taps * chans, weight_ref.shape[2]),
        preferred_element_type=jnp.float32,
    )


def first_kernel(before, here, after, taps_ref, gain_ref, weight_ref, out, select_ref, picked_ref):
    product = convolved(taps_ref, (before, here, after), weight_ref, select_ref, picked_ref)
    out[...] = settled(product, gain_ref[...]).astype(out.dtype)


def second_kernel(
    before, here, after, taps_ref, gain_ref, weight_ref, feature_ref, parent_ref,
    fine_ref, own_ref, sent_ref, select_ref, picked_ref,
):
    product = convolved(taps_ref, (before, here, after), weight_ref, select_ref, picked_ref)
    fine = feature_ref[...].astype(jnp.float32) + settled(product, gain_ref[...])
    fine = fine.astype(fine_ref.dtype)
    fine_ref[...] = fine
    half, chans = own_ref.shape[0], fine.shape[1]
    ids = parent_ref[...] - lax.axis_index(SPACE) * half
    member = lax.broadcasted_iota(jnp.int32, (2 * half, fine.shape[0]), 0) == ids
    member = member.astype(jnp.float32)
    sums = jnp.dot(member.astype(jnp.bfloat16), fine, preferred_element_type=jnp.float32)
    counts = jnp.broadcast_to(jnp.sum(member, axis=1, keepdims=True), (2 * half, 128))
    own_ref[:, :chans] = sums[:half]
    own_ref[:, chans:] = counts[:half]
    sent_ref[:, :chans] = sums[half:]
    sent_ref[:, chans:] = counts[half:]


def coarse_kernel(own_ref, moved_ref, down_ref, cotangent_ref, coarse_ref, grad_ref):
    total = own_ref[...] + moved_ref[...]
    chans = down_ref.shape[0]
    counts = jnp.maximum(total[:, chans : chans + 1], 1.0)
    pooled = (total[:, :chans] / counts).astype(jnp.bfloat16)
    coarse_ref[...] = jnp.dot(pooled, down_ref[...], preferred_element_type=jnp.float32).astype(coarse_ref.dtype)
    grad_ref[...] = lax.dot_general(
        pooled, cotangent_ref[...], (((0,), (0,)), ((), ())), preferred_element_type=jnp.float32
    ).astype(grad_ref.dtype)


def in_vmem(kernel, outs, inputs, scratch=(), name=None):
    vmem = pl.BlockSpec(memory_space=pltpu.VMEM)
    return pl.pallas_call(
        kernel,
        out_shape=outs,
        in_specs=[vmem] * len(inputs),
        out_specs=jax.tree.map(lambda _: vmem, outs),
        scratch_shapes=scratch,
        compiler_params=pltpu.CompilerParams(vmem_limit_bytes=VMEM_BYTES),
        name=name,
    )(*inputs)


def exchanged(pieces, axes):
    return lax.all_to_all(pieces, axes, 0, 0, tiled=True)


def reduced(local_grad, scale):
    rows, cols = local_grad.shape
    plane = lax.axis_size(PLANE)
    parts = local_grad.reshape(plane, rows // plane, cols)
    part = jnp.sum(exchanged(parts, PLANE).astype(jnp.float32), axis=0)
    copies = jnp.broadcast_to(part[None], (lax.axis_size("z"),) + part.shape)
    part = jnp.sum(exchanged(copies, "z"), axis=0) * scale
    copies = jnp.broadcast_to(part.astype(jnp.bfloat16)[None], (plane,) + part.shape)
    return exchanged(copies, PLANE).astype(jnp.float32).reshape(rows, cols)


def body(
    features,
    neighbours,
    parents,
    conv_first,
    conv_second,
    gain_first,
    gain_second,
    down_weight,
    cotangent,
):
    field, taps_ids, grad_in = features[0], neighbours[0], cotangent[0]
    taps, rows = taps_ids.shape
    chans = field.shape[1]
    par_rows, out_chans = grad_in.shape
    bf16 = functools.partial(jax.ShapeDtypeStruct, dtype=jnp.bfloat16)
    f32 = functools.partial(jax.ShapeDtypeStruct, dtype=jnp.float32)
    scratch = [
        pltpu.VMEM((taps * rows, 3 * rows), jnp.bfloat16),
        pltpu.VMEM((rows, taps * chans), jnp.bfloat16),
    ]
    middle = in_vmem(
        first_kernel,
        bf16((rows, chans)),
        (shifted(field, 1), field, shifted(field, -1), taps_ids, gain_first[None], conv_first),
        scratch,
        "first_conv",
    )
    fine, own, sent = in_vmem(
        second_kernel,
        (bf16((rows, chans)), f32((par_rows, chans + 128)), f32((par_rows, chans + 128))),
        (
            shifted(middle, 1), middle, shifted(middle, -1), taps_ids, gain_second[None], conv_second,
            field, parents,
        ),
        scratch,
        "second_conv",
    )
    coarse, local_grad = in_vmem(
        coarse_kernel,
        (bf16((par_rows, out_chans)), bf16((chans, out_chans))),
        (own, shifted(sent, 1), down_weight, grad_in),
        name="coarse",
    )
    worlds_all = lax.axis_size(DP)
    parents_all = par_rows * lax.axis_size(SPACE)
    down_grad = reduced(local_grad, 1.0 / math.sqrt(worlds_all * parents_all))
    return (fine[None], coarse[None], down_grad)


def solution(mesh):
    return jax.shard_map(
        body,
        mesh=split_mesh(mesh),
        in_specs=(
            P(DP, SPACE, None),
            P(DP, None, SPACE),
            P(DP, SPACE),
            P(),
            P(),
            P(),
            P(),
            P(),
            P(DP, SPACE, None),
        ),
        out_specs=(P(DP, SPACE, None), P(DP, SPACE, None), P()),
        check_vma=False,
    )
```

time: 162 us -> 85.9 us (0.53)
  matrix products: 77.7 us -> 0 us
  Pallas kernels: 0 us -> 10.2 us
  starting transfers between devices: 21.3 us -> 12.7 us
  blocking collectives: 40.7 us -> 44.5 us
  local copies, waits for them, and re-layouts: 1.25 us -> 4.39 us
  other arithmetic: 3.47 us -> 0.92 us
  loops' own time: 1.87 us -> 0 us
    dot_general x57 -> x0, matrix products: 77.7 us -> none  [the longest x54 76.4 us: one_tap(): jnp.einsum('wsc,cd->wsd', picked, weight, preferred_element_type=jnp.floa...]
    pallas_call x0 -> x3, Pallas kernels: none -> 10.2 us  [in_vmem(): pl.pallas_call(kernel, out_shape=outs, in_specs=[vmem] * len(inputs), out...]
    all_to_all x1 -> x0, waiting for transfers between devices: 8.2 us -> none  [exchanged(): return lax.all_to_all(pieces, axes, 0, 0, tiled=True)]
    ppermute x6 -> x5, waiting for transfers between devices: 5.45 us -> 12.2 us  [shifted(): lax.ppermute(array, SPACE, [(i, (i + by) % length) for i in range(length)])]
    all_to_all x1 -> x0, starting transfers between devices: 5.35 us -> none  [exchanged(): return lax.all_to_all(pieces, axes, 0, 0, tiled=True)]
    unnamed x14 -> x19, local copies, waits for them, and re-layouts: 0.04 us -> 4.36 us
    all_to_all x2 -> x3, blocking collectives: 40.7 us -> 44.5 us  [exchanged(): return lax.all_to_all(pieces, axes, 0, 0, tiled=True)]
    ppermute x6 -> x5, starting transfers between devices: 16 us -> 12.7 us  [shifted(): lax.ppermute(array, SPACE, [(i, (i + by) % length) for i in range(length)])]
  transfers between devices with their start and end apart: 7 -> 5, of which waited for: 4 -> 5; matrix products, arithmetic and copies ran while one was open for 25% -> 1% of each run, Pallas kernels for 0% -> 0%
where the time goes in v2:
time: 85.9 us; the launch traced here: 85.6 us
  blocking collectives  44.5 us (52%)
  starting transfers between devices  12.7 us (15%)
  waiting for transfers between devices  12.2 us (14%)
  Pallas kernels  10.2 us (12%)
  local copies, waits for them, and re-layouts  4.39 us (5%)
  other arithmetic  0.92 us (1%)
    all_to_all x3, blocking collectives, exchanged(): return lax.all_to_all(pieces, axes, 0, 0, tiled=True)  44.5 us
    ppermute x5, starting transfers between devices, shifted(): lax.ppermute(array, SPACE, [(i, (i + by) % length) for i in range(length)])  12.7 us
    ppermute x5, waiting for transfers between devices, shifted(): lax.ppermute(array, SPACE, [(i, (i + by) % length) for i in range(length)])  12.2 us
    pallas_call x3, Pallas kernels, in_vmem(): pl.pallas_call(kernel, out_shape=outs, in_specs=[vmem] * len(inputs), out...  10.2 us
    unnamed x19, local copies, waits for them, and re-layouts  4.36 us
  transfers between devices with their start and end apart: 5, of which 5 were waited for; matrix products, arithmetic and copies ran while one was open for 1% of the time, Pallas kernels for 0%

profile of v2, /device:TPU:1, one launch (start us, length us, event | category | flops | bytes accessed | tf_op | source)
XLA Modules:
  0.0 85.6 jit_solution(10633754572333852846)
XLA Ops:
  0.6 0.0 copy-start
  0.6 3.3 %collective-permute-start.1 = (bf16[256,256]{1,0:T(8,128)(2,1)}, bf16[256,256]{1,0:T(8,128)(2,1)S(1)}, u32[]{:S(2)}, u32[]{:S(2)}) collective-permute-start(bf16[256,256]{1,0:T(8,128)(2,1)} %bitcast.13), channel_id=1, source_target_pairs={{0,63},{1,0},{2,1},{3,2},{4,3},{5,4},{6,5},{7,6},{8,7},{9,8},{10,9... | collective-permute-start | bytes 393224 | tf_op jit(solution)/shard_map/ppermute | solution.py:27
  4.0 0.0 collective-permute-start
  4.0 0.7 copy.14
  4.7 1.5 %collective-permute-done.1.after = bf16[256,256]{1,0:T(8,128)(2,1)S(1)} collective-permute-done((bf16[256,256]{1,0:T(8,128)(2,1)}, bf16[256,256]{1,0:T(8,128)(2,1)S(1)}, u32[]{:S(2)}, u32[]{:S(2)}) %collective-permute-start.1) | collective-permute-done | bytes 131104 | tf_op jit(solution)/shard_map/ppermute | solution.py:27
  6.2 4.6 %collective-permute-done.before = bf16[256,256]{1,0:T(8,128)(2,1)S(1)} collective-permute-done((bf16[256,256]{1,0:T(8,128)(2,1)}, bf16[256,256]{1,0:T(8,128)(2,1)S(1)}, u32[]{:S(2)}, u32[]{:S(2)}) %collective-permute-start) | collective-permute-done | bytes 131104 | tf_op jit(solution)/shard_map/ppermute | solution.py:27
  10.8 2.0 %copy-done.1 = bf16[27,256,256]{2,1,0:T(8,128)(2,1)S(1)} copy-done((bf16[27,256,256]{2,1,0:T(8,128)(2,1)S(1)}, bf16[27,256,256]{2,1,0:T(8,128)(2,1)}, u32[]{:S(2)}) %copy-start.1) | copy-done | bytes 3538968
  12.8 0.9 %copy-done.2 = bf16[1,256,256]{2,1,0:T(8,128)(2,1)S(1)} copy-done((bf16[1,256,256]{2,1,0:T(8,128)(2,1)S(1)}, bf16[1,256,256]{2,1,0:T(8,128)(2,1)}, u32[]{:S(2)}) %copy-start.2) | copy-done | bytes 131096
  13.7 0.7 copy-done.6
  14.4 0.0 copy-start.5
  14.4 4.3 %first_conv.1.here = bf16[256,256]{1,0:T(8,128)(2,1)S(1)} custom-call(bf16[256,256]{1,0:T(8,128)(2,1)S(1)} %collective-permute-done.before, bf16[256,256]{1,0:T(8,128)(2,1)S(1)} %bitcast.15, bf16[256,256]{1,0:T(8,128)(2,1)S(1)} %collective-permute-done.1.after, s32[27,256]{1,0:T(8,128)S(1)} %bitcast.17, f32[1,256]{1,0:T(1,128)S(1)} %bitcast.21, ...), custom_call_target="tpu_custom_call" | custom-call | tf_op jit(solution)/shard_map/first_conv/pallas_call | solution.py:106
  18.7 7.0 %collective-permute-start.3 = (bf16[256,256]{1,0:T(8,128)(2,1)S(1)}, bf16[256,256]{1,0:T(8,128)(2,1)S(1)}, u32[]{:S(2)}, u32[]{:S(2)}) collective-permute-start(bf16[256,256]{1,0:T(8,128)(2,1)S(1)} %first_conv.1.here), channel_id=1, source_target_pairs={{0,63},{1,0},{2,1},{3,2},{4,3},{5,4},{6,5},{7,6},{8,7},{9,8},{10,9... | collective-permute-start | bytes 393224 | tf_op jit(solution)/shard_map/ppermute | solution.py:27
  25.7 0.0 collective-permute-start.2
  25.7 1.0 %collective-permute-done.3.after = bf16[256,256]{1,0:T(8,128)(2,1)S(1)} collective-permute-done((bf16[256,256]{1,0:T(8,128)(2,1)S(1)}, bf16[256,256]{1,0:T(8,128)(2,1)S(1)}, u32[]{:S(2)}, u32[]{:S(2)}) %collective-permute-start.3) | collective-permute-done | bytes 131104 | tf_op jit(solution)/shard_map/ppermute | solution.py:27
  26.6 1.0 %collective-permute-done.2.before = bf16[256,256]{1,0:T(8,128)(2,1)S(1)} collective-permute-done((bf16[256,256]{1,0:T(8,128)(2,1)S(1)}, bf16[256,256]{1,0:T(8,128)(2,1)S(1)}, u32[]{:S(2)}, u32[]{:S(2)}) %collective-permute-start.2) | collective-permute-done | bytes 131104 | tf_op jit(solution)/shard_map/ppermute | solution.py:27
  27.6 0.0 copy-done
  27.6 5.0 %second_conv.1 = (bf16[256,256]{1,0:T(8,128)(2,1)}, f32[64,384]{1,0:T(8,128)S(1)}, f32[64,384]{1,0:T(8,128)S(1)}) custom-call(bf16[256,256]{1,0:T(8,128)(2,1)S(1)} %collective-permute-done.2.before, bf16[256,256]{1,0:T(8,128)(2,1)S(1)} %first_conv.1.here, bf16[256,256]{1,0:T(8,128)(2,1)S(1)} %collective-permute-done.3.after, s32[27,256]{1,0:T(8,128)S(1)} %bitcast.18, ...), custom_call_target="tpu_custom_call" | custom-call | tf_op jit(solution)/shard_map/second_conv/pallas_call | solution.py:106
  32.6 2.5 %collective-permute-start.4 = (f32[64,384]{1,0:T(8,128)S(1)}, f32[64,384]{1,0:T(8,128)S(1)}, u32[]{:S(2)}, u32[]{:S(2)}) collective-permute-start(f32[64,384]{1,0:T(8,128)S(1)} %get-tuple-element.10), channel_id=1, source_target_pairs={{0,1},{1,2},{2,3},{3,4},{4,5},{5,6},{6,7},{7,8},{8,9},{9,10},{10,1... | collective-permute-start | bytes 294920 | tf_op jit(solution)/shard_map/ppermute | solution.py:27
  35.1 4.2 %collective-permute-done.4.moved_ref = f32[64,384]{1,0:T(8,128)S(1)} collective-permute-done((f32[64,384]{1,0:T(8,128)S(1)}, f32[64,384]{1,0:T(8,128)S(1)}, u32[]{:S(2)}, u32[]{:S(2)}) %collective-permute-start.4) | collective-permute-done | bytes 98336 | tf_op jit(solution)/shard_map/ppermute | solution.py:27
  39.3 0.9 coarse.1
  40.1 19.9 %all_to_all.15 = bf16[32,8,512]{2,1,0:T(8,128)(2,1)S(1)} all-to-all(bf16[32,8,512]{2,1,0:T(8,128)(2,1)S(1)} %bitcast.19), channel_id=1, replica_groups=mesh['y'=4,'z'=8,'x'=4,'core'=2] {'y','x','core'}, dimensions={0} | all-to-all | bytes 524288 | tf_op jit(solution)/shard_map/all_to_all | solution.py:118
  60.1 10.8 %all_to_all.16 = f32[8,8,512]{2,1,0:T(8,128)S(1)} all-to-all(f32[8,8,512]{2,1,0:T(8,128)S(1)} %broadcast_in_dim.28), channel_id=1, replica_groups=mesh['y'=4,'z'=8,'x'=4,'core'=2] {'z'}, dimensions={0} | all-to-all | bytes 262144 | tf_op jit(solution)/shard_map/all_to_all | solution.py:118
  70.9 13.8 %all_to_all.17 = bf16[32,8,512]{2,1,0:T(8,128)(2,1)S(1)} all-to-all(bf16[32,8,512]{2,1,0:T(8,128)(2,1)S(1)} %broadcast_in_dim.29), channel_id=1, replica_groups=mesh['y'=4,'z'=8,'x'=4,'core'=2] {'y','x','core'}, dimensions={0} | all-to-all | bytes 524288 | tf_op jit(solution)/shard_map/all_to_all | solution.py:118
  84.7 0.9 bitcast_convert_fusion
  (17 shorter events, 0.1 us)
Async XLA Ops:
  0.6 27.0 %copy-start = (bf16[27,256,256]{2,1,0:T(8,128)(2,1)S(1)}, bf16[27,256,256]{2,1,0:T(8,128)(2,1)}, u32[]{:S(2)}) copy-start(bf16[27,256,256]{2,1,0:T(8,128)(2,1)} %weight_ref.3) | copy-start | bytes 10616836
  0.6 5.5 %collective-permute-start.1 = (bf16[256,256]{1,0:T(8,128)(2,1)}, bf16[256,256]{1,0:T(8,128)(2,1)S(1)}, u32[]{:S(2)}, u32[]{:S(2)}) collective-permute-start(bf16[256,256]{1,0:T(8,128)(2,1)} %bitcast.13), channel_id=1, source_target_pairs={{0,63},{1,0},{2,1},{3,2},{4,3},{5,4},{6,5},{7,6},{8,7},{9,8},{10,9... | collective-permute-start | bytes 393224 | tf_op jit(solution)/shard_map/ppermute | solution.py:27
  4.0 6.8 %collective-permute-start = (bf16[256,256]{1,0:T(8,128)(2,1)}, bf16[256,256]{1,0:T(8,128)(2,1)S(1)}, u32[]{:S(2)}, u32[]{:S(2)}) collective-permute-start(bf16[256,256]{1,0:T(8,128)(2,1)} %bitcast.14), channel_id=1, source_target_pairs={{0,1},{1,2},{2,3},{3,4},{4,5},{5,6},{6,7},{7,8},{8,9},{9,10},{10,1... | collective-permute-start | bytes 393224 | tf_op jit(solution)/shard_map/ppermute | solution.py:27
  10.8 2.0 %copy-start.1 = (bf16[27,256,256]{2,1,0:T(8,128)(2,1)S(1)}, bf16[27,256,256]{2,1,0:T(8,128)(2,1)}, u32[]{:S(2)}) copy-start(bf16[27,256,256]{2,1,0:T(8,128)(2,1)} %weight_ref.2) | copy-start | bytes 10616836
  12.8 0.9 %copy-start.2 = (bf16[1,256,256]{2,1,0:T(8,128)(2,1)S(1)}, bf16[1,256,256]{2,1,0:T(8,128)(2,1)}, u32[]{:S(2)}) copy-start(bf16[1,256,256]{2,1,0:T(8,128)(2,1)} %param.9) | copy-start | bytes 393220
  13.7 0.7 copy-start.6
  14.4 13.3 %copy-start.3 = (bf16[1,256,256]{2,1,0:T(8,128)(2,1)S(1)}, bf16[1,256,256]{2,1,0:T(8,128)(2,1)}, u32[]{:S(2)}) copy-start(bf16[1,256,256]{2,1,0:T(8,128)(2,1)} %param.9) | copy-start | bytes 393220
  14.4 13.3 %copy-start.7 = (f32[256]{0:T(256)S(1)}, f32[256]{0:T(256)}, u32[]{:S(2)}) copy-start(f32[256]{0:T(256)} %param.15) | copy-start | bytes 3076
  14.4 13.3 %copy-start.8 = (s32[1,256]{1,0:T(1,128)S(1)}, s32[1,256]{1,0:T(1,128)}, u32[]{:S(2)}) copy-start(s32[1,256]{1,0:T(1,128)} %parent_ref.1) | copy-start | bytes 3076
  14.4 24.9 %copy-start.4 = (bf16[256,512]{1,0:T(8,128)(2,1)S(1)}, bf16[256,512]{1,0:T(8,128)(2,1)}, u32[]{:S(2)}) copy-start(bf16[256,512]{1,0:T(8,128)(2,1)} %down_ref.1) | copy-start | bytes 786436
  14.4 24.9 %copy-start.5 = (bf16[1,64,512]{2,1,0:T(8,128)(2,1)S(1)}, bf16[1,64,512]{2,1,0:T(8,128)(2,1)}, u32[]{:S(2)}) copy-start(bf16[1,64,512]{2,1,0:T(8,128)(2,1)} %param.17) | copy-start | bytes 196612
  18.7 7.9 %collective-permute-start.3 = (bf16[256,256]{1,0:T(8,128)(2,1)S(1)}, bf16[256,256]{1,0:T(8,128)(2,1)S(1)}, u32[]{:S(2)}, u32[]{:S(2)}) collective-permute-start(bf16[256,256]{1,0:T(8,128)(2,1)S(1)} %first_conv.1.here), channel_id=1, source_target_pairs={{0,63},{1,0},{2,1},{3,2},{4,3},{5,4},{6,5},{7,6},{8,7},{9,8},{10,9... | collective-permute-start | bytes 393224 | tf_op jit(solution)/shard_map/ppermute | solution.py:27
  25.7 2.0 %collective-permute-start.2 = (bf16[256,256]{1,0:T(8,128)(2,1)S(1)}, bf16[256,256]{1,0:T(8,128)(2,1)S(1)}, u32[]{:S(2)}, u32[]{:S(2)}) collective-permute-start(bf16[256,256]{1,0:T(8,128)(2,1)S(1)} %first_conv.1.here), channel_id=1, source_target_pairs={{0,1},{1,2},{2,3},{3,4},{4,5},{5,6},{6,7},{7,8},{8,9},{9,10},{10,1... | collective-permute-start | bytes 393224 | tf_op jit(solution)/shard_map/ppermute | solution.py:27
  32.6 6.7 %collective-permute-start.4 = (f32[64,384]{1,0:T(8,128)S(1)}, f32[64,384]{1,0:T(8,128)S(1)}, u32[]{:S(2)}, u32[]{:S(2)}) collective-permute-start(f32[64,384]{1,0:T(8,128)S(1)} %get-tuple-element.10), channel_id=1, source_target_pairs={{0,1},{1,2},{2,3},{3,4},{4,5},{5,6},{6,7},{7,8},{8,9},{9,10},{10,1... | collective-permute-start | bytes 294920 | tf_op jit(solution)/shard_map/ppermute | solution.py:27

commit v3 on v2

v3 whole, which is shorter than its diff:
```python
import functools
import math

import jax
import jax.numpy as jnp
from jax import lax
from jax.experimental import pallas as pl
from jax.experimental.pallas import tpu as pltpu
from jax.sharding import Mesh
from jax.sharding import PartitionSpec as P


DP = "y"
SPACE = ("z", "x", "core")
PLANE = ("y", "x", "core")
GROUP = 3
VMEM_BYTES = 32 << 20
PAR_ROWS = 64
COST_BYTES = 1 << 20


def split_mesh(mesh):
    dp, space = mesh.devices.shape
    return Mesh(mesh.devices.reshape(dp, space // 8, 4, 2), (DP,) + SPACE)


def shifted(array, by):
    length = lax.axis_size(SPACE)
    return lax.ppermute(array, SPACE, [(i, i + by) for i in range(length) if 0 <= i + by < length])


def from_partner(array):
    length = lax.axis_size(SPACE)
    return lax.ppermute(array, SPACE, [(i, i ^ 1) for i in range(length)])


def from_across(array):
    last = lax.axis_size(SPACE) - 1
    pairs = [(i, i + 1) for i in range(1, last, 2)]
    return lax.ppermute(array, SPACE, pairs + [(j, i) for i, j in pairs])


def settled(running, gain):
    inverse = lax.rsqrt(jnp.mean(running * running, axis=-1, keepdims=True) + 1e-05)
    scaled = running * inverse * gain
    return scaled / (1.0 + jnp.exp(-scaled))


def local_table(taps_ref):
    taps, _, rows = taps_ref.shape
    lowest = (lax.axis_index(SPACE) - 1) * rows
    ids = taps_ref[...].reshape(taps, rows)
    local = jnp.where(ids < 0, -4 * rows, ids - lowest)
    return jnp.concatenate([local, jnp.full((-taps % 8, rows), -1, jnp.int32)], axis=0).T


def pick(local, taps, blocks, select_ref, put):
    rows = local.shape[0]
    places = lax.broadcasted_iota(jnp.int16, (rows, rows), 1)
    one, zero = jnp.ones((), jnp.bfloat16), jnp.zeros((), jnp.bfloat16)
    for tap in range(taps):
        column = jnp.broadcast_to(local[:, tap : tap + 1], (rows, 128))
        for b, (_, start) in enumerate(blocks):
            wanted = (column - start).astype(jnp.int16)
            wanted = jnp.concatenate([wanted] * (rows // 128), axis=1)
            select_ref[tap * rows : (tap + 1) * rows, b * rows : (b + 1) * rows] = jnp.where(
                wanted == places, one, zero
            )
    for first in range(0, taps, GROUP):
        part = select_ref[first * rows : (first + GROUP) * rows]
        picked = sum(
            jnp.dot(part[:, b * rows : (b + 1) * rows], block, preferred_element_type=jnp.float32)
            for b, (block, _) in enumerate(blocks)
        ).astype(jnp.bfloat16)
        for j in range(GROUP):
            put(first + j, picked[j * rows : (j + 1) * rows])


def pick_near(local, here, partner, select_ref, near_ref):
    rows, chans = here.shape
    blocks = ((here, rows), (partner, 2 * rows * (1 - lax.axis_index("core"))))

    def put(tap, picked):
        near_ref[:, tap * chans : (tap + 1) * chans] = picked

    pick(local, near_ref.shape[1] // chans, blocks, select_ref, put)


def convolved(local, across, near_ref, weight_ref, select_ref, picked_ref):
    rows, chans = across.shape
    taps = weight_ref.shape[0]

    def put(tap, picked):
        columns = slice(tap * chans, (tap + 1) * chans)
        picked_ref[:, columns] = near_ref[:, columns] + picked

    pick(local, taps, ((across, 2 * rows * lax.axis_index("core")),), select_ref, put)
    return jnp.dot(
        picked_ref[...],
        weight_ref[...].reshape(taps * chans, weight_ref.shape[2]),
        preferred_element_type=jnp.float32,
    )


def first_near_kernel(taps_ref, here, partner, near_ref, local_ref, select_ref):
    local = local_table(taps_ref)
    local_ref[...] = local
    pick_near(local, here[...], partner[...], select_ref, near_ref)


def first_far_kernel(
    local_ref, across, near_ref, weight_ref, gain_ref, parent_ref, middle_ref, select_ref, picked_ref
):
    total = convolved(local_ref[...], across[...], near_ref, weight_ref, select_ref, picked_ref)
    rows = total.shape[0]
    middle_ref[:rows] = settled(total, gain_ref[...]).astype(middle_ref.dtype)
    ids = parent_ref[...] - lax.axis_index(SPACE) * PAR_ROWS
    ids = jnp.broadcast_to(ids.astype(jnp.float32), (middle_ref.shape[0] - rows, ids.shape[1]))
    middle_ref[rows:] = ids.astype(middle_ref.dtype)


def second_near_kernel(local_ref, here, partner, near_ref, select_ref):
    rows = local_ref.shape[0]
    pick_near(local_ref[...], here[:rows], partner[:rows], select_ref, near_ref)


def membership(ids, parents):
    return (lax.broadcasted_iota(jnp.int32, (parents, ids.shape[1]), 0) == ids).astype(jnp.float32)


def second_far_kernel(
    local_ref, across, partner, near_ref, weight_ref, gain_ref, feature_ref, parent_ref,
    cotangent_ref, after_ref,
    fine_ref, own_ref, sent_ref, grad_ref, select_ref, picked_ref,
):
    rows, chans = feature_ref.shape
    total = convolved(local_ref[...], across[:rows], near_ref, weight_ref, select_ref, picked_ref)
    fine = feature_ref[...].astype(jnp.float32) + settled(total, gain_ref[...])
    fine = fine.astype(fine_ref.dtype)
    fine_ref[...] = fine
    half = cotangent_ref.shape[0]
    member = membership(parent_ref[...] - lax.axis_index(SPACE) * half, 2 * half)
    sums = jnp.dot(member.astype(jnp.bfloat16), fine, preferred_element_type=jnp.float32)

    def tally(ids):
        return jnp.sum(membership(ids, 2 * half), axis=1, keepdims=True)

    tally_own = jnp.sum(member, axis=1, keepdims=True)
    tally_partner = tally(partner[rows:].astype(jnp.float32)[:1].astype(jnp.int32))
    tally_across = tally(across[rows:].astype(jnp.float32)[:1].astype(jnp.int32))
    upper = lax.axis_index("core") == 1
    tally_before = jnp.where(upper, tally_partner, tally_across)[half:]
    tally_after = jnp.where(upper, tally_across, tally_partner)[:half]
    count_own = jnp.maximum(tally_own[:half] + tally_before, 1.0)
    count_after = jnp.maximum(tally_own[half:] + tally_after, 1.0)
    own_ref[:, :chans] = sums[:half]
    own_ref[:, chans:] = jnp.broadcast_to(count_own, (half, own_ref.shape[1] - chans))
    sent_ref[...] = sums[half:]
    shares = sums / jnp.concatenate([count_own, count_after], axis=0)
    grads_in = jnp.concatenate([cotangent_ref[...], after_ref[...]], axis=0)
    grad_ref[...] = lax.dot_general(
        shares.astype(jnp.bfloat16), grads_in, (((0,), (0,)), ((), ())), preferred_element_type=jnp.float32
    ).astype(grad_ref.dtype)


def coarse_kernel(own_ref, moved_ref, down_ref, coarse_ref):
    chans = down_ref.shape[0]
    own = own_ref[...]
    pooled = ((own[:, :chans] + moved_ref[...]) / own[:, chans : chans + 1]).astype(jnp.bfloat16)
    coarse_ref[...] = jnp.dot(pooled, down_ref[...], preferred_element_type=jnp.float32).astype(coarse_ref.dtype)


def in_vmem(kernel, outs, inputs, name, scratch=(), flops=0):
    vmem = pl.BlockSpec(memory_space=pltpu.VMEM)
    return pl.pallas_call(
        kernel,
        out_shape=outs,
        in_specs=[vmem] * len(inputs),
        out_specs=jax.tree.map(lambda _: vmem, outs),
        scratch_shapes=scratch,
        compiler_params=pltpu.CompilerParams(vmem_limit_bytes=VMEM_BYTES),
        cost_estimate=pl.CostEstimate(flops=flops, bytes_accessed=COST_BYTES, transcendentals=0),
        name=name,
    )(*inputs)


def exchanged(pieces, axes):
    return lax.all_to_all(pieces, axes, 0, 0, tiled=True)


def plane_summed(local_grad):
    rows, cols = local_grad.shape
    plane = lax.axis_size(PLANE)
    return exchanged(local_grad.reshape(plane, rows // plane, cols), PLANE)


def finished(parts, scale):
    plane, _, cols = parts.shape
    part = jnp.sum(parts.astype(jnp.float32), axis=0)
    copies = jnp.broadcast_to(part[None], (lax.axis_size("z"),) + part.shape)
    part = jnp.sum(exchanged(copies, "z"), axis=0) * scale
    copies = jnp.broadcast_to(part.astype(jnp.bfloat16)[None], (plane,) + part.shape)
    return exchanged(copies, PLANE).astype(jnp.float32).reshape(-1, cols)


def body(
    features,
    neighbours,
    parents,
    conv_first,
    conv_second,
    gain_first,
    gain_second,
    down_weight,
    cotangent,
):
    field, grad_in = features[0], cotangent[0]
    _, taps, rows = neighbours.shape
    chans = field.shape[1]
    par_rows, out_chans = grad_in.shape
    bf16 = functools.partial(jax.ShapeDtypeStruct, dtype=jnp.bfloat16)
    f32 = functools.partial(jax.ShapeDtypeStruct, dtype=jnp.float32)
    product = 2 * taps * rows * chans * rows
    near_shape = bf16((rows, taps * chans))
    select = [pltpu.VMEM((taps * rows, 2 * rows), jnp.bfloat16)]
    select_and_picked = [
        pltpu.VMEM((taps * rows, rows), jnp.bfloat16),
        pltpu.VMEM((rows, taps * chans), jnp.bfloat16),
    ]
    across = from_across(field)
    near, local = in_vmem(
        first_near_kernel,
        (near_shape, jax.ShapeDtypeStruct((rows, taps + -taps % 8), jnp.int32)),
        (jnp.moveaxis(neighbours, 1, 0), field, from_partner(field)),
        "first_near", select, 2 * product,
    )
    ready, near = lax.optimization_barrier((grad_in, near))
    after = shifted(ready, -1)
    middle = in_vmem(
        first_far_kernel,
        bf16((rows + 16, chans)),
        (local, across, near, conv_first, gain_first[None], parents),
        "first_far", select_and_picked, 2 * product,
    )
    middle, after = lax.optimization_barrier((middle, after))
    across = from_across(middle)
    partner = from_partner(middle)
    near = in_vmem(
        second_near_kernel, near_shape, (local, middle, partner), "second_near", select, 2 * product
    )
    fine, own, sent, local_grad = in_vmem(
        second_far_kernel,
        (
            bf16((rows, chans)),
            f32((par_rows, chans + 128)),
            f32((par_rows, chans)),
            bf16((chans, out_chans)),
        ),
        (
            local, across, partner, near, conv_second, gain_second[None], field, parents,
            grad_in, after,
        ),
        "second_far", select_and_picked, 2 * product,
    )
    parts = plane_summed(local_grad)
    sent, parts = lax.optimization_barrier((sent, parts))
    coarse = in_vmem(
        coarse_kernel, bf16((par_rows, out_chans)), (own, shifted(sent, 1), down_weight), "coarse"
    )
    worlds_all = lax.axis_size(DP)
    parents_all = par_rows * lax.axis_size(SPACE)
    down_grad = finished(parts, 1.0 / math.sqrt(worlds_all * parents_all))
    return (fine[None], coarse[None], down_grad)


def solution(mesh):
    return jax.shard_map(
        body,
        mesh=split_mesh(mesh),
        in_specs=(
            P(DP, SPACE, None),
            P(DP, None, SPACE),
            P(DP, SPACE),
            P(),
            P(),
            P(),
            P(),
            P(),
            P(DP, SPACE, None),
        ),
        out_specs=(P(DP, SPACE, None), P(DP, SPACE, None), P()),
        check_vma=False,
    )
```

time: 85.9 us -> 78.4 us (0.913)
  blocking collectives: 44.5 us -> 37.1 us
  starting transfers between devices: 12.7 us -> 19.3 us
  waiting for transfers between devices: 12.2 us -> 6.93 us
  local copies, waits for them, and re-layouts: 4.39 us -> 2.41 us
    ppermute x5 -> x6, waiting for transfers between devices: 12.2 us -> 3.62 us  [the longest x2 2.59 us: shifted(): lax.ppermute(array, SPACE, [(i, i + by) for i in range(length) if 0 <= i...]
    all_to_all x3 -> x2, blocking collectives: 44.5 us -> 37.1 us  [exchanged(): return lax.all_to_all(pieces, axes, 0, 0, tiled=True)]
    all_to_all x0 -> x1, starting transfers between devices: none -> 5.35 us  [exchanged(): return lax.all_to_all(pieces, axes, 0, 0, tiled=True)]
    all_to_all x0 -> x1, waiting for transfers between devices: none -> 3.3 us  [exchanged(): return lax.all_to_all(pieces, axes, 0, 0, tiled=True)]
    unnamed x19 -> x18, local copies, waits for them, and re-layouts: 4.36 us -> 1.67 us
    ppermute x5 -> x6, starting transfers between devices: 12.7 us -> 14 us  [the longest x2 5.47 us: shifted(): lax.ppermute(array, SPACE, [(i, i + by) for i in range(length) if 0 <= i...]
    pallas_call x3 -> x5, Pallas kernels: 10.2 us -> 10.5 us  [in_vmem(): pl.pallas_call(kernel, out_shape=outs, in_specs=[vmem] * len(inputs), out...]
  transfers between devices with their start and end apart: 5 -> 7, of which waited for: 5 -> 4; matrix products, arithmetic and copies ran while one was open for 1% -> 0% of each run, Pallas kernels for 0% -> 10%
where the time goes in v3:
time: 78.4 us; the launch traced here: 78 us
  blocking collectives  37.1 us (47%)
  starting transfers between devices  19.3 us (25%)
  Pallas kernels  10.5 us (13%)
  waiting for transfers between devices  6.93 us (9%)
  local copies, waits for them, and re-layouts  2.41 us (3%)
  other arithmetic  0.92 us (1%)
  between operations  0.8 us (1%)
    all_to_all x2, blocking collectives, exchanged(): return lax.all_to_all(pieces, axes, 0, 0, tiled=True)  37.1 us
    pallas_call x5, Pallas kernels, in_vmem(): pl.pallas_call(kernel, out_shape=outs, in_specs=[vmem] * len(inputs), out...  10.5 us
    ppermute x2, starting transfers between devices, shifted(): lax.ppermute(array, SPACE, [(i, i + by) for i in range(length) if 0 <= i...  5.47 us
    all_to_all x1, starting transfers between devices, exchanged(): return lax.all_to_all(pieces, axes, 0, 0, tiled=True)  5.35 us
    ppermute x2, starting transfers between devices, from_across(): return lax.ppermute(array, SPACE, pairs + [(j, i) for i, j in pairs])  5.17 us
    ppermute x2, starting transfers between devices, from_partner(): return lax.ppermute(array, SPACE, [(i, i ^ 1) for i in range(length)])  3.33 us
    all_to_all x1, waiting for transfers between devices, exchanged(): return lax.all_to_all(pieces, axes, 0, 0, tiled=True)  3.3 us
    ppermute x2, waiting for transfers between devices, shifted(): lax.ppermute(array, SPACE, [(i, i + by) for i in range(length) if 0 <= i...  2.59 us
  transfers between devices with their start and end apart: 7, of which 4 were waited for; matrix products, arithmetic and copies ran while one was open for 0% of the time, Pallas kernels for 10%

profile of v3, /device:TPU:1, one launch (start us, length us, event | category | flops | bytes accessed | tf_op | source)
XLA Modules:
  0.0 78.0 jit_solution(12617384071865098335)
XLA Ops:
  0.6 3.3 %collective-permute-start = (bf16[256,256]{1,0:T(8,128)(2,1)}, bf16[256,256]{1,0:T(8,128)(2,1)S(1)}, u32[]{:S(2)}, u32[]{:S(2)}) collective-permute-start(bf16[256,256]{1,0:T(8,128)(2,1)} %bitcast.12), channel_id=1, source_target_pairs={{0,1},{1,0},{2,3},{3,2},{4,5},{5,4},{6,7},{7,6},{8,9},{9,8},{10,11... | collective-permute-start | bytes 393224 | tf_op jit(solution)/shard_map/ppermute | solution.py:34
  4.0 1.9 %collective-permute-start.1 = (bf16[256,256]{1,0:T(8,128)(2,1)}, bf16[256,256]{1,0:T(8,128)(2,1)S(1)}, u32[]{:S(2)}, u32[]{:S(2)}) collective-permute-start(bf16[256,256]{1,0:T(8,128)(2,1)} %bitcast.13), channel_id=1, source_target_pairs={{1,2},{3,4},{5,6},{7,8},{9,10},{11,12},{13,14},{15,16},{17,18},{19... | collective-permute-start | bytes 393224 | tf_op jit(solution)/shard_map/ppermute | solution.py:40
  5.9 0.0 collective-permute-done.partner
  5.9 0.9 %copy-done.3 = bf16[1,256,256]{2,1,0:T(8,128)(2,1)S(1)} copy-done((bf16[1,256,256]{2,1,0:T(8,128)(2,1)S(1)}, bf16[1,256,256]{2,1,0:T(8,128)(2,1)}, u32[]{:S(2)}) %copy-start.3) | copy-done | bytes 131096
  6.8 0.7 copy-done.8
  7.6 2.3 %first_near.1 = (bf16[256,6912]{1,0:T(8,128)(2,1)S(1)}, s32[256,32]{1,0:T(8,128)S(1)}) custom-call(s32[27,1,256]{2,1,0:T(1,128)S(1)} %bitcast.20, bf16[256,256]{1,0:T(8,128)(2,1)S(1)} %bitcast.14, bf16[256,256]{1,0:T(8,128)(2,1)S(1)} %collective-permute-done.partner), custom_call_target="tpu_custom_call" | custom-call | flops 1811939328 | bytes 1048576 | tf_op jit(solution)/shard_map/first_near/pallas_call | solution.py:175
  9.9 1.9 %collective-permute-start.2 = (bf16[64,512]{1,0:T(8,128)(2,1)S(1)}, bf16[64,512]{1,0:T(8,128)(2,1)S(1)}, u32[]{:S(2)}, u32[]{:S(2)}) collective-permute-start(bf16[64,512]{1,0:T(8,128)(2,1)S(1)} %bitcast.16), channel_id=1, source_target_pairs={{1,0},{2,1},{3,2},{4,3},{5,4},{6,5},{7,6},{8,7},{9,8},{10,9},{11,1... | collective-permute-start | bytes 196616 | tf_op jit(solution)/shard_map/ppermute | solution.py:29
  11.8 2.3 %first_far.1.here = bf16[272,256]{1,0:T(8,128)(2,1)S(1)} custom-call(s32[256,32]{1,0:T(8,128)S(1)} %get-tuple-element.15.local_ref, bf16[256,256]{1,0:T(8,128)(2,1)S(1)} %collective-permute-done.1.across, bf16[256,6912]{1,0:T(8,128)(2,1)S(1)} %get-tuple-element.17.near_ref, bf16[27,256,256]{2,1,0:T(8,128)(2,1)S(1)} %copy-done, f32[1,256]{1,0:T(1,128)S(1)} %bitcast.18, ...), custom_call_target="tpu_custom_call" | custom-call | flops 1811939328 | bytes 1048576 | tf_op jit(solution)/shard_map/first_far/pallas_call | solution.py:175
  14.2 0.0 copy-start.1
  14.2 0.0 copy-start.7
  14.2 1.3 %collective-permute-done.2.after_ref = bf16[64,512]{1,0:T(8,128)(2,1)S(1)} collective-permute-done((bf16[64,512]{1,0:T(8,128)(2,1)S(1)}, bf16[64,512]{1,0:T(8,128)(2,1)S(1)}, u32[]{:S(2)}, u32[]{:S(2)}) %collective-permute-start.2) | collective-permute-done | bytes 65568 | tf_op jit(solution)/shard_map/ppermute | solution.py:29
  15.5 3.3 %collective-permute-start.3 = (bf16[272,256]{1,0:T(8,128)(2,1)S(1)}, bf16[272,256]{1,0:T(8,128)(2,1)S(1)}, u32[]{:S(2)}, u32[]{:S(2)}) collective-permute-start(bf16[272,256]{1,0:T(8,128)(2,1)S(1)} %first_far.1.here), channel_id=1, source_target_pairs={{1,2},{3,4},{5,6},{7,8},{9,10},{11,12},{13,14},{15,16},{17,18},{19... | collective-permute-start | bytes 417800 | tf_op jit(solution)/shard_map/ppermute | solution.py:40
  18.7 2.0 %second_near.1.near_ref = bf16[256,6912]{1,0:T(8,128)(2,1)S(1)} custom-call(s32[256,32]{1,0:T(8,128)S(1)} %get-tuple-element.15.local_ref, bf16[272,256]{1,0:T(8,128)(2,1)S(1)} %first_far.1.here, bf16[272,256]{1,0:T(8,128)(2,1)S(1)} %collective-permute-done.4.partner), custom_call_target="tpu_custom_call" | custom-call | flops 1811939328 | bytes 1048576 | tf_op jit(solution)/shard_map/second_near/pallas_call | solution.py:175
  20.8 1.0 %collective-permute-done.3.across = bf16[272,256]{1,0:T(8,128)(2,1)S(1)} collective-permute-done((bf16[272,256]{1,0:T(8,128)(2,1)S(1)}, bf16[272,256]{1,0:T(8,128)(2,1)S(1)}, u32[]{:S(2)}, u32[]{:S(2)}) %collective-permute-start.3) | collective-permute-done | bytes 139296 | tf_op jit(solution)/shard_map/ppermute | solution.py:40
  21.8 3.0 %second_far.1 = (bf16[256,256]{1,0:T(8,128)(2,1)}, f32[64,384]{1,0:T(8,128)S(1)}, f32[64,256]{1,0:T(8,128)S(1)}, bf16[256,512]{1,0:T(8,128)(2,1)S(1)}) custom-call(s32[256,32]{1,0:T(8,128)S(1)} %get-tuple-element.15.local_ref, bf16[272,256]{1,0:T(8,128)(2,1)S(1)} %collective-permute-done.3.across, bf16[272,256]{1,0:T(8,128)(2,1)S(1)} %collective-permute-done.4.partner, ...), custom_call_target="tpu_custom_call" | custom-call | flops 1811939328 | bytes 1048576 | tf_op jit(solution)/shard_map/second_far/pallas_call | solution.py:175
  24.8 19.8 %all_to_all.15 = bf16[32,8,512]{2,1,0:T(8,128)(2,1)S(1)} all-to-all(bf16[32,8,512]{2,1,0:T(8,128)(2,1)S(1)} %bitcast.11), channel_id=1, replica_groups=mesh['y'=4,'z'=8,'x'=4,'core'=2] {'y','x','core'}, dimensions={0} | all-to-all | bytes 524288 | tf_op jit(solution)/shard_map/all_to_all | solution.py:188
  44.7 17.2 %all_to_all.16 = f32[8,8,512]{2,1,0:T(8,128)S(1)} all-to-all(f32[8,8,512]{2,1,0:T(8,128)S(1)} %broadcast_in_dim.28), channel_id=1, replica_groups=mesh['y'=4,'z'=8,'x'=4,'core'=2] {'z'}, dimensions={0} | all-to-all | bytes 262144 | tf_op jit(solution)/shard_map/all_to_all | solution.py:188
  62.0 0.7 broadcast_in_dim.29
  62.7 5.4 %all-to-all-start.2 = ((bf16[32,8,512]{2,1,0:T(8,128)(2,1)}), bf16[32,8,512]{2,1,0:T(8,128)(2,1)S(1)}, u32[]{:S(2)}, u32[]{:S(2)}) async-start(bf16[32,8,512]{2,1,0:T(8,128)(2,1)} %broadcast_in_dim.29), calls=%async_computation.2 | async-start | bytes 524288 | tf_op jit(solution)/shard_map/all_to_all | solution.py:188
  68.1 3.5 %collective-permute-start.5 = (f32[64,256]{1,0:T(8,128)S(1)}, f32[64,256]{1,0:T(8,128)S(1)}, u32[]{:S(2)}, u32[]{:S(2)}) collective-permute-start(f32[64,256]{1,0:T(8,128)S(1)} %get-tuple-element.25), channel_id=1, source_target_pairs={{0,1},{1,2},{2,3},{3,4},{4,5},{5,6},{6,7},{7,8},{8,9},{9,10},{10,1... | collective-permute-start | bytes 196616 | tf_op jit(solution)/shard_map/ppermute | solution.py:29
  71.6 1.3 %collective-permute-done.5.moved_ref = f32[64,256]{1,0:T(8,128)S(1)} collective-permute-done((f32[64,256]{1,0:T(8,128)S(1)}, f32[64,256]{1,0:T(8,128)S(1)}, u32[]{:S(2)}, u32[]{:S(2)}) %collective-permute-start.5) | collective-permute-done | bytes 65568 | tf_op jit(solution)/shard_map/ppermute | solution.py:29
  73.0 0.8 %coarse.1 = bf16[64,512]{1,0:T(8,128)(2,1)} custom-call(f32[64,384]{1,0:T(8,128)S(1)} %get-tuple-element.22.own_ref, f32[64,256]{1,0:T(8,128)S(1)} %collective-permute-done.5.moved_ref, bf16[256,512]{1,0:T(8,128)(2,1)S(1)} %copy-done.2), custom_call_target="tpu_custom_call" | custom-call | bytes 1048576 | tf_op jit(solution)/shard_map/coarse/pallas_call | solution.py:175
  73.8 3.3 %all-to-all-done.2 = bf16[32,8,512]{2,1,0:T(8,128)(2,1)S(1)} async-done(((bf16[32,8,512]{2,1,0:T(8,128)(2,1)}), bf16[32,8,512]{2,1,0:T(8,128)(2,1)S(1)}, u32[]{:S(2)}, u32[]{:S(2)}) %all-to-all-start.2) | async-done | bytes 262176 | tf_op jit(solution)/shard_map/all_to_all | solution.py:188
  77.1 0.9 %bitcast_convert_fusion = f32[256,512]{1,0:T(8,128)} fusion(bf16[32,8,512]{2,1,0:T(8,128)(2,1)S(1)} %all-to-all-done.2), kind=kLoop, calls=%fused_computation.1 | loop fusion | flops 131072 | bytes 786432 | tf_op jit(solution)/shard_map/reshape | solution.py:203
  (21 shorter events, 0.1 us)
Async XLA Ops:
  0.6 11.2 %copy-start = (bf16[27,256,256]{2,1,0:T(8,128)(2,1)S(1)}, bf16[27,256,256]{2,1,0:T(8,128)(2,1)}, u32[]{:S(2)}) copy-start(bf16[27,256,256]{2,1,0:T(8,128)(2,1)} %weight_ref.2) | copy-start | bytes 10616836
  0.6 5.2 %collective-permute-start = (bf16[256,256]{1,0:T(8,128)(2,1)}, bf16[256,256]{1,0:T(8,128)(2,1)S(1)}, u32[]{:S(2)}, u32[]{:S(2)}) collective-permute-start(bf16[256,256]{1,0:T(8,128)(2,1)} %bitcast.12), channel_id=1, source_target_pairs={{0,1},{1,0},{2,3},{3,2},{4,5},{5,4},{6,7},{7,6},{8,9},{9,8},{10,11... | collective-permute-start | bytes 393224 | tf_op jit(solution)/shard_map/ppermute | solution.py:34
  4.0 7.8 %collective-permute-start.1 = (bf16[256,256]{1,0:T(8,128)(2,1)}, bf16[256,256]{1,0:T(8,128)(2,1)S(1)}, u32[]{:S(2)}, u32[]{:S(2)}) collective-permute-start(bf16[256,256]{1,0:T(8,128)(2,1)} %bitcast.13), channel_id=1, source_target_pairs={{1,2},{3,4},{5,6},{7,8},{9,10},{11,12},{13,14},{15,16},{17,18},{19... | collective-permute-start | bytes 393224 | tf_op jit(solution)/shard_map/ppermute | solution.py:40
  5.9 0.9 %copy-start.3 = (bf16[1,256,256]{2,1,0:T(8,128)(2,1)S(1)}, bf16[1,256,256]{2,1,0:T(8,128)(2,1)}, u32[]{:S(2)}) copy-start(bf16[1,256,256]{2,1,0:T(8,128)(2,1)} %param.9) | copy-start | bytes 393220
  6.8 0.7 copy-start.8
  7.5 2.3 %copy-start.4 = (bf16[1,64,512]{2,1,0:T(8,128)(2,1)S(1)}, bf16[1,64,512]{2,1,0:T(8,128)(2,1)}, u32[]{:S(2)}) copy-start(bf16[1,64,512]{2,1,0:T(8,128)(2,1)} %param.17) | copy-start | bytes 196612
  7.5 4.3 %copy-start.5 = (s32[1,256]{1,0:T(1,128)S(1)}, s32[1,256]{1,0:T(1,128)}, u32[]{:S(2)}) copy-start(s32[1,256]{1,0:T(1,128)} %parent_ref.3) | copy-start | bytes 3076
  7.6 4.3 %copy-start.6 = (f32[256]{0:T(256)S(1)}, f32[256]{0:T(256)}, u32[]{:S(2)}) copy-start(f32[256]{0:T(256)} %param.14) | copy-start | bytes 3076
  9.9 5.6 %collective-permute-start.2 = (bf16[64,512]{1,0:T(8,128)(2,1)S(1)}, bf16[64,512]{1,0:T(8,128)(2,1)S(1)}, u32[]{:S(2)}, u32[]{:S(2)}) collective-permute-start(bf16[64,512]{1,0:T(8,128)(2,1)S(1)} %bitcast.16), channel_id=1, source_target_pairs={{1,0},{2,1},{3,2},{4,3},{5,4},{6,5},{7,6},{8,7},{9,8},{10,9},{11,1... | collective-permute-start | bytes 196616 | tf_op jit(solution)/shard_map/ppermute | solution.py:29
  14.2 7.7 %copy-start.1 = (bf16[27,256,256]{2,1,0:T(8,128)(2,1)S(1)}, bf16[27,256,256]{2,1,0:T(8,128)(2,1)}, u32[]{:S(2)}) copy-start(bf16[27,256,256]{2,1,0:T(8,128)(2,1)} %weight_ref.3) | copy-start | bytes 10616836
  14.2 7.7 %copy-start.7 = (f32[256]{0:T(256)S(1)}, f32[256]{0:T(256)}, u32[]{:S(2)}) copy-start(f32[256]{0:T(256)} %param.15) | copy-start | bytes 3076
  15.5 3.3 %collective-permute-start.4 = (bf16[272,256]{1,0:T(8,128)(2,1)S(1)}, bf16[272,256]{1,0:T(8,128)(2,1)S(1)}, u32[]{:S(2)}, u32[]{:S(2)}) collective-permute-start(bf16[272,256]{1,0:T(8,128)(2,1)S(1)} %first_far.1.here), channel_id=1, source_target_pairs={{0,1},{1,0},{2,3},{3,2},{4,5},{5,4},{6,7},{7,6},{8,9},{9,8},{10,11... | collective-permute-start | bytes 417800 | tf_op jit(solution)/shard_map/ppermute | solution.py:34
  15.5 6.4 %collective-permute-start.3 = (bf16[272,256]{1,0:T(8,128)(2,1)S(1)}, bf16[272,256]{1,0:T(8,128)(2,1)S(1)}, u32[]{:S(2)}, u32[]{:S(2)}) collective-permute-start(bf16[272,256]{1,0:T(8,128)(2,1)S(1)} %first_far.1.here), channel_id=1, source_target_pairs={{1,2},{3,4},{5,6},{7,8},{9,10},{11,12},{13,14},{15,16},{17,18},{19... | collective-permute-start | bytes 417800 | tf_op jit(solution)/shard_map/ppermute | solution.py:40
  21.8 51.1 %copy-start.2 = (bf16[256,512]{1,0:T(8,128)(2,1)S(1)}, bf16[256,512]{1,0:T(8,128)(2,1)}, u32[]{:S(2)}) copy-start(bf16[256,512]{1,0:T(8,128)(2,1)} %down_ref.1) | copy-start | bytes 786436
  62.7 14.4 %all-to-all-start.2 = ((bf16[32,8,512]{2,1,0:T(8,128)(2,1)}), bf16[32,8,512]{2,1,0:T(8,128)(2,1)S(1)}, u32[]{:S(2)}, u32[]{:S(2)}) async-start(bf16[32,8,512]{2,1,0:T(8,128)(2,1)} %broadcast_in_dim.29), calls=%async_computation.2 | async-start | bytes 524288 | tf_op jit(solution)/shard_map/all_to_all | solution.py:188
  68.1 4.9 %collective-permute-start.5 = (f32[64,256]{1,0:T(8,128)S(1)}, f32[64,256]{1,0:T(8,128)S(1)}, u32[]{:S(2)}, u32[]{:S(2)}) collective-permute-start(f32[64,256]{1,0:T(8,128)S(1)} %get-tuple-element.25), channel_id=1, source_target_pairs={{0,1},{1,2},{2,3},{3,4},{4,5},{5,6},{6,7},{7,8},{8,9},{9,10},{10,1... | collective-permute-start | bytes 196616 | tf_op jit(solution)/shard_map/ppermute | solution.py:29

commit v4 on v3

--- a/solution.py
+++ b/solution.py
@@ -15,7 +15,6 @@
 PLANE = ("y", "x", "core")
 GROUP = 3
 VMEM_BYTES = 32 << 20
-PAR_ROWS = 64
 COST_BYTES = 1 << 20
 
 
@@ -37,7 +36,7 @@
 def from_across(array):
     last = lax.axis_size(SPACE) - 1
     pairs = [(i, i + 1) for i in range(1, last, 2)]
-    return lax.ppermute(array, SPACE, pairs + [(j, i) for i, j in pairs])
+    return lax.ppermute(array, SPACE, [(0, 0), (last, last)] + pairs + [(j, i) for i, j in pairs])
 
 
 def settled(running, gain):
@@ -109,14 +108,19 @@
 
 
 def first_far_kernel(
-    local_ref, across, near_ref, weight_ref, gain_ref, parent_ref, middle_ref, select_ref, picked_ref
+    local_ref, across, near_ref, weight_ref, gain_ref, parent_ref, cotangent_ref,
+    middle_ref, select_ref, picked_ref,
 ):
     total = convolved(local_ref[...], across[...], near_ref, weight_ref, select_ref, picked_ref)
     rows = total.shape[0]
     middle_ref[:rows] = settled(total, gain_ref[...]).astype(middle_ref.dtype)
-    ids = parent_ref[...] - lax.axis_index(SPACE) * PAR_ROWS
-    ids = jnp.broadcast_to(ids.astype(jnp.float32), (middle_ref.shape[0] - rows, ids.shape[1]))
-    middle_ref[rows:] = ids.astype(middle_ref.dtype)
+    half, wide = cotangent_ref.shape
+    for j in range(wide // rows):
+        middle_ref[rows + j * half : rows + (j + 1) * half] = cotangent_ref[:, j * rows : (j + 1) * rows]
+    ids = parent_ref[...] - lax.axis_index(SPACE) * half
+    last = rows + half * (wide // rows)
+    ids = jnp.broadcast_to(ids.astype(jnp.float32), (middle_ref.shape[0] - last, ids.shape[1]))
+    middle_ref[last:] = ids.astype(middle_ref.dtype)
 
 
 def second_near_kernel(local_ref, here, partner, near_ref, select_ref):
@@ -130,7 +134,7 @@
 
 def second_far_kernel(
     local_ref, across, partner, near_ref, weight_ref, gain_ref, feature_ref, parent_ref,
-    cotangent_ref, after_ref,
+    cotangent_ref,
     fine_ref, own_ref, sent_ref, grad_ref, select_ref, picked_ref,
 ):
     rows, chans = feature_ref.shape
@@ -138,7 +142,8 @@
     fine = feature_ref[...].astype(jnp.float32) + settled(total, gain_ref[...])
     fine = fine.astype(fine_ref.dtype)
     fine_ref[...] = fine
-    half = cotangent_ref.shape[0]
+    half, wide = cotangent_ref.shape
+    last = rows + half * (wide // rows)
     member = membership(parent_ref[...] - lax.axis_index(SPACE) * half, 2 * half)
     sums = jnp.dot(member.astype(jnp.bfloat16), fine, preferred_element_type=jnp.float32)
 
@@ -146,10 +151,11 @@
         return jnp.sum(membership(ids, 2 * half), axis=1, keepdims=True)
 
     tally_own = jnp.sum(member, axis=1, keepdims=True)
-    tally_partner = tally(partner[rows:].astype(jnp.float32)[:1].astype(jnp.int32))
-    tally_across = tally(across[rows:].astype(jnp.float32)[:1].astype(jnp.int32))
+    tally_partner = tally(partner[last:].astype(jnp.float32)[:1].astype(jnp.int32))
+    tally_across = tally(across[last:].astype(jnp.float32)[:1].astype(jnp.int32))
     upper = lax.axis_index("core") == 1
     tally_before = jnp.where(upper, tally_partner, tally_across)[half:]
+    tally_before = jnp.where(lax.axis_index(SPACE) == 0, 0.0, tally_before)
     tally_after = jnp.where(upper, tally_across, tally_partner)[:half]
     count_own = jnp.maximum(tally_own[:half] + tally_before, 1.0)
     count_after = jnp.maximum(tally_own[half:] + tally_after, 1.0)
@@ -157,7 +163,9 @@
     own_ref[:, chans:] = jnp.broadcast_to(count_own, (half, own_ref.shape[1] - chans))
     sent_ref[...] = sums[half:]
     shares = sums / jnp.concatenate([count_own, count_after], axis=0)
-    grads_in = jnp.concatenate([cotangent_ref[...], after_ref[...]], axis=0)
+    after = jnp.where(upper, across[rows:last], partner[rows:last])
+    after = jnp.concatenate([after[j * half : (j + 1) * half] for j in range(wide // rows)], axis=1)
+    grads_in = jnp.concatenate([cotangent_ref[...], after], axis=0)
     grad_ref[...] = lax.dot_general(
         shares.astype(jnp.bfloat16), grads_in, (((0,), (0,)), ((), ())), preferred_element_type=jnp.float32
     ).astype(grad_ref.dtype)
@@ -234,15 +242,12 @@
         (jnp.moveaxis(neighbours, 1, 0), field, from_partner(field)),
         "first_near", select, 2 * product,
     )
-    ready, near = lax.optimization_barrier((grad_in, near))
-    after = shifted(ready, -1)
     middle = in_vmem(
         first_far_kernel,
-        bf16((rows + 16, chans)),
-        (local, across, near, conv_first, gain_first[None], parents),
+        bf16((rows + par_rows * (out_chans // chans) + 16, chans)),
+        (local, across, near, conv_first, gain_first[None], parents, grad_in),
         "first_far", select_and_picked, 2 * product,
     )
-    middle, after = lax.optimization_barrier((middle, after))
     across = from_across(middle)
     partner = from_partner(middle)
     near = in_vmem(
@@ -258,15 +263,15 @@
         ),
         (
             local, across, partner, near, conv_second, gain_second[None], field, parents,
-            grad_in, after,
+            grad_in,
         ),
         "second_far", select_and_picked, 2 * product,
     )
     parts = plane_summed(local_grad)
-    sent, parts = lax.optimization_barrier((sent, parts))
     coarse = in_vmem(
         coarse_kernel, bf16((par_rows, out_chans)), (own, shifted(sent, 1), down_weight), "coarse"
     )
+    coarse, parts = lax.optimization_barrier((coarse, parts))
     worlds_all = lax.axis_size(DP)
     parents_all = par_rows * lax.axis_size(SPACE)
     down_grad = finished(parts, 1.0 / math.sqrt(worlds_all * parents_all))

time: 78.4 us -> 75.7 us (0.966)
  blocking collectives: 37.1 us -> 32.1 us
  starting transfers between devices: 19.3 us -> 21.8 us
    all_to_all x2, blocking collectives: 37.1 us -> 32.1 us  [exchanged(): return lax.all_to_all(pieces, axes, 0, 0, tiled=True)]
    all_to_all x1, starting transfers between devices: 5.35 us -> 9.55 us  [exchanged(): return lax.all_to_all(pieces, axes, 0, 0, tiled=True)]
    ppermute x2 -> x1, starting transfers between devices: 5.47 us -> 3.54 us  [shifted(): lax.ppermute(array, SPACE, [(i, i + by) for i in range(length) if 0 <= i...]
    ppermute x2, waiting for transfers between devices: 1.03 us -> 2.53 us  [from_across(): lax.ppermute(array, SPACE, [(0, 0), (last, last)] + pairs + [(j, i) for i...]
    ppermute x2 -> x1, waiting for transfers between devices: 2.59 us -> 1.31 us  [shifted(): lax.ppermute(array, SPACE, [(i, i + by) for i in range(length) if 0 <= i...]
  transfers between devices with their start and end apart: 7 -> 6, of which waited for: 4 -> 4; matrix products, arithmetic and copies ran while one was open for 0% -> 0% of each run, Pallas kernels for 10% -> 7%
where the time goes in v4:
time: 75.7 us; the launch traced here: 75.4 us
  blocking collectives  32.1 us (42%)
  starting transfers between devices  21.8 us (29%)
  Pallas kernels  11 us (15%)
  waiting for transfers between devices  7.04 us (9%)
  local copies, waits for them, and re-layouts  1.71 us (2%)
  other arithmetic  0.92 us (1%)
  between operations  0.79 us (1%)
    all_to_all x2, blocking collectives, exchanged(): return lax.all_to_all(pieces, axes, 0, 0, tiled=True)  32.1 us
    pallas_call x5, Pallas kernels, in_vmem(): pl.pallas_call(kernel, out_shape=outs, in_specs=[vmem] * len(inputs), out...  11 us
    all_to_all x1, starting transfers between devices, exchanged(): return lax.all_to_all(pieces, axes, 0, 0, tiled=True)  9.55 us
    ppermute x2, starting transfers between devices, from_across(): lax.ppermute(array, SPACE, [(0, 0), (last, last)] + pairs + [(j, i) for i...  5.24 us
    ppermute x1, starting transfers between devices, shifted(): lax.ppermute(array, SPACE, [(i, i + by) for i in range(length) if 0 <= i...  3.54 us
    ppermute x2, starting transfers between devices, from_partner(): return lax.ppermute(array, SPACE, [(i, i ^ 1) for i in range(length)])  3.42 us
    all_to_all x1, waiting for transfers between devices, exchanged(): return lax.all_to_all(pieces, axes, 0, 0, tiled=True)  3.2 us
    ppermute x2, waiting for transfers between devices, from_across(): lax.ppermute(array, SPACE, [(0, 0), (last, last)] + pairs + [(j, i) for i...  2.53 us
  transfers between devices with their start and end apart: 6, of which 4 were waited for; matrix products, arithmetic and copies ran while one was open for 0% of the time, Pallas kernels for 7%

profile of v4, /device:TPU:1, one launch (start us, length us, event | category | flops | bytes accessed | tf_op | source)
XLA Modules:
  0.0 75.4 jit_solution(1105110855011629546)
XLA Ops:
  0.7 3.3 %collective-permute-start = (bf16[256,256]{1,0:T(8,128)(2,1)}, bf16[256,256]{1,0:T(8,128)(2,1)S(1)}, u32[]{:S(2)}, u32[]{:S(2)}) collective-permute-start(bf16[256,256]{1,0:T(8,128)(2,1)} %bitcast.13), channel_id=1, source_target_pairs={{0,1},{1,0},{2,3},{3,2},{4,5},{5,4},{6,7},{7,6},{8,9},{9,8},{10,11... | collective-permute-start | bytes 393224 | tf_op jit(solution)/shard_map/ppermute | solution.py:33
  4.0 1.9 %collective-permute-start.1 = (bf16[256,256]{1,0:T(8,128)(2,1)}, bf16[256,256]{1,0:T(8,128)(2,1)S(1)}, u32[]{:S(2)}, u32[]{:S(2)}) collective-permute-start(bf16[256,256]{1,0:T(8,128)(2,1)} %bitcast.14), channel_id=1, source_target_pairs={{0,0},{63,63},{1,2},{3,4},{5,6},{7,8},{9,10},{11,12},{13,14},{15,1... | collective-permute-start | bytes 393224 | tf_op jit(solution)/shard_map/ppermute | solution.py:39
  5.9 0.0 collective-permute-done.partner
  5.9 0.9 %copy-done.4 = bf16[1,256,256]{2,1,0:T(8,128)(2,1)S(1)} copy-done((bf16[1,256,256]{2,1,0:T(8,128)(2,1)S(1)}, bf16[1,256,256]{2,1,0:T(8,128)(2,1)}, u32[]{:S(2)}) %copy-start.4) | copy-done | bytes 131096
  6.8 0.7 copy-done.8
  7.6 2.3 %first_near.1 = (bf16[256,6912]{1,0:T(8,128)(2,1)S(1)}, s32[256,32]{1,0:T(8,128)S(1)}) custom-call(s32[27,1,256]{2,1,0:T(1,128)S(1)} %bitcast.19, bf16[256,256]{1,0:T(8,128)(2,1)S(1)} %bitcast.15, bf16[256,256]{1,0:T(8,128)(2,1)S(1)} %collective-permute-done.partner), custom_call_target="tpu_custom_call" | custom-call | flops 1811939328 | bytes 1048576 | tf_op jit(solution)/shard_map/first_near/pallas_call | solution.py:183
  9.9 0.6 collective-permute-done.1.across
  10.5 2.3 %first_far.1.here = bf16[400,256]{1,0:T(8,128)(2,1)S(1)} custom-call(s32[256,32]{1,0:T(8,128)S(1)} %get-tuple-element.11.local_ref, bf16[256,256]{1,0:T(8,128)(2,1)S(1)} %collective-permute-done.1.across, bf16[256,6912]{1,0:T(8,128)(2,1)S(1)} %get-tuple-element.12.near_ref, bf16[27,256,256]{2,1,0:T(8,128)(2,1)S(1)} %copy-done, f32[1,256]{1,0:T(1,128)S(1)} %bitcast.17, ...), custom_call_target="tpu_custom_call" | custom-call | flops 1811939328 | bytes 1048576 | tf_op jit(solution)/shard_map/first_far/pallas_call | solution.py:183
  12.8 0.0 copy-start.1
  12.8 0.0 copy-start.7
  12.8 0.1 collective-permute-start.3
  12.9 3.3 %collective-permute-start.2 = (bf16[400,256]{1,0:T(8,128)(2,1)S(1)}, bf16[400,256]{1,0:T(8,128)(2,1)S(1)}, u32[]{:S(2)}, u32[]{:S(2)}) collective-permute-start(bf16[400,256]{1,0:T(8,128)(2,1)S(1)} %first_far.1.here), channel_id=1, source_target_pairs={{0,0},{63,63},{1,2},{3,4},{5,6},{7,8},{9,10},{11,12},{13,14},{15,1... | collective-permute-start | bytes 614408 | tf_op jit(solution)/shard_map/ppermute | solution.py:39
  16.3 0.0 collective-permute-done.3.partner
  16.3 2.0 %second_near.1.near_ref = bf16[256,6912]{1,0:T(8,128)(2,1)S(1)} custom-call(s32[256,32]{1,0:T(8,128)S(1)} %get-tuple-element.11.local_ref, bf16[400,256]{1,0:T(8,128)(2,1)S(1)} %first_far.1.here, bf16[400,256]{1,0:T(8,128)(2,1)S(1)} %collective-permute-done.3.partner), custom_call_target="tpu_custom_call" | custom-call | flops 1811939328 | bytes 1048576 | tf_op jit(solution)/shard_map/second_near/pallas_call | solution.py:183
  18.3 1.9 %collective-permute-done.2.across = bf16[400,256]{1,0:T(8,128)(2,1)S(1)} collective-permute-done((bf16[400,256]{1,0:T(8,128)(2,1)S(1)}, bf16[400,256]{1,0:T(8,128)(2,1)S(1)}, u32[]{:S(2)}, u32[]{:S(2)}) %collective-permute-start.2) | collective-permute-done | bytes 204832 | tf_op jit(solution)/shard_map/ppermute | solution.py:39
  20.3 3.5 %second_far.1 = (bf16[256,256]{1,0:T(8,128)(2,1)}, f32[64,384]{1,0:T(8,128)S(1)}, f32[64,256]{1,0:T(8,128)S(1)}, bf16[256,512]{1,0:T(8,128)(2,1)}) custom-call(s32[256,32]{1,0:T(8,128)S(1)} %get-tuple-element.11.local_ref, bf16[400,256]{1,0:T(8,128)(2,1)S(1)} %collective-permute-done.2.across, bf16[400,256]{1,0:T(8,128)(2,1)S(1)} %collective-permute-done.3.partner, ...), custom_call_target="tpu_custom_call" | custom-call | flops 1811939328 | bytes 1048576 | tf_op jit(solution)/shard_map/second_far/pallas_call | solution.py:183
  23.8 9.6 %all-to-all-start = ((bf16[32,8,512]{2,1,0:T(8,128)(2,1)}), bf16[32,8,512]{2,1,0:T(8,128)(2,1)S(1)}, u32[]{:S(2)}, u32[]{:S(2)}) async-start(bf16[32,8,512]{2,1,0:T(8,128)(2,1)} %bitcast.6), calls=%async_computation | async-start | bytes 524288 | tf_op jit(solution)/shard_map/all_to_all | solution.py:196
  33.4 3.5 %collective-permute-start.4 = (f32[64,256]{1,0:T(8,128)S(1)}, f32[64,256]{1,0:T(8,128)S(1)}, u32[]{:S(2)}, u32[]{:S(2)}) collective-permute-start(f32[64,256]{1,0:T(8,128)S(1)} %get-tuple-element.15), channel_id=1, source_target_pairs={{0,1},{1,2},{2,3},{3,4},{4,5},{5,6},{6,7},{7,8},{8,9},{9,10},{10,1... | collective-permute-start | bytes 196616 | tf_op jit(solution)/shard_map/ppermute | solution.py:28
  36.9 1.3 %collective-permute-done.4.moved_ref = f32[64,256]{1,0:T(8,128)S(1)} collective-permute-done((f32[64,256]{1,0:T(8,128)S(1)}, f32[64,256]{1,0:T(8,128)S(1)}, u32[]{:S(2)}, u32[]{:S(2)}) %collective-permute-start.4) | collective-permute-done | bytes 65568 | tf_op jit(solution)/shard_map/ppermute | solution.py:28
  38.2 0.8 %coarse.1 = bf16[64,512]{1,0:T(8,128)(2,1)} custom-call(f32[64,384]{1,0:T(8,128)S(1)} %get-tuple-element.14.own_ref, f32[64,256]{1,0:T(8,128)S(1)} %collective-permute-done.4.moved_ref, bf16[256,512]{1,0:T(8,128)(2,1)S(1)} %copy-done.3), custom_call_target="tpu_custom_call" | custom-call | bytes 1048576 | tf_op jit(solution)/shard_map/coarse/pallas_call | solution.py:183
  39.1 3.2 %all-to-all-done = bf16[32,8,512]{2,1,0:T(8,128)(2,1)S(1)} async-done(((bf16[32,8,512]{2,1,0:T(8,128)(2,1)}), bf16[32,8,512]{2,1,0:T(8,128)(2,1)S(1)}, u32[]{:S(2)}, u32[]{:S(2)}) %all-to-all-start) | async-done | bytes 262176 | tf_op jit(solution)/shard_map/all_to_all | solution.py:196
  42.3 16.3 %all_to_all.15 = f32[8,8,512]{2,1,0:T(8,128)S(1)} all-to-all(f32[8,8,512]{2,1,0:T(8,128)S(1)} %broadcast_in_dim.28), channel_id=1, replica_groups=mesh['y'=4,'z'=8,'x'=4,'core'=2] {'z'}, dimensions={0} | all-to-all | bytes 262144 | tf_op jit(solution)/shard_map/all_to_all | solution.py:196
  58.7 15.9 %all_to_all.16 = bf16[32,8,512]{2,1,0:T(8,128)(2,1)S(1)} all-to-all(bf16[32,8,512]{2,1,0:T(8,128)(2,1)S(1)} %broadcast_in_dim.29), channel_id=1, replica_groups=mesh['y'=4,'z'=8,'x'=4,'core'=2] {'y','x','core'}, dimensions={0} | all-to-all | bytes 524288 | tf_op jit(solution)/shard_map/all_to_all | solution.py:196
  74.5 0.9 %bitcast_convert_fusion = f32[256,512]{1,0:T(8,128)} fusion(bf16[32,8,512]{2,1,0:T(8,128)(2,1)S(1)} %all_to_all.16), kind=kLoop, calls=%fused_computation.1 | loop fusion | flops 131072 | bytes 786432 | tf_op jit(solution)/shard_map/reshape | solution.py:211
  (19 shorter events, 0.1 us)
Async XLA Ops:
  0.6 9.8 %copy-start.2 = (bf16[1,64,512]{2,1,0:T(8,128)(2,1)S(1)}, bf16[1,64,512]{2,1,0:T(8,128)(2,1)}, u32[]{:S(2)}) copy-start(bf16[1,64,512]{2,1,0:T(8,128)(2,1)} %param.17) | copy-start | bytes 196612
  0.6 9.8 %copy-start = (bf16[27,256,256]{2,1,0:T(8,128)(2,1)S(1)}, bf16[27,256,256]{2,1,0:T(8,128)(2,1)}, u32[]{:S(2)}) copy-start(bf16[27,256,256]{2,1,0:T(8,128)(2,1)} %weight_ref.2) | copy-start | bytes 10616836
  0.7 5.2 %collective-permute-start = (bf16[256,256]{1,0:T(8,128)(2,1)}, bf16[256,256]{1,0:T(8,128)(2,1)S(1)}, u32[]{:S(2)}, u32[]{:S(2)}) collective-permute-start(bf16[256,256]{1,0:T(8,128)(2,1)} %bitcast.13), channel_id=1, source_target_pairs={{0,1},{1,0},{2,3},{3,2},{4,5},{5,4},{6,7},{7,6},{8,9},{9,8},{10,11... | collective-permute-start | bytes 393224 | tf_op jit(solution)/shard_map/ppermute | solution.py:33
  4.0 6.5 %collective-permute-start.1 = (bf16[256,256]{1,0:T(8,128)(2,1)}, bf16[256,256]{1,0:T(8,128)(2,1)S(1)}, u32[]{:S(2)}, u32[]{:S(2)}) collective-permute-start(bf16[256,256]{1,0:T(8,128)(2,1)} %bitcast.14), channel_id=1, source_target_pairs={{0,0},{63,63},{1,2},{3,4},{5,6},{7,8},{9,10},{11,12},{13,14},{15,1... | collective-permute-start | bytes 393224 | tf_op jit(solution)/shard_map/ppermute | solution.py:39
  5.9 0.9 %copy-start.4 = (bf16[1,256,256]{2,1,0:T(8,128)(2,1)S(1)}, bf16[1,256,256]{2,1,0:T(8,128)(2,1)}, u32[]{:S(2)}) copy-start(bf16[1,256,256]{2,1,0:T(8,128)(2,1)} %param.9) | copy-start | bytes 393220
  6.8 0.7 copy-start.8
  7.6 2.9 %copy-start.5 = (s32[1,256]{1,0:T(1,128)S(1)}, s32[1,256]{1,0:T(1,128)}, u32[]{:S(2)}) copy-start(s32[1,256]{1,0:T(1,128)} %parent_ref.3) | copy-start | bytes 3076
  7.6 2.9 %copy-start.6 = (f32[256]{0:T(256)S(1)}, f32[256]{0:T(256)}, u32[]{:S(2)}) copy-start(f32[256]{0:T(256)} %param.14) | copy-start | bytes 3076
  12.8 7.5 %copy-start.1 = (bf16[27,256,256]{2,1,0:T(8,128)(2,1)S(1)}, bf16[27,256,256]{2,1,0:T(8,128)(2,1)}, u32[]{:S(2)}) copy-start(bf16[27,256,256]{2,1,0:T(8,128)(2,1)} %weight_ref.3) | copy-start | bytes 10616836
  12.8 7.5 %copy-start.7 = (f32[256]{0:T(256)S(1)}, f32[256]{0:T(256)}, u32[]{:S(2)}) copy-start(f32[256]{0:T(256)} %param.15) | copy-start | bytes 3076
  12.8 3.4 %collective-permute-start.3 = (bf16[400,256]{1,0:T(8,128)(2,1)S(1)}, bf16[400,256]{1,0:T(8,128)(2,1)S(1)}, u32[]{:S(2)}, u32[]{:S(2)}) collective-permute-start(bf16[400,256]{1,0:T(8,128)(2,1)S(1)} %first_far.1.here), channel_id=1, source_target_pairs={{0,1},{1,0},{2,3},{3,2},{4,5},{5,4},{6,7},{7,6},{8,9},{9,8},{10,11... | collective-permute-start | bytes 614408 | tf_op jit(solution)/shard_map/ppermute | solution.py:33
  12.9 7.3 %collective-permute-start.2 = (bf16[400,256]{1,0:T(8,128)(2,1)S(1)}, bf16[400,256]{1,0:T(8,128)(2,1)S(1)}, u32[]{:S(2)}, u32[]{:S(2)}) collective-permute-start(bf16[400,256]{1,0:T(8,128)(2,1)S(1)} %first_far.1.here), channel_id=1, source_target_pairs={{0,0},{63,63},{1,2},{3,4},{5,6},{7,8},{9,10},{11,12},{13,14},{15,1... | collective-permute-start | bytes 614408 | tf_op jit(solution)/shard_map/ppermute | solution.py:39
  20.3 17.9 %copy-start.3 = (bf16[256,512]{1,0:T(8,128)(2,1)S(1)}, bf16[256,512]{1,0:T(8,128)(2,1)}, u32[]{:S(2)}) copy-start(bf16[256,512]{1,0:T(8,128)(2,1)} %down_ref.1) | copy-start | bytes 786436
  23.8 18.5 %all-to-all-start = ((bf16[32,8,512]{2,1,0:T(8,128)(2,1)}), bf16[32,8,512]{2,1,0:T(8,128)(2,1)S(1)}, u32[]{:S(2)}, u32[]{:S(2)}) async-start(bf16[32,8,512]{2,1,0:T(8,128)(2,1)} %bitcast.6), calls=%async_computation | async-start | bytes 524288 | tf_op jit(solution)/shard_map/all_to_all | solution.py:196
  33.4 4.9 %collective-permute-start.4 = (f32[64,256]{1,0:T(8,128)S(1)}, f32[64,256]{1,0:T(8,128)S(1)}, u32[]{:S(2)}, u32[]{:S(2)}) collective-permute-start(f32[64,256]{1,0:T(8,128)S(1)} %get-tuple-element.15), channel_id=1, source_target_pairs={{0,1},{1,2},{2,3},{3,4},{4,5},{5,6},{6,7},{7,8},{8,9},{9,10},{10,1... | collective-permute-start | bytes 196616 | tf_op jit(solution)/shard_map/ppermute | solution.py:28

commit v5 on v4

--- a/solution.py
+++ b/solution.py
@@ -25,18 +25,12 @@
 
 def shifted(array, by):
     length = lax.axis_size(SPACE)
-    return lax.ppermute(array, SPACE, [(i, i + by) for i in range(length) if 0 <= i + by < length])
+    return lax.ppermute(array, SPACE, [(i, (i + by) % length) for i in range(length)])
 
 
 def from_partner(array):
     length = lax.axis_size(SPACE)
     return lax.ppermute(array, SPACE, [(i, i ^ 1) for i in range(length)])
-
-
-def from_across(array):
-    last = lax.axis_size(SPACE) - 1
-    pairs = [(i, i + 1) for i in range(1, last, 2)]
-    return lax.ppermute(array, SPACE, [(0, 0), (last, last)] + pairs + [(j, i) for i, j in pairs])
 
 
 def settled(running, gain):
@@ -85,8 +79,9 @@
     pick(local, near_ref.shape[1] // chans, blocks, select_ref, put)
 
 
-def convolved(local, across, near_ref, weight_ref, select_ref, picked_ref):
-    rows, chans = across.shape
+def convolved(local, before, after, near_ref, weight_ref, select_ref, picked_ref):
+    rows, chans = before.shape
+    across = jnp.where(lax.axis_index("core") == 1, after, before)
     taps = weight_ref.shape[0]
 
     def put(tap, picked):
@@ -108,19 +103,21 @@
 
 
 def first_far_kernel(
-    local_ref, across, near_ref, weight_ref, gain_ref, parent_ref, cotangent_ref,
-    middle_ref, select_ref, picked_ref,
+    local_ref, before, after, near_ref, weight_ref, gain_ref, parent_ref, cotangent_ref,
+    middle_ref, wide_ref, select_ref, picked_ref,
 ):
-    total = convolved(local_ref[...], across[...], near_ref, weight_ref, select_ref, picked_ref)
+    total = convolved(local_ref[...], before[...], after[...], near_ref, weight_ref, select_ref, picked_ref)
     rows = total.shape[0]
-    middle_ref[:rows] = settled(total, gain_ref[...]).astype(middle_ref.dtype)
+    middle = settled(total, gain_ref[...]).astype(middle_ref.dtype)
+    middle_ref[:rows] = middle
+    wide_ref[:rows] = middle
     half, wide = cotangent_ref.shape
     for j in range(wide // rows):
-        middle_ref[rows + j * half : rows + (j + 1) * half] = cotangent_ref[:, j * rows : (j + 1) * rows]
+        wide_ref[rows + j * half : rows + (j + 1) * half] = cotangent_ref[:, j * rows : (j + 1) * rows]
     ids = parent_ref[...] - lax.axis_index(SPACE) * half
-    last = rows + half * (wide // rows)
-    ids = jnp.broadcast_to(ids.astype(jnp.float32), (middle_ref.shape[0] - last, ids.shape[1]))
-    middle_ref[last:] = ids.astype(middle_ref.dtype)
+    ids = jnp.broadcast_to(ids.astype(jnp.float32), (middle_ref.shape[0] - rows, ids.shape[1]))
+    middle_ref[rows:] = ids.astype(middle_ref.dtype)
+    wide_ref[rows + half * (wide // rows) :] = ids.astype(wide_ref.dtype)
 
 
 def second_near_kernel(local_ref, here, partner, near_ref, select_ref):
@@ -133,12 +130,12 @@
 
 
 def second_far_kernel(
-    local_ref, across, partner, near_ref, weight_ref, gain_ref, feature_ref, parent_ref,
+    local_ref, before, after, near_ref, weight_ref, gain_ref, feature_ref, parent_ref,
     cotangent_ref,
     fine_ref, own_ref, sent_ref, grad_ref, select_ref, picked_ref,
 ):
     rows, chans = feature_ref.shape
-    total = convolved(local_ref[...], across[:rows], near_ref, weight_ref, select_ref, picked_ref)
+    total = convolved(local_ref[...], before[:rows], after[:rows], near_ref, weight_ref, select_ref, picked_ref)
     fine = feature_ref[...].astype(jnp.float32) + settled(total, gain_ref[...])
     fine = fine.astype(fine_ref.dtype)
     fine_ref[...] = fine
@@ -151,21 +148,17 @@
         return jnp.sum(membership(ids, 2 * half), axis=1, keepdims=True)
 
     tally_own = jnp.sum(member, axis=1, keepdims=True)
-    tally_partner = tally(partner[last:].astype(jnp.float32)[:1].astype(jnp.int32))
-    tally_across = tally(across[last:].astype(jnp.float32)[:1].astype(jnp.int32))
-    upper = lax.axis_index("core") == 1
-    tally_before = jnp.where(upper, tally_partner, tally_across)[half:]
-    tally_before = jnp.where(lax.axis_index(SPACE) == 0, 0.0, tally_before)
-    tally_after = jnp.where(upper, tally_across, tally_partner)[:half]
+    tally_before = tally(before[rows:].astype(jnp.float32)[:1].astype(jnp.int32))[half:]
+    tally_after = tally(after[last:].astype(jnp.float32)[:1].astype(jnp.int32))[:half]
     count_own = jnp.maximum(tally_own[:half] + tally_before, 1.0)
     count_after = jnp.maximum(tally_own[half:] + tally_after, 1.0)
     own_ref[:, :chans] = sums[:half]
     own_ref[:, chans:] = jnp.broadcast_to(count_own, (half, own_ref.shape[1] - chans))
     sent_ref[...] = sums[half:]
     shares = sums / jnp.concatenate([count_own, count_after], axis=0)
-    after = jnp.where(upper, across[rows:last], partner[rows:last])
-    after = jnp.concatenate([after[j * half : (j + 1) * half] for j in range(wide // rows)], axis=1)
-    grads_in = jnp.concatenate([cotangent_ref[...], after], axis=0)
+    next_grads = after[rows:last]
+    next_grads = jnp.concatenate([next_grads[j * half : (j + 1) * half] for j in range(wide // rows)], axis=1)
+    grads_in = jnp.concatenate([cotangent_ref[...], next_grads], axis=0)
     grad_ref[...] = lax.dot_general(
         shares.astype(jnp.bfloat16), grads_in, (((0,), (0,)), ((), ())), preferred_element_type=jnp.float32
     ).astype(grad_ref.dtype)
@@ -235,20 +228,20 @@
         pltpu.VMEM((taps * rows, rows), jnp.bfloat16),
         pltpu.VMEM((rows, taps * chans), jnp.bfloat16),
     ]
-    across = from_across(field)
+    before, after = shifted(field, 1), shifted(field, -1)
     near, local = in_vmem(
         first_near_kernel,
         (near_shape, jax.ShapeDtypeStruct((rows, taps + -taps % 8), jnp.int32)),
         (jnp.moveaxis(neighbours, 1, 0), field, from_partner(field)),
         "first_near", select, 2 * product,
     )
-    middle = in_vmem(
+    middle, wide = in_vmem(
         first_far_kernel,
-        bf16((rows + par_rows * (out_chans // chans) + 16, chans)),
-        (local, across, near, conv_first, gain_first[None], parents, grad_in),
+        (bf16((rows + 16, chans)), bf16((rows + par_rows * (out_chans // chans) + 16, chans))),
+        (local, before, after, near, conv_first, gain_first[None], parents, grad_in),
         "first_far", select_and_picked, 2 * product,
     )
-    across = from_across(middle)
+    before, after = shifted(middle, 1), shifted(wide, -1)
     partner = from_partner(middle)
     near = in_vmem(
         second_near_kernel, near_shape, (local, middle, partner), "second_near", select, 2 * product
@@ -262,16 +255,14 @@
             bf16((chans, out_chans)),
         ),
         (
-            local, across, partner, near, conv_second, gain_second[None], field, parents,
+            local, before, after, near, conv_second, gain_second[None], field, parents,
             grad_in,
         ),
         "second_far", select_and_picked, 2 * product,
     )
     parts = plane_summed(local_grad)
-    coarse = in_vmem(
-        coarse_kernel, bf16((par_rows, out_chans)), (own, shifted(sent, 1), down_weight), "coarse"
-    )
-    coarse, parts = lax.optimization_barrier((coarse, parts))
+    moved, parts = lax.optimization_barrier((shifted(sent, 1), parts))
+    coarse = in_vmem(coarse_kernel, bf16((par_rows, out_chans)), (own, moved, down_weight), "coarse")
     worlds_all = lax.axis_size(DP)
     parents_all = par_rows * lax.axis_size(SPACE)
     down_grad = finished(parts, 1.0 / math.sqrt(worlds_all * parents_all))

time: 75.7 us -> 74.3 us (0.982)
  blocking collectives: 32.1 us -> 11.4 us
  waiting for transfers between devices: 7.04 us -> 18.8 us
  starting transfers between devices: 21.8 us -> 28.5 us
    all_to_all x2 -> x1, blocking collectives: 32.1 us -> 11.4 us  [exchanged(): return lax.all_to_all(pieces, axes, 0, 0, tiled=True)]
    all_to_all x1 -> x2, waiting for transfers between devices: 3.2 us -> 13.3 us  [exchanged(): return lax.all_to_all(pieces, axes, 0, 0, tiled=True)]
    ppermute x2, starting transfers between devices: 3.42 us -> 10.3 us  [from_partner(): return lax.ppermute(array, SPACE, [(i, i ^ 1) for i in range(length)])]
    ppermute x3 -> x5, starting transfers between devices: 8.78 us -> 5.2 us  [shifted(): lax.ppermute(array, SPACE, [(i, (i + by) % length) for i in range(length)])]
    all_to_all x1 -> x2, starting transfers between devices: 9.55 us -> 13 us  [exchanged(): return lax.all_to_all(pieces, axes, 0, 0, tiled=True)]
    ppermute x3 -> x5, waiting for transfers between devices: 3.84 us -> 5.49 us  [shifted(): lax.ppermute(array, SPACE, [(i, (i + by) % length) for i in range(length)])]
    unnamed x18 -> x20, local copies, waits for them, and re-layouts: 1.67 us -> 1.72 us
  transfers between devices with their start and end apart: 6 -> 9, of which waited for: 4 -> 5; matrix products, arithmetic and copies ran while one was open for 0% -> 0% of each run, Pallas kernels for 7% -> 7%
where the time goes in v5:
time: 74.3 us; the launch traced here: 73.9 us
  starting transfers between devices  28.5 us (38%)
  waiting for transfers between devices  18.8 us (25%)
  blocking collectives  11.4 us (15%)
  Pallas kernels  11 us (15%)
  local copies, waits for them, and re-layouts  2.45 us (3%)
  other arithmetic  0.92 us (1%)
  between operations  0.78 us (1%)
    all_to_all x2, waiting for transfers between devices, exchanged(): return lax.all_to_all(pieces, axes, 0, 0, tiled=True)  13.3 us
    all_to_all x2, starting transfers between devices, exchanged(): return lax.all_to_all(pieces, axes, 0, 0, tiled=True)  13 us
    all_to_all x1, blocking collectives, exchanged(): return lax.all_to_all(pieces, axes, 0, 0, tiled=True)  11.4 us
    pallas_call x5, Pallas kernels, in_vmem(): pl.pallas_call(kernel, out_shape=outs, in_specs=[vmem] * len(inputs), out...  11 us
    ppermute x2, starting transfers between devices, from_partner(): return lax.ppermute(array, SPACE, [(i, i ^ 1) for i in range(length)])  10.3 us
    ppermute x5, waiting for transfers between devices, shifted(): lax.ppermute(array, SPACE, [(i, (i + by) % length) for i in range(length)])  5.49 us
    ppermute x5, starting transfers between devices, shifted(): lax.ppermute(array, SPACE, [(i, (i + by) % length) for i in range(length)])  5.2 us
    unnamed x20, local copies, waits for them, and re-layouts  1.72 us
  transfers between devices with their start and end apart: 9, of which 5 were waited for; matrix products, arithmetic and copies ran while one was open for 0% of the time, Pallas kernels for 7%

profile of v5, /device:TPU:1, one launch (start us, length us, event | category | flops | bytes accessed | tf_op | source)
XLA Modules:
  0.0 73.9 jit_solution(3245579941089718202)
XLA Ops:
  0.7 3.3 %collective-permute-start = (bf16[256,256]{1,0:T(8,128)(2,1)}, bf16[256,256]{1,0:T(8,128)(2,1)S(1)}, u32[]{:S(2)}, u32[]{:S(2)}) collective-permute-start(bf16[256,256]{1,0:T(8,128)(2,1)} %bitcast.13), channel_id=1, source_target_pairs={{0,1},{1,0},{2,3},{3,2},{4,5},{5,4},{6,7},{7,6},{8,9},{9,8},{10,11... | collective-permute-start | bytes 393224 | tf_op jit(solution)/shard_map/ppermute | solution.py:33
  4.0 0.1 collective-permute-start.2
  4.1 1.7 %collective-permute-start.1 = (bf16[256,256]{1,0:T(8,128)(2,1)}, bf16[256,256]{1,0:T(8,128)(2,1)S(1)}, u32[]{:S(2)}, u32[]{:S(2)}) collective-permute-start(bf16[256,256]{1,0:T(8,128)(2,1)} %bitcast.15), channel_id=1, source_target_pairs={{0,1},{1,2},{2,3},{3,4},{4,5},{5,6},{6,7},{7,8},{8,9},{9,10},{10,1... | collective-permute-start | bytes 393224 | tf_op jit(solution)/shard_map/ppermute | solution.py:28
  5.7 0.9 %copy-done.4 = bf16[1,256,256]{2,1,0:T(8,128)(2,1)S(1)} copy-done((bf16[1,256,256]{2,1,0:T(8,128)(2,1)S(1)}, bf16[1,256,256]{2,1,0:T(8,128)(2,1)}, u32[]{:S(2)}) %copy-start.4) | copy-done | bytes 131096
  6.7 0.7 %copy-done.9 = s32[1,27,256]{2,0,1:T(1,128)S(1)} copy-done((s32[1,27,256]{2,0,1:T(1,128)S(1)}, s32[1,27,256]{2,0,1:T(1,128)}, u32[]{:S(2)}) %copy-start.9) | copy-done | bytes 27672
  7.4 2.3 %first_near.1 = (bf16[256,6912]{1,0:T(8,128)(2,1)S(1)}, s32[256,32]{1,0:T(8,128)S(1)}) custom-call(s32[27,1,256]{2,1,0:T(1,128)S(1)} %bitcast.20, bf16[256,256]{1,0:T(8,128)(2,1)S(1)} %bitcast.16, bf16[256,256]{1,0:T(8,128)(2,1)S(1)} %collective-permute-done.partner), custom_call_target="tpu_custom_call" | custom-call | flops 1811939328 | bytes 1048576 | tf_op jit(solution)/shard_map/first_near/pallas_call | solution.py:176
  9.7 1.7 %collective-permute-done.1.before = bf16[256,256]{1,0:T(8,128)(2,1)S(1)} collective-permute-done((bf16[256,256]{1,0:T(8,128)(2,1)}, bf16[256,256]{1,0:T(8,128)(2,1)S(1)}, u32[]{:S(2)}, u32[]{:S(2)}) %collective-permute-start.1) | collective-permute-done | bytes 131104 | tf_op jit(solution)/shard_map/ppermute | solution.py:28
  11.5 2.3 %first_far.1 = (bf16[272,256]{1,0:T(8,128)(2,1)S(1)}, bf16[400,256]{1,0:T(8,128)(2,1)S(1)}) custom-call(s32[256,32]{1,0:T(8,128)S(1)} %get-tuple-element.13.local_ref, bf16[256,256]{1,0:T(8,128)(2,1)S(1)} %collective-permute-done.1.before, bf16[256,256]{1,0:T(8,128)(2,1)S(1)} %collective-permute-done.2.after, ...), custom_call_target="tpu_custom_call" | custom-call | flops 1811939328 | bytes 1048576 | tf_op jit(solution)/shard_map/first_far/pallas_call | solution.py:176
  13.8 7.0 %collective-permute-start.5 = (bf16[272,256]{1,0:T(8,128)(2,1)S(1)}, bf16[272,256]{1,0:T(8,128)(2,1)S(1)}, u32[]{:S(2)}, u32[]{:S(2)}) collective-permute-start(bf16[272,256]{1,0:T(8,128)(2,1)S(1)} %get-tuple-element.15.here), channel_id=1, source_target_pairs={{0,1},{1,0},{2,3},{3,2},{4,5},{5,4},{6,7},{7,6},{8,9},{9,8},{10,11... | collective-permute-start | bytes 417800 | tf_op jit(solution)/shard_map/ppermute | solution.py:33
  20.8 0.1 collective-permute-start.4
  20.9 1.7 %collective-permute-start.3 = (bf16[272,256]{1,0:T(8,128)(2,1)S(1)}, bf16[272,256]{1,0:T(8,128)(2,1)S(1)}, u32[]{:S(2)}, u32[]{:S(2)}) collective-permute-start(bf16[272,256]{1,0:T(8,128)(2,1)S(1)} %get-tuple-element.15.here), channel_id=1, source_target_pairs={{0,1},{1,2},{2,3},{3,4},{4,5},{5,6},{6,7},{7,8},{8,9},{9,10},{10,1... | collective-permute-start | bytes 417800 | tf_op jit(solution)/shard_map/ppermute | solution.py:28
  22.5 2.1 %second_near.1.near_ref = bf16[256,6912]{1,0:T(8,128)(2,1)S(1)} custom-call(s32[256,32]{1,0:T(8,128)S(1)} %get-tuple-element.13.local_ref, bf16[272,256]{1,0:T(8,128)(2,1)S(1)} %get-tuple-element.15.here, bf16[272,256]{1,0:T(8,128)(2,1)S(1)} %collective-permute-done.5.partner), custom_call_target="tpu_custom_call" | custom-call | flops 1811939328 | bytes 1048576 | tf_op jit(solution)/shard_map/second_near/pallas_call | solution.py:176
  24.6 1.4 %collective-permute-done.4.after = bf16[400,256]{1,0:T(8,128)(2,1)S(1)} collective-permute-done((bf16[400,256]{1,0:T(8,128)(2,1)S(1)}, bf16[400,256]{1,0:T(8,128)(2,1)S(1)}, u32[]{:S(2)}, u32[]{:S(2)}) %collective-permute-start.4) | collective-permute-done | bytes 204832 | tf_op jit(solution)/shard_map/ppermute | solution.py:28
  26.0 3.5 %second_far.1 = (bf16[256,256]{1,0:T(8,128)(2,1)}, f32[64,384]{1,0:T(8,128)S(1)}, f32[64,256]{1,0:T(8,128)S(1)}, bf16[256,512]{1,0:T(8,128)(2,1)}) custom-call(s32[256,32]{1,0:T(8,128)S(1)} %get-tuple-element.13.local_ref, bf16[272,256]{1,0:T(8,128)(2,1)S(1)} %collective-permute-done.3.before, bf16[400,256]{1,0:T(8,128)(2,1)S(1)} %collective-permute-done.4.after, ...), custom_call_target="tpu_custom_call" | custom-call | flops 1811939328 | bytes 1048576 | tf_op jit(solution)/shard_map/second_far/pallas_call | solution.py:176
  29.5 8.5 %all-to-all-start = ((bf16[32,8,512]{2,1,0:T(8,128)(2,1)}), bf16[32,8,512]{2,1,0:T(8,128)(2,1)S(1)}, u32[]{:S(2)}, u32[]{:S(2)}) async-start(bf16[32,8,512]{2,1,0:T(8,128)(2,1)} %bitcast.6), calls=%async_computation | async-start | bytes 524288 | tf_op jit(solution)/shard_map/all_to_all | solution.py:189
  38.0 1.7 %collective-permute-start.6 = (f32[64,256]{1,0:T(8,128)S(1)}, f32[64,256]{1,0:T(8,128)S(1)}, u32[]{:S(2)}, u32[]{:S(2)}) collective-permute-start(f32[64,256]{1,0:T(8,128)S(1)} %get-tuple-element.19), channel_id=1, source_target_pairs={{0,1},{1,2},{2,3},{3,4},{4,5},{5,6},{6,7},{7,8},{8,9},{9,10},{10,1... | collective-permute-start | bytes 196616 | tf_op jit(solution)/shard_map/ppermute | solution.py:28
  39.7 2.4 %collective-permute-done.6.moved_ref = f32[64,256]{1,0:T(8,128)S(1)} collective-permute-done((f32[64,256]{1,0:T(8,128)S(1)}, f32[64,256]{1,0:T(8,128)S(1)}, u32[]{:S(2)}, u32[]{:S(2)}) %collective-permute-start.6) | collective-permute-done | bytes 65568 | tf_op jit(solution)/shard_map/ppermute | solution.py:28
  42.2 5.1 %all-to-all-done = bf16[32,8,512]{2,1,0:T(8,128)(2,1)S(1)} async-done(((bf16[32,8,512]{2,1,0:T(8,128)(2,1)}), bf16[32,8,512]{2,1,0:T(8,128)(2,1)S(1)}, u32[]{:S(2)}, u32[]{:S(2)}) %all-to-all-start) | async-done | bytes 262176 | tf_op jit(solution)/shard_map/all_to_all | solution.py:189
  47.4 11.4 %all_to_all.15 = f32[8,8,512]{2,1,0:T(8,128)S(1)} all-to-all(f32[8,8,512]{2,1,0:T(8,128)S(1)} %broadcast_in_dim.28), channel_id=1, replica_groups=mesh['y'=4,'z'=8,'x'=4,'core'=2] {'z'}, dimensions={0} | all-to-all | bytes 262144 | tf_op jit(solution)/shard_map/all_to_all | solution.py:189
  58.8 0.7 broadcast_in_dim.29
  59.5 4.5 %all-to-all-start.2 = ((bf16[32,8,512]{2,1,0:T(8,128)(2,1)}), bf16[32,8,512]{2,1,0:T(8,128)(2,1)S(1)}, u32[]{:S(2)}, u32[]{:S(2)}) async-start(bf16[32,8,512]{2,1,0:T(8,128)(2,1)} %broadcast_in_dim.29), calls=%async_computation.2 | async-start | bytes 524288 | tf_op jit(solution)/shard_map/all_to_all | solution.py:189
  64.0 0.8 %coarse.1 = bf16[64,512]{1,0:T(8,128)(2,1)} custom-call(f32[64,384]{1,0:T(8,128)S(1)} %get-tuple-element.18.own_ref, f32[64,256]{1,0:T(8,128)S(1)} %collective-permute-done.6.moved_ref, bf16[256,512]{1,0:T(8,128)(2,1)S(1)} %copy-done.3), custom_call_target="tpu_custom_call" | custom-call | bytes 1048576 | tf_op jit(solution)/shard_map/coarse/pallas_call | solution.py:176
  64.9 8.2 %all-to-all-done.2 = bf16[32,8,512]{2,1,0:T(8,128)(2,1)S(1)} async-done(((bf16[32,8,512]{2,1,0:T(8,128)(2,1)}), bf16[32,8,512]{2,1,0:T(8,128)(2,1)S(1)}, u32[]{:S(2)}, u32[]{:S(2)}) %all-to-all-start.2) | async-done | bytes 262176 | tf_op jit(solution)/shard_map/all_to_all | solution.py:189
  73.0 0.9 %bitcast_convert_fusion = f32[256,512]{1,0:T(8,128)} fusion(bf16[32,8,512]{2,1,0:T(8,128)(2,1)S(1)} %all-to-all-done.2), kind=kLoop, calls=%fused_computation.1 | loop fusion | flops 131072 | bytes 786432 | tf_op jit(solution)/shard_map/reshape | solution.py:204
  (26 shorter events, 0.1 us)
Async XLA Ops:
  0.6 10.8 %copy-start.2 = (bf16[1,64,512]{2,1,0:T(8,128)(2,1)S(1)}, bf16[1,64,512]{2,1,0:T(8,128)(2,1)}, u32[]{:S(2)}) copy-start(bf16[1,64,512]{2,1,0:T(8,128)(2,1)} %param.17) | copy-start | bytes 196612
  0.6 10.8 %copy-start.1 = (bf16[27,256,256]{2,1,0:T(8,128)(2,1)S(1)}, bf16[27,256,256]{2,1,0:T(8,128)(2,1)}, u32[]{:S(2)}) copy-start(bf16[27,256,256]{2,1,0:T(8,128)(2,1)} %weight_ref.2) | copy-start | bytes 10616836
  0.7 5.1 %collective-permute-start = (bf16[256,256]{1,0:T(8,128)(2,1)}, bf16[256,256]{1,0:T(8,128)(2,1)S(1)}, u32[]{:S(2)}, u32[]{:S(2)}) collective-permute-start(bf16[256,256]{1,0:T(8,128)(2,1)} %bitcast.13), channel_id=1, source_target_pairs={{0,1},{1,0},{2,3},{3,2},{4,5},{5,4},{6,7},{7,6},{8,9},{9,8},{10,11... | collective-permute-start | bytes 393224 | tf_op jit(solution)/shard_map/ppermute | solution.py:33
  4.0 5.7 %collective-permute-start.2 = (bf16[256,256]{1,0:T(8,128)(2,1)}, bf16[256,256]{1,0:T(8,128)(2,1)S(1)}, u32[]{:S(2)}, u32[]{:S(2)}) collective-permute-start(bf16[256,256]{1,0:T(8,128)(2,1)} %bitcast.14), channel_id=1, source_target_pairs={{0,63},{1,0},{2,1},{3,2},{4,3},{5,4},{6,5},{7,6},{8,7},{9,8},{10,9... | collective-permute-start | bytes 393224 | tf_op jit(solution)/shard_map/ppermute | solution.py:28
  4.1 7.4 %collective-permute-start.1 = (bf16[256,256]{1,0:T(8,128)(2,1)}, bf16[256,256]{1,0:T(8,128)(2,1)S(1)}, u32[]{:S(2)}, u32[]{:S(2)}) collective-permute-start(bf16[256,256]{1,0:T(8,128)(2,1)} %bitcast.15), channel_id=1, source_target_pairs={{0,1},{1,2},{2,3},{3,4},{4,5},{5,6},{6,7},{7,8},{8,9},{9,10},{10,1... | collective-permute-start | bytes 393224 | tf_op jit(solution)/shard_map/ppermute | solution.py:28
  5.7 0.9 %copy-start.4 = (bf16[1,256,256]{2,1,0:T(8,128)(2,1)S(1)}, bf16[1,256,256]{2,1,0:T(8,128)(2,1)}, u32[]{:S(2)}) copy-start(bf16[1,256,256]{2,1,0:T(8,128)(2,1)} %param.9) | copy-start | bytes 393220
  6.7 0.7 %copy-start.9 = (s32[1,27,256]{2,0,1:T(1,128)S(1)}, s32[1,27,256]{2,0,1:T(1,128)}, u32[]{:S(2)}) copy-start(s32[1,27,256]{2,0,1:T(1,128)} %param.10) | copy-start | bytes 82948
  7.4 4.1 %copy-start.6 = (s32[1,256]{1,0:T(1,128)S(1)}, s32[1,256]{1,0:T(1,128)}, u32[]{:S(2)}) copy-start(s32[1,256]{1,0:T(1,128)} %parent_ref.3) | copy-start | bytes 3076
  7.4 4.1 %copy-start.7 = (f32[256]{0:T(256)S(1)}, f32[256]{0:T(256)}, u32[]{:S(2)}) copy-start(f32[256]{0:T(256)} %param.14) | copy-start | bytes 3076
  13.8 12.2 %copy-start = (bf16[27,256,256]{2,1,0:T(8,128)(2,1)S(1)}, bf16[27,256,256]{2,1,0:T(8,128)(2,1)}, u32[]{:S(2)}) copy-start(bf16[27,256,256]{2,1,0:T(8,128)(2,1)} %weight_ref.3) | copy-start | bytes 10616836
  13.8 12.2 %copy-start.5 = (bf16[1,256,256]{2,1,0:T(8,128)(2,1)S(1)}, bf16[1,256,256]{2,1,0:T(8,128)(2,1)}, u32[]{:S(2)}) copy-start(bf16[1,256,256]{2,1,0:T(8,128)(2,1)} %param.9) | copy-start | bytes 393220
  13.8 12.2 %copy-start.8 = (f32[256]{0:T(256)S(1)}, f32[256]{0:T(256)}, u32[]{:S(2)}) copy-start(f32[256]{0:T(256)} %param.15) | copy-start | bytes 3076
  13.8 8.7 %collective-permute-start.5 = (bf16[272,256]{1,0:T(8,128)(2,1)S(1)}, bf16[272,256]{1,0:T(8,128)(2,1)S(1)}, u32[]{:S(2)}, u32[]{:S(2)}) collective-permute-start(bf16[272,256]{1,0:T(8,128)(2,1)S(1)} %get-tuple-element.15.here), channel_id=1, source_target_pairs={{0,1},{1,0},{2,3},{3,2},{4,5},{5,4},{6,7},{7,6},{8,9},{9,8},{10,11... | collective-permute-start | bytes 417800 | tf_op jit(solution)/shard_map/ppermute | solution.py:33
  20.8 5.2 %collective-permute-start.4 = (bf16[400,256]{1,0:T(8,128)(2,1)S(1)}, bf16[400,256]{1,0:T(8,128)(2,1)S(1)}, u32[]{:S(2)}, u32[]{:S(2)}) collective-permute-start(bf16[400,256]{1,0:T(8,128)(2,1)S(1)} %get-tuple-element.16), channel_id=1, source_target_pairs={{0,63},{1,0},{2,1},{3,2},{4,3},{5,4},{6,5},{7,6},{8,7},{9,8},{10,9... | collective-permute-start | bytes 614408 | tf_op jit(solution)/shard_map/ppermute | solution.py:28
  20.9 3.7 %collective-permute-start.3 = (bf16[272,256]{1,0:T(8,128)(2,1)S(1)}, bf16[272,256]{1,0:T(8,128)(2,1)S(1)}, u32[]{:S(2)}, u32[]{:S(2)}) collective-permute-start(bf16[272,256]{1,0:T(8,128)(2,1)S(1)} %get-tuple-element.15.here), channel_id=1, source_target_pairs={{0,1},{1,2},{2,3},{3,4},{4,5},{5,6},{6,7},{7,8},{8,9},{9,10},{10,1... | collective-permute-start | bytes 417800 | tf_op jit(solution)/shard_map/ppermute | solution.py:28
  26.0 38.1 %copy-start.3 = (bf16[256,512]{1,0:T(8,128)(2,1)S(1)}, bf16[256,512]{1,0:T(8,128)(2,1)}, u32[]{:S(2)}) copy-start(bf16[256,512]{1,0:T(8,128)(2,1)} %down_ref.1) | copy-start | bytes 786436
  29.5 17.8 %all-to-all-start = ((bf16[32,8,512]{2,1,0:T(8,128)(2,1)}), bf16[32,8,512]{2,1,0:T(8,128)(2,1)S(1)}, u32[]{:S(2)}, u32[]{:S(2)}) async-start(bf16[32,8,512]{2,1,0:T(8,128)(2,1)} %bitcast.6), calls=%async_computation | async-start | bytes 524288 | tf_op jit(solution)/shard_map/all_to_all | solution.py:189
  38.0 4.1 %collective-permute-start.6 = (f32[64,256]{1,0:T(8,128)S(1)}, f32[64,256]{1,0:T(8,128)S(1)}, u32[]{:S(2)}, u32[]{:S(2)}) collective-permute-start(f32[64,256]{1,0:T(8,128)S(1)} %get-tuple-element.19), channel_id=1, source_target_pairs={{0,1},{1,2},{2,3},{3,4},{4,5},{5,6},{6,7},{7,8},{8,9},{9,10},{10,1... | collective-permute-start | bytes 196616 | tf_op jit(solution)/shard_map/ppermute | solution.py:28
  59.5 13.5 %all-to-all-start.2 = ((bf16[32,8,512]{2,1,0:T(8,128)(2,1)}), bf16[32,8,512]{2,1,0:T(8,128)(2,1)S(1)}, u32[]{:S(2)}, u32[]{:S(2)}) async-start(bf16[32,8,512]{2,1,0:T(8,128)(2,1)} %broadcast_in_dim.29), calls=%async_computation.2 | async-start | bytes 524288 | tf_op jit(solution)/shard_map/all_to_all | solution.py:189

commit v6 on v5

--- a/solution.py
+++ b/solution.py
@@ -47,7 +47,7 @@
     return jnp.concatenate([local, jnp.full((-taps % 8, rows), -1, jnp.int32)], axis=0).T
 
 
-def pick(local, taps, blocks, select_ref, put):
+def pick(local, taps, blocks, select_ref, put, wait=None):
     rows = local.shape[0]
     places = lax.broadcasted_iota(jnp.int16, (rows, rows), 1)
     one, zero = jnp.ones((), jnp.bfloat16), jnp.zeros((), jnp.bfloat16)
@@ -59,24 +59,26 @@
             select_ref[tap * rows : (tap + 1) * rows, b * rows : (b + 1) * rows] = jnp.where(
                 wanted == places, one, zero
             )
+    if wait is not None:
+        wait()
     for first in range(0, taps, GROUP):
         part = select_ref[first * rows : (first + GROUP) * rows]
         picked = sum(
-            jnp.dot(part[:, b * rows : (b + 1) * rows], block, preferred_element_type=jnp.float32)
+            jnp.dot(part[:, b * rows : (b + 1) * rows], block[...], preferred_element_type=jnp.float32)
             for b, (block, _) in enumerate(blocks)
         ).astype(jnp.bfloat16)
         for j in range(GROUP):
             put(first + j, picked[j * rows : (j + 1) * rows])
 
 
-def pick_near(local, here, partner, select_ref, near_ref):
+def pick_near(local, here, partner, select_ref, near_ref, wait=None):
     rows, chans = here.shape
     blocks = ((here, rows), (partner, 2 * rows * (1 - lax.axis_index("core"))))
 
     def put(tap, picked):
         near_ref[:, tap * chans : (tap + 1) * chans] = picked
 
-    pick(local, near_ref.shape[1] // chans, blocks, select_ref, put)
+    pick(local, near_ref.shape[1] // chans, blocks, select_ref, put, wait)
 
 
 def convolved(local, before, after, near_ref, weight_ref, select_ref, picked_ref):
@@ -96,14 +98,21 @@
     )
 
 
-def first_near_kernel(taps_ref, here, partner, near_ref, local_ref, select_ref):
+def first_near_kernel(
+    partner, taps_hbm, here_hbm, near_ref, local_ref, select_ref, taps_ref, here, taps_sem, here_sem
+):
+    taps_copy = pltpu.make_async_copy(taps_hbm, taps_ref, taps_sem)
+    here_copy = pltpu.make_async_copy(here_hbm, here, here_sem)
+    taps_copy.start()
+    here_copy.start()
+    taps_copy.wait()
     local = local_table(taps_ref)
     local_ref[...] = local
-    pick_near(local, here[...], partner[...], select_ref, near_ref)
+    pick_near(local, here, partner, select_ref, near_ref, here_copy.wait)
 
 
 def first_far_kernel(
-    local_ref, before, after, near_ref, weight_ref, gain_ref, parent_ref, cotangent_ref,
+    local_ref, after, before, near_ref, weight_ref, gain_ref, parent_ref, cotangent_ref,
     middle_ref, wide_ref, select_ref, picked_ref,
 ):
     total = convolved(local_ref[...], before[...], after[...], near_ref, weight_ref, select_ref, picked_ref)
@@ -130,7 +139,7 @@
 
 
 def second_far_kernel(
-    local_ref, before, after, near_ref, weight_ref, gain_ref, feature_ref, parent_ref,
+    local_ref, after, before, near_ref, weight_ref, gain_ref, feature_ref, parent_ref,
     cotangent_ref,
     fine_ref, own_ref, sent_ref, grad_ref, select_ref, picked_ref,
 ):
@@ -148,7 +157,7 @@
         return jnp.sum(membership(ids, 2 * half), axis=1, keepdims=True)
 
     tally_own = jnp.sum(member, axis=1, keepdims=True)
-    tally_before = tally(before[rows:].astype(jnp.float32)[:1].astype(jnp.int32))[half:]
+    tally_before = tally(before[last:].astype(jnp.float32)[:1].astype(jnp.int32))[half:]
     tally_after = tally(after[last:].astype(jnp.float32)[:1].astype(jnp.int32))[:half]
     count_own = jnp.maximum(tally_own[:half] + tally_before, 1.0)
     count_after = jnp.maximum(tally_own[half:] + tally_after, 1.0)
@@ -171,18 +180,18 @@
     coarse_ref[...] = jnp.dot(pooled, down_ref[...], preferred_element_type=jnp.float32).astype(coarse_ref.dtype)
 
 
-def in_vmem(kernel, outs, inputs, name, scratch=(), flops=0):
+def in_vmem(kernel, outs, inputs, name, scratch=(), flops=0, from_hbm=()):
     vmem = pl.BlockSpec(memory_space=pltpu.VMEM)
     return pl.pallas_call(
         kernel,
         out_shape=outs,
-        in_specs=[vmem] * len(inputs),
+        in_specs=[vmem] * len(inputs) + [pl.BlockSpec(memory_space=pltpu.HBM)] * len(from_hbm),
         out_specs=jax.tree.map(lambda _: vmem, outs),
         scratch_shapes=scratch,
         compiler_params=pltpu.CompilerParams(vmem_limit_bytes=VMEM_BYTES),
         cost_estimate=pl.CostEstimate(flops=flops, bytes_accessed=COST_BYTES, transcendentals=0),
         name=name,
-    )(*inputs)
+    )(*inputs, *[pltpu.with_memory_space_constraint(array, pltpu.HBM) for array in from_hbm])
 
 
 def exchanged(pieces, axes):
@@ -195,13 +204,14 @@
     return exchanged(local_grad.reshape(plane, rows // plane, cols), PLANE)
 
 
-def finished(parts, scale):
+def finished(parts, sent, scale):
     plane, _, cols = parts.shape
     part = jnp.sum(parts.astype(jnp.float32), axis=0)
     copies = jnp.broadcast_to(part[None], (lax.axis_size("z"),) + part.shape)
-    part = jnp.sum(exchanged(copies, "z"), axis=0) * scale
+    moved, copies = lax.optimization_barrier((shifted(sent, 1), exchanged(copies, "z")))
+    part = jnp.sum(copies, axis=0) * scale
     copies = jnp.broadcast_to(part.astype(jnp.bfloat16)[None], (plane,) + part.shape)
-    return exchanged(copies, PLANE).astype(jnp.float32).reshape(-1, cols)
+    return exchanged(copies, PLANE).astype(jnp.float32).reshape(-1, cols), moved
 
 
 def body(
@@ -228,20 +238,29 @@
         pltpu.VMEM((taps * rows, rows), jnp.bfloat16),
         pltpu.VMEM((rows, taps * chans), jnp.bfloat16),
     ]
-    before, after = shifted(field, 1), shifted(field, -1)
+    after, before = shifted(field, -1), shifted(field, 1)
     near, local = in_vmem(
         first_near_kernel,
         (near_shape, jax.ShapeDtypeStruct((rows, taps + -taps % 8), jnp.int32)),
-        (jnp.moveaxis(neighbours, 1, 0), field, from_partner(field)),
-        "first_near", select, 2 * product,
+        (from_partner(field),),
+        "first_near",
+        select
+        + [
+            pltpu.VMEM((taps, 1, rows), jnp.int32),
+            pltpu.VMEM((rows, chans), jnp.bfloat16),
+            pltpu.SemaphoreType.DMA,
+            pltpu.SemaphoreType.DMA,
+        ],
+        2 * product,
+        (jnp.moveaxis(neighbours, 1, 0), field),
     )
     middle, wide = in_vmem(
         first_far_kernel,
         (bf16((rows + 16, chans)), bf16((rows + par_rows * (out_chans // chans) + 16, chans))),
-        (local, before, after, near, conv_first, gain_first[None], parents, grad_in),
+        (local, after, before, near, conv_first, gain_first[None], parents, grad_in),
         "first_far", select_and_picked, 2 * product,
     )
-    before, after = shifted(middle, 1), shifted(wide, -1)
+    after, before = shifted(wide, -1), shifted(wide, 1)
     partner = from_partner(middle)
     near = in_vmem(
         second_near_kernel, near_shape, (local, middle, partner), "second_near", select, 2 * product
@@ -255,17 +274,16 @@
             bf16((chans, out_chans)),
         ),
         (
-            local, before, after, near, conv_second, gain_second[None], field, parents,
+            local, after, before, near, conv_second, gain_second[None], field, parents,
             grad_in,
         ),
         "second_far", select_and_picked, 2 * product,
     )
     parts = plane_summed(local_grad)
-    moved, parts = lax.optimization_barrier((shifted(sent, 1), parts))
-    coarse = in_vmem(coarse_kernel, bf16((par_rows, out_chans)), (own, moved, down_weight), "coarse")
     worlds_all = lax.axis_size(DP)
     parents_all = par_rows * lax.axis_size(SPACE)
-    down_grad = finished(parts, 1.0 / math.sqrt(worlds_all * parents_all))
+    down_grad, moved = finished(parts, sent, 1.0 / math.sqrt(worlds_all * parents_all))
+    coarse = in_vmem(coarse_kernel, bf16((par_rows, out_chans)), (own, moved, down_weight), "coarse")
     return (fine[None], coarse[None], down_grad)
 
 

time: 74.3 us -> 74.7 us (level)
  blocking collectives: 11.4 us -> 16.7 us
  starting transfers between devices: 28.5 us -> 23.5 us
  Pallas kernels: 11 us -> 12.1 us
  local copies, waits for them, and re-layouts: 2.45 us -> 1.43 us
    all_to_all x1, blocking collectives: 11.4 us -> 16.7 us  [exchanged(): return lax.all_to_all(pieces, axes, 0, 0, tiled=True)]
    ppermute x5, starting transfers between devices: 5.2 us -> 1.72 us  [shifted(): lax.ppermute(array, SPACE, [(i, (i + by) % length) for i in range(length)])]
    ppermute x5, waiting for transfers between devices: 5.49 us -> 3.45 us  [shifted(): lax.ppermute(array, SPACE, [(i, (i + by) % length) for i in range(length)])]
    unnamed x20 -> x16, local copies, waits for them, and re-layouts: 1.72 us -> 0.04 us
    ppermute x2, starting transfers between devices: 10.3 us -> 8.66 us  [from_partner(): return lax.ppermute(array, SPACE, [(i, i ^ 1) for i in range(length)])]
    ppermute x2, waiting for transfers between devices: 0.01 us -> 1.17 us  [from_partner(): return lax.ppermute(array, SPACE, [(i, i ^ 1) for i in range(length)])]
    pallas_call x5, Pallas kernels: 11 us -> 12.1 us  [in_vmem(): pl.pallas_call(kernel, out_shape=outs, in_specs=[vmem] * len(inputs) + [p...]
    all_to_all x2, waiting for transfers between devices: 13.3 us -> 14.2 us  [exchanged(): return lax.all_to_all(pieces, axes, 0, 0, tiled=True)]
  transfers between devices with their start and end apart: 9 -> 9, of which waited for: 5 -> 6; matrix products, arithmetic and copies ran while one was open for 0% -> 0% of each run, Pallas kernels for 7% -> 9%
where the time goes in v6:
time: 74.7 us; the launch traced here: 74.4 us
  starting transfers between devices  23.5 us (31%)
  waiting for transfers between devices  18.8 us (25%)
  blocking collectives  16.7 us (22%)
  Pallas kernels  12.1 us (16%)
  local copies, waits for them, and re-layouts  1.43 us (2%)
  other arithmetic  0.92 us (1%)
  between operations  0.81 us (1%)
    all_to_all x1, blocking collectives, exchanged(): return lax.all_to_all(pieces, axes, 0, 0, tiled=True)  16.7 us
    all_to_all x2, waiting for transfers between devices, exchanged(): return lax.all_to_all(pieces, axes, 0, 0, tiled=True)  14.2 us
    all_to_all x2, starting transfers between devices, exchanged(): return lax.all_to_all(pieces, axes, 0, 0, tiled=True)  13.2 us
    pallas_call x5, Pallas kernels, in_vmem(): pl.pallas_call(kernel, out_shape=outs, in_specs=[vmem] * len(inputs) + [p...  12.1 us
    ppermute x2, starting transfers between devices, from_partner(): return lax.ppermute(array, SPACE, [(i, i ^ 1) for i in range(length)])  8.66 us
    ppermute x5, waiting for transfers between devices, shifted(): lax.ppermute(array, SPACE, [(i, (i + by) % length) for i in range(length)])  3.45 us
    ppermute x5, starting transfers between devices, shifted(): lax.ppermute(array, SPACE, [(i, (i + by) % length) for i in range(length)])  1.72 us
  transfers between devices with their start and end apart: 9, of which 6 were waited for; matrix products, arithmetic and copies ran while one was open for 0% of the time, Pallas kernels for 9%

profile of v6, /device:TPU:1, one launch (start us, length us, event | category | flops | bytes accessed | tf_op | source)
XLA Modules:
  0.0 74.4 jit_solution(7126167720816630952)
XLA Ops:
  0.7 3.3 %collective-permute-start = (bf16[256,256]{1,0:T(8,128)(2,1)}, bf16[256,256]{1,0:T(8,128)(2,1)S(1)}, u32[]{:S(2)}, u32[]{:S(2)}) collective-permute-start(bf16[256,256]{1,0:T(8,128)(2,1)} %bitcast.14), channel_id=1, source_target_pairs={{0,1},{1,0},{2,3},{3,2},{4,5},{5,4},{6,7},{7,6},{8,9},{9,8},{10,11... | collective-permute-start | bytes 393224 | tf_op jit(solution)/shard_map/ppermute | solution.py:33
  4.0 0.5 collective-permute-start.1
  4.5 0.7 collective-permute-done.partner
  5.2 3.9 %first_near.1 = (bf16[256,6912]{1,0:T(8,128)(2,1)S(1)}, s32[256,32]{1,0:T(8,128)S(1)}) custom-call(bf16[256,256]{1,0:T(8,128)(2,1)S(1)} %collective-permute-done.partner, s32[27,1,256]{2,1,0:T(1,128)} %bitcast.23, bf16[256,256]{1,0:T(8,128)(2,1)} %bitcast.17), custom_call_target="tpu_custom_call" | custom-call | flops 1811939328 | bytes 1048576 | tf_op jit(solution)/shard_map/first_near/pallas_call | solution.py:185
  9.1 2.3 %first_far.1 = (bf16[272,256]{1,0:T(8,128)(2,1)S(1)}, bf16[400,256]{1,0:T(8,128)(2,1)S(1)}) custom-call(s32[256,32]{1,0:T(8,128)S(1)} %get-tuple-element.13.local_ref, bf16[256,256]{1,0:T(8,128)(2,1)S(1)} %collective-permute-done.1.after, bf16[256,256]{1,0:T(8,128)(2,1)S(1)} %collective-permute-done.2.before, ...), custom_call_target="tpu_custom_call" | custom-call | flops 1811939328 | bytes 1048576 | tf_op jit(solution)/shard_map/first_far/pallas_call | solution.py:185
  11.5 0.0 copy-start.4
  11.5 0.0 copy-start.7
  11.5 5.3 %collective-permute-start.5 = (bf16[272,256]{1,0:T(8,128)(2,1)S(1)}, bf16[272,256]{1,0:T(8,128)(2,1)S(1)}, u32[]{:S(2)}, u32[]{:S(2)}) collective-permute-start(bf16[272,256]{1,0:T(8,128)(2,1)S(1)} %get-tuple-element.16.here), channel_id=1, source_target_pairs={{0,1},{1,0},{2,3},{3,2},{4,5},{5,4},{6,7},{7,6},{8,9},{9,8},{10,11... | collective-permute-start | bytes 417800 | tf_op jit(solution)/shard_map/ppermute | solution.py:33
  16.8 0.5 collective-permute-start.3
  17.3 0.5 collective-permute-done.5.partner
  17.8 2.1 %second_near.1.near_ref = bf16[256,6912]{1,0:T(8,128)(2,1)S(1)} custom-call(s32[256,32]{1,0:T(8,128)S(1)} %get-tuple-element.13.local_ref, bf16[272,256]{1,0:T(8,128)(2,1)S(1)} %get-tuple-element.16.here, bf16[272,256]{1,0:T(8,128)(2,1)S(1)} %collective-permute-done.5.partner), custom_call_target="tpu_custom_call" | custom-call | flops 1811939328 | bytes 1048576 | tf_op jit(solution)/shard_map/second_near/pallas_call | solution.py:185
  19.9 2.1 %collective-permute-done.3.after = bf16[400,256]{1,0:T(8,128)(2,1)S(1)} collective-permute-done((bf16[400,256]{1,0:T(8,128)(2,1)S(1)}, bf16[400,256]{1,0:T(8,128)(2,1)S(1)}, u32[]{:S(2)}, u32[]{:S(2)}) %collective-permute-start.3) | collective-permute-done | bytes 204832 | tf_op jit(solution)/shard_map/ppermute | solution.py:28
  22.0 3.0 %second_far.1 = (bf16[256,256]{1,0:T(8,128)(2,1)}, f32[64,384]{1,0:T(8,128)S(1)}, f32[64,256]{1,0:T(8,128)S(1)}, bf16[256,512]{1,0:T(8,128)(2,1)S(1)}) custom-call(s32[256,32]{1,0:T(8,128)S(1)} %get-tuple-element.13.local_ref, bf16[400,256]{1,0:T(8,128)(2,1)S(1)} %collective-permute-done.3.after, bf16[400,256]{1,0:T(8,128)(2,1)S(1)} %collective-permute-done.4.before, ...), custom_call_target="tpu_custom_call" | custom-call | flops 1811939328 | bytes 1048576 | tf_op jit(solution)/shard_map/second_far/pallas_call | solution.py:185
  25.1 16.7 %all_to_all.15 = bf16[32,8,512]{2,1,0:T(8,128)(2,1)S(1)} all-to-all(bf16[32,8,512]{2,1,0:T(8,128)(2,1)S(1)} %bitcast.13), channel_id=1, replica_groups=mesh['y'=4,'z'=8,'x'=4,'core'=2] {'y','x','core'}, dimensions={0} | all-to-all | bytes 524288 | tf_op jit(solution)/shard_map/all_to_all | solution.py:198
  41.8 0.7 broadcast_in_dim.27
  42.5 7.6 %all-to-all-start.1 = ((f32[8,8,512]{2,1,0:T(8,128)}), f32[8,8,512]{2,1,0:T(8,128)S(1)}, u32[]{:S(2)}, u32[]{:S(2)}) async-start(f32[8,8,512]{2,1,0:T(8,128)} %broadcast_in_dim.27), calls=%async_computation.1 | async-start | bytes 262144 | tf_op jit(solution)/shard_map/all_to_all | solution.py:198
  50.1 0.7 collective-permute-start.6
  50.8 1.3 %collective-permute-done.6.moved_ref = f32[64,256]{1,0:T(8,128)S(1)} collective-permute-done((f32[64,256]{1,0:T(8,128)S(1)}, f32[64,256]{1,0:T(8,128)S(1)}, u32[]{:S(2)}, u32[]{:S(2)}) %collective-permute-start.6) | collective-permute-done | bytes 65568 | tf_op jit(solution)/shard_map/ppermute | solution.py:28
  52.1 6.2 %all-to-all-done.1 = f32[8,8,512]{2,1,0:T(8,128)S(1)} async-done(((f32[8,8,512]{2,1,0:T(8,128)}), f32[8,8,512]{2,1,0:T(8,128)S(1)}, u32[]{:S(2)}, u32[]{:S(2)}) %all-to-all-start.1) | async-done | bytes 131104 | tf_op jit(solution)/shard_map/all_to_all | solution.py:198
  58.3 0.7 broadcast_in_dim.29
  59.0 5.6 %all-to-all-start.2 = ((bf16[32,8,512]{2,1,0:T(8,128)(2,1)}), bf16[32,8,512]{2,1,0:T(8,128)(2,1)S(1)}, u32[]{:S(2)}, u32[]{:S(2)}) async-start(bf16[32,8,512]{2,1,0:T(8,128)(2,1)} %broadcast_in_dim.29), calls=%async_computation.2 | async-start | bytes 524288 | tf_op jit(solution)/shard_map/all_to_all | solution.py:198
  64.6 0.8 %coarse.1 = bf16[64,512]{1,0:T(8,128)(2,1)} custom-call(f32[64,384]{1,0:T(8,128)S(1)} %get-tuple-element.18.own_ref, f32[64,256]{1,0:T(8,128)S(1)} %collective-permute-done.6.moved_ref, bf16[256,512]{1,0:T(8,128)(2,1)S(1)} %copy-done.3), custom_call_target="tpu_custom_call" | custom-call | bytes 1048576 | tf_op jit(solution)/shard_map/coarse/pallas_call | solution.py:185
  65.4 8.0 %all-to-all-done.2 = bf16[32,8,512]{2,1,0:T(8,128)(2,1)S(1)} async-done(((bf16[32,8,512]{2,1,0:T(8,128)(2,1)}), bf16[32,8,512]{2,1,0:T(8,128)(2,1)S(1)}, u32[]{:S(2)}, u32[]{:S(2)}) %all-to-all-start.2) | async-done | bytes 262176 | tf_op jit(solution)/shard_map/all_to_all | solution.py:198
  73.5 0.9 %bitcast_convert_fusion = f32[256,512]{1,0:T(8,128)} fusion(bf16[32,8,512]{2,1,0:T(8,128)(2,1)S(1)} %all-to-all-done.2), kind=kLoop, calls=%fused_computation.1 | loop fusion | flops 131072 | bytes 786432 | tf_op jit(solution)/shard_map/reshape | solution.py:214
  (22 shorter events, 0.1 us)
Async XLA Ops:
  0.6 8.5 %copy-start.5 = (s32[1,256]{1,0:T(1,128)S(1)}, s32[1,256]{1,0:T(1,128)}, u32[]{:S(2)}) copy-start(s32[1,256]{1,0:T(1,128)} %parent_ref.3) | copy-start | bytes 3076
  0.6 8.5 %copy-start.2 = (bf16[1,64,512]{2,1,0:T(8,128)(2,1)S(1)}, bf16[1,64,512]{2,1,0:T(8,128)(2,1)}, u32[]{:S(2)}) copy-start(bf16[1,64,512]{2,1,0:T(8,128)(2,1)} %param.17) | copy-start | bytes 196612
  0.7 8.5 %copy-start.6 = (f32[256]{0:T(256)S(1)}, f32[256]{0:T(256)}, u32[]{:S(2)}) copy-start(f32[256]{0:T(256)} %param.14) | copy-start | bytes 3076
  0.7 8.5 %copy-start.1 = (bf16[27,256,256]{2,1,0:T(8,128)(2,1)S(1)}, bf16[27,256,256]{2,1,0:T(8,128)(2,1)}, u32[]{:S(2)}) copy-start(bf16[27,256,256]{2,1,0:T(8,128)(2,1)} %weight_ref.2) | copy-start | bytes 10616836
  0.7 4.5 %collective-permute-start = (bf16[256,256]{1,0:T(8,128)(2,1)}, bf16[256,256]{1,0:T(8,128)(2,1)S(1)}, u32[]{:S(2)}, u32[]{:S(2)}) collective-permute-start(bf16[256,256]{1,0:T(8,128)(2,1)} %bitcast.14), channel_id=1, source_target_pairs={{0,1},{1,0},{2,3},{3,2},{4,5},{5,4},{6,7},{7,6},{8,9},{9,8},{10,11... | collective-permute-start | bytes 393224 | tf_op jit(solution)/shard_map/ppermute | solution.py:33
  4.0 5.1 %collective-permute-start.2 = (bf16[256,256]{1,0:T(8,128)(2,1)}, bf16[256,256]{1,0:T(8,128)(2,1)S(1)}, u32[]{:S(2)}, u32[]{:S(2)}) collective-permute-start(bf16[256,256]{1,0:T(8,128)(2,1)} %bitcast.15), channel_id=1, source_target_pairs={{0,1},{1,2},{2,3},{3,4},{4,5},{5,6},{6,7},{7,8},{8,9},{9,10},{10,1... | collective-permute-start | bytes 393224 | tf_op jit(solution)/shard_map/ppermute | solution.py:28
  4.0 5.1 %collective-permute-start.1 = (bf16[256,256]{1,0:T(8,128)(2,1)}, bf16[256,256]{1,0:T(8,128)(2,1)S(1)}, u32[]{:S(2)}, u32[]{:S(2)}) collective-permute-start(bf16[256,256]{1,0:T(8,128)(2,1)} %bitcast.16), channel_id=1, source_target_pairs={{0,63},{1,0},{2,1},{3,2},{4,3},{5,4},{6,5},{7,6},{8,7},{9,8},{10,9... | collective-permute-start | bytes 393224 | tf_op jit(solution)/shard_map/ppermute | solution.py:28
  11.5 10.6 %copy-start = (bf16[27,256,256]{2,1,0:T(8,128)(2,1)S(1)}, bf16[27,256,256]{2,1,0:T(8,128)(2,1)}, u32[]{:S(2)}) copy-start(bf16[27,256,256]{2,1,0:T(8,128)(2,1)} %weight_ref.3) | copy-start | bytes 10616836
  11.5 10.5 %copy-start.4 = (bf16[1,256,256]{2,1,0:T(8,128)(2,1)S(1)}, bf16[1,256,256]{2,1,0:T(8,128)(2,1)}, u32[]{:S(2)}) copy-start(bf16[1,256,256]{2,1,0:T(8,128)(2,1)} %param.9) | copy-start | bytes 393220
  11.5 10.5 %copy-start.7 = (f32[256]{0:T(256)S(1)}, f32[256]{0:T(256)}, u32[]{:S(2)}) copy-start(f32[256]{0:T(256)} %param.15) | copy-start | bytes 3076
  11.5 6.3 %collective-permute-start.5 = (bf16[272,256]{1,0:T(8,128)(2,1)S(1)}, bf16[272,256]{1,0:T(8,128)(2,1)S(1)}, u32[]{:S(2)}, u32[]{:S(2)}) collective-permute-start(bf16[272,256]{1,0:T(8,128)(2,1)S(1)} %get-tuple-element.16.here), channel_id=1, source_target_pairs={{0,1},{1,0},{2,3},{3,2},{4,5},{5,4},{6,7},{7,6},{8,9},{9,8},{10,11... | collective-permute-start | bytes 417800 | tf_op jit(solution)/shard_map/ppermute | solution.py:33
  16.8 3.1 %collective-permute-start.4 = (bf16[400,256]{1,0:T(8,128)(2,1)S(1)}, bf16[400,256]{1,0:T(8,128)(2,1)S(1)}, u32[]{:S(2)}, u32[]{:S(2)}) collective-permute-start(bf16[400,256]{1,0:T(8,128)(2,1)S(1)} %get-tuple-element.15), channel_id=1, source_target_pairs={{0,1},{1,2},{2,3},{3,4},{4,5},{5,6},{6,7},{7,8},{8,9},{9,10},{10,1... | collective-permute-start | bytes 614408 | tf_op jit(solution)/shard_map/ppermute | solution.py:28
  16.8 5.2 %collective-permute-start.3 = (bf16[400,256]{1,0:T(8,128)(2,1)S(1)}, bf16[400,256]{1,0:T(8,128)(2,1)S(1)}, u32[]{:S(2)}, u32[]{:S(2)}) collective-permute-start(bf16[400,256]{1,0:T(8,128)(2,1)S(1)} %get-tuple-element.15), channel_id=1, source_target_pairs={{0,63},{1,0},{2,1},{3,2},{4,3},{5,4},{6,5},{7,6},{8,7},{9,8},{10,9... | collective-permute-start | bytes 614408 | tf_op jit(solution)/shard_map/ppermute | solution.py:28
  22.0 42.6 %copy-start.3 = (bf16[256,512]{1,0:T(8,128)(2,1)S(1)}, bf16[256,512]{1,0:T(8,128)(2,1)}, u32[]{:S(2)}) copy-start(bf16[256,512]{1,0:T(8,128)(2,1)} %down_ref.1) | copy-start | bytes 786436
  42.5 15.8 %all-to-all-start.1 = ((f32[8,8,512]{2,1,0:T(8,128)}), f32[8,8,512]{2,1,0:T(8,128)S(1)}, u32[]{:S(2)}, u32[]{:S(2)}) async-start(f32[8,8,512]{2,1,0:T(8,128)} %broadcast_in_dim.27), calls=%async_computation.1 | async-start | bytes 262144 | tf_op jit(solution)/shard_map/all_to_all | solution.py:198
  50.1 2.0 %collective-permute-start.6 = (f32[64,256]{1,0:T(8,128)S(1)}, f32[64,256]{1,0:T(8,128)S(1)}, u32[]{:S(2)}, u32[]{:S(2)}) collective-permute-start(f32[64,256]{1,0:T(8,128)S(1)} %get-tuple-element.19), channel_id=1, source_target_pairs={{0,1},{1,2},{2,3},{3,4},{4,5},{5,6},{6,7},{7,8},{8,9},{9,10},{10,1... | collective-permute-start | bytes 196616 | tf_op jit(solution)/shard_map/ppermute | solution.py:28
  59.0 14.5 %all-to-all-start.2 = ((bf16[32,8,512]{2,1,0:T(8,128)(2,1)}), bf16[32,8,512]{2,1,0:T(8,128)(2,1)S(1)}, u32[]{:S(2)}, u32[]{:S(2)}) async-start(bf16[32,8,512]{2,1,0:T(8,128)(2,1)} %broadcast_in_dim.29), calls=%async_computation.2 | async-start | bytes 524288 | tf_op jit(solution)/shard_map/all_to_all | solution.py:198

commit v7 on v6

--- a/solution.py
+++ b/solution.py
@@ -15,6 +15,7 @@
 PLANE = ("y", "x", "core")
 GROUP = 3
 VMEM_BYTES = 32 << 20
+PAR_ROWS = 64
 COST_BYTES = 1 << 20
 
 
@@ -112,21 +113,15 @@
 
 
 def first_far_kernel(
-    local_ref, after, before, near_ref, weight_ref, gain_ref, parent_ref, cotangent_ref,
-    middle_ref, wide_ref, select_ref, picked_ref,
+    local_ref, after, before, near_ref, weight_ref, gain_ref, parent_ref,
+    middle_ref, select_ref, picked_ref,
 ):
     total = convolved(local_ref[...], before[...], after[...], near_ref, weight_ref, select_ref, picked_ref)
     rows = total.shape[0]
-    middle = settled(total, gain_ref[...]).astype(middle_ref.dtype)
-    middle_ref[:rows] = middle
-    wide_ref[:rows] = middle
-    half, wide = cotangent_ref.shape
-    for j in range(wide // rows):
-        wide_ref[rows + j * half : rows + (j + 1) * half] = cotangent_ref[:, j * rows : (j + 1) * rows]
-    ids = parent_ref[...] - lax.axis_index(SPACE) * half
+    middle_ref[:rows] = settled(total, gain_ref[...]).astype(middle_ref.dtype)
+    ids = parent_ref[...] - lax.axis_index(SPACE) * PAR_ROWS
     ids = jnp.broadcast_to(ids.astype(jnp.float32), (middle_ref.shape[0] - rows, ids.shape[1]))
     middle_ref[rows:] = ids.astype(middle_ref.dtype)
-    wide_ref[rows + half * (wide // rows) :] = ids.astype(wide_ref.dtype)
 
 
 def second_near_kernel(local_ref, here, partner, near_ref, select_ref):
@@ -140,7 +135,7 @@
 
 def second_far_kernel(
     local_ref, after, before, near_ref, weight_ref, gain_ref, feature_ref, parent_ref,
-    cotangent_ref,
+    cotangent_ref, next_ref,
     fine_ref, own_ref, sent_ref, grad_ref, select_ref, picked_ref,
 ):
     rows, chans = feature_ref.shape
@@ -148,8 +143,7 @@
     fine = feature_ref[...].astype(jnp.float32) + settled(total, gain_ref[...])
     fine = fine.astype(fine_ref.dtype)
     fine_ref[...] = fine
-    half, wide = cotangent_ref.shape
-    last = rows + half * (wide // rows)
+    half = cotangent_ref.shape[0]
     member = membership(parent_ref[...] - lax.axis_index(SPACE) * half, 2 * half)
     sums = jnp.dot(member.astype(jnp.bfloat16), fine, preferred_element_type=jnp.float32)
 
@@ -157,17 +151,15 @@
         return jnp.sum(membership(ids, 2 * half), axis=1, keepdims=True)
 
     tally_own = jnp.sum(member, axis=1, keepdims=True)
-    tally_before = tally(before[last:].astype(jnp.float32)[:1].astype(jnp.int32))[half:]
-    tally_after = tally(after[last:].astype(jnp.float32)[:1].astype(jnp.int32))[:half]
+    tally_before = tally(before[rows:].astype(jnp.float32)[:1].astype(jnp.int32))[half:]
+    tally_after = tally(after[rows:].astype(jnp.float32)[:1].astype(jnp.int32))[:half]
     count_own = jnp.maximum(tally_own[:half] + tally_before, 1.0)
     count_after = jnp.maximum(tally_own[half:] + tally_after, 1.0)
     own_ref[:, :chans] = sums[:half]
     own_ref[:, chans:] = jnp.broadcast_to(count_own, (half, own_ref.shape[1] - chans))
     sent_ref[...] = sums[half:]
     shares = sums / jnp.concatenate([count_own, count_after], axis=0)
-    next_grads = after[rows:last]
-    next_grads = jnp.concatenate([next_grads[j * half : (j + 1) * half] for j in range(wide // rows)], axis=1)
-    grads_in = jnp.concatenate([cotangent_ref[...], next_grads], axis=0)
+    grads_in = jnp.concatenate([cotangent_ref[...], next_ref[...]], axis=0)
     grad_ref[...] = lax.dot_general(
         shares.astype(jnp.bfloat16), grads_in, (((0,), (0,)), ((), ())), preferred_element_type=jnp.float32
     ).astype(grad_ref.dtype)
@@ -204,14 +196,13 @@
     return exchanged(local_grad.reshape(plane, rows // plane, cols), PLANE)
 
 
-def finished(parts, sent, scale):
+def finished(parts, scale):
     plane, _, cols = parts.shape
     part = jnp.sum(parts.astype(jnp.float32), axis=0)
     copies = jnp.broadcast_to(part[None], (lax.axis_size("z"),) + part.shape)
-    moved, copies = lax.optimization_barrier((shifted(sent, 1), exchanged(copies, "z")))
-    part = jnp.sum(copies, axis=0) * scale
+    part = jnp.sum(exchanged(copies, "z"), axis=0) * scale
     copies = jnp.broadcast_to(part.astype(jnp.bfloat16)[None], (plane,) + part.shape)
-    return exchanged(copies, PLANE).astype(jnp.float32).reshape(-1, cols), moved
+    return exchanged(copies, PLANE).astype(jnp.float32).reshape(-1, cols)
 
 
 def body(
@@ -254,13 +245,16 @@
         2 * product,
         (jnp.moveaxis(neighbours, 1, 0), field),
     )
-    middle, wide = in_vmem(
+    ready, near = lax.optimization_barrier((grad_in, near))
+    next_grad = shifted(ready, -1)
+    middle = in_vmem(
         first_far_kernel,
-        (bf16((rows + 16, chans)), bf16((rows + par_rows * (out_chans // chans) + 16, chans))),
-        (local, after, before, near, conv_first, gain_first[None], parents, grad_in),
+        bf16((rows + 16, chans)),
+        (local, after, before, near, conv_first, gain_first[None], parents),
         "first_far", select_and_picked, 2 * product,
     )
-    after, before = shifted(wide, -1), shifted(wide, 1)
+    middle, next_grad = lax.optimization_barrier((middle, next_grad))
+    after, before = shifted(middle, -1), shifted(middle, 1)
     partner = from_partner(middle)
     near = in_vmem(
         second_near_kernel, near_shape, (local, middle, partner), "second_near", select, 2 * product
@@ -275,15 +269,16 @@
         ),
         (
             local, after, before, near, conv_second, gain_second[None], field, parents,
-            grad_in,
+            grad_in, next_grad,
         ),
         "second_far", select_and_picked, 2 * product,
     )
     parts = plane_summed(local_grad)
     worlds_all = lax.axis_size(DP)
     parents_all = par_rows * lax.axis_size(SPACE)
-    down_grad, moved = finished(parts, sent, 1.0 / math.sqrt(worlds_all * parents_all))
+    moved, parts = lax.optimization_barrier((shifted(sent, 1), parts))
     coarse = in_vmem(coarse_kernel, bf16((par_rows, out_chans)), (own, moved, down_weight), "coarse")
+    down_grad = finished(parts, 1.0 / math.sqrt(worlds_all * parents_all))
     return (fine[None], coarse[None], down_grad)
 
 

time: 74.7 us -> 74.8 us (level)
  starting transfers between devices: 23.5 us -> 26.4 us
  blocking collectives: 16.7 us -> 14.9 us
    ppermute x5 -> x6, starting transfers between devices: 1.72 us -> 8.05 us  [shifted(): lax.ppermute(array, SPACE, [(i, (i + by) % length) for i in range(length)])]
    ppermute x2, starting transfers between devices: 8.66 us -> 4.6 us  [from_partner(): return lax.ppermute(array, SPACE, [(i, i ^ 1) for i in range(length)])]
    all_to_all x1, blocking collectives: 16.7 us -> 14.9 us  [exchanged(): return lax.all_to_all(pieces, axes, 0, 0, tiled=True)]
    all_to_all x2, waiting for transfers between devices: 14.2 us -> 13.2 us  [exchanged(): return lax.all_to_all(pieces, axes, 0, 0, tiled=True)]
    ppermute x5 -> x6, waiting for transfers between devices: 3.45 us -> 3.83 us  [shifted(): lax.ppermute(array, SPACE, [(i, (i + by) % length) for i in range(length)])]
  transfers between devices with their start and end apart: 9 -> 10, of which waited for: 6 -> 6; matrix products, arithmetic and copies ran while one was open for 0% -> 0% of each run, Pallas kernels for 9% -> 12%
where the time goes in v7:
time: 74.8 us; the launch traced here: 74.5 us
  starting transfers between devices  26.4 us (35%)
  waiting for transfers between devices  18.2 us (24%)
  blocking collectives  14.9 us (20%)
  Pallas kernels  12.6 us (17%)
  other arithmetic  0.92 us (1%)
  between operations  0.81 us (1%)
  local copies, waits for them, and re-layouts  0.78 us (1%)
    all_to_all x1, blocking collectives, exchanged(): return lax.all_to_all(pieces, axes, 0, 0, tiled=True)  14.9 us
    all_to_all x2, starting transfers between devices, exchanged(): return lax.all_to_all(pieces, axes, 0, 0, tiled=True)  13.7 us
    all_to_all x2, waiting for transfers between devices, exchanged(): return lax.all_to_all(pieces, axes, 0, 0, tiled=True)  13.2 us
    pallas_call x5, Pallas kernels, in_vmem(): pl.pallas_call(kernel, out_shape=outs, in_specs=[vmem] * len(inputs) + [p...  12.6 us
    ppermute x6, starting transfers between devices, shifted(): lax.ppermute(array, SPACE, [(i, (i + by) % length) for i in range(length)])  8.05 us
    ppermute x2, starting transfers between devices, from_partner(): return lax.ppermute(array, SPACE, [(i, i ^ 1) for i in range(length)])  4.6 us
    ppermute x6, waiting for transfers between devices, shifted(): lax.ppermute(array, SPACE, [(i, (i + by) % length) for i in range(length)])  3.83 us
  transfers between devices with their start and end apart: 10, of which 6 were waited for; matrix products, arithmetic and copies ran while one was open for 0% of the time, Pallas kernels for 12%

profile of v7, /device:TPU:1, one launch (start us, length us, event | category | flops | bytes accessed | tf_op | source)
XLA Modules:
  0.0 74.5 jit_solution(15356859882178796328)
XLA Ops:
  0.7 3.3 %collective-permute-start = (bf16[256,256]{1,0:T(8,128)(2,1)}, bf16[256,256]{1,0:T(8,128)(2,1)S(1)}, u32[]{:S(2)}, u32[]{:S(2)}) collective-permute-start(bf16[256,256]{1,0:T(8,128)(2,1)} %bitcast.11), channel_id=1, source_target_pairs={{0,1},{1,0},{2,3},{3,2},{4,5},{5,4},{6,7},{7,6},{8,9},{9,8},{10,11... | collective-permute-start | bytes 393224 | tf_op jit(solution)/shard_map/ppermute | solution.py:34
  4.0 0.5 collective-permute-start.1
  4.5 0.7 collective-permute-done.partner
  5.2 3.9 %first_near.1 = (bf16[256,6912]{1,0:T(8,128)(2,1)S(1)}, s32[256,32]{1,0:T(8,128)S(1)}) custom-call(bf16[256,256]{1,0:T(8,128)(2,1)S(1)} %collective-permute-done.partner, s32[27,1,256]{2,1,0:T(1,128)} %bitcast.22, bf16[256,256]{1,0:T(8,128)(2,1)} %bitcast.14), custom_call_target="tpu_custom_call" | custom-call | flops 1811939328 | bytes 1048576 | tf_op jit(solution)/shard_map/first_near/pallas_call | solution.py:177
  9.1 5.3 %collective-permute-start.3 = (bf16[64,512]{1,0:T(8,128)(2,1)S(1)}, bf16[64,512]{1,0:T(8,128)(2,1)S(1)}, u32[]{:S(2)}, u32[]{:S(2)}) collective-permute-start(bf16[64,512]{1,0:T(8,128)(2,1)S(1)} %bitcast.16), channel_id=1, source_target_pairs={{0,63},{1,0},{2,1},{3,2},{4,3},{5,4},{6,5},{7,6},{8,7},{9,8},{10,9... | collective-permute-start | bytes 196616 | tf_op jit(solution)/shard_map/ppermute | solution.py:29
  14.4 2.3 %first_far.1.here = bf16[272,256]{1,0:T(8,128)(2,1)S(1)} custom-call(s32[256,32]{1,0:T(8,128)S(1)} %get-tuple-element.15.local_ref, bf16[256,256]{1,0:T(8,128)(2,1)S(1)} %collective-permute-done.1.after, bf16[256,256]{1,0:T(8,128)(2,1)S(1)} %collective-permute-done.2.before, bf16[256,6912]{1,0:T(8,128)(2,1)S(1)} %get-tuple-element.17.near_ref, ...), custom_call_target="tpu_custom_call" | custom-call | flops 1811939328 | bytes 1048576 | tf_op jit(solution)/shard_map/first_far/pallas_call | solution.py:177
  16.8 0.0 copy-start.7
  16.8 1.3 %collective-permute-start.6 = (bf16[272,256]{1,0:T(8,128)(2,1)S(1)}, bf16[272,256]{1,0:T(8,128)(2,1)S(1)}, u32[]{:S(2)}, u32[]{:S(2)}) collective-permute-start(bf16[272,256]{1,0:T(8,128)(2,1)S(1)} %first_far.1.here), channel_id=1, source_target_pairs={{0,1},{1,0},{2,3},{3,2},{4,5},{5,4},{6,7},{7,6},{8,9},{9,8},{10,11... | collective-permute-start | bytes 417800 | tf_op jit(solution)/shard_map/ppermute | solution.py:34
  18.1 0.5 collective-permute-start.4
  18.6 0.5 collective-permute-done.6.partner
  19.1 2.1 %second_near.1.near_ref = bf16[256,6912]{1,0:T(8,128)(2,1)S(1)} custom-call(s32[256,32]{1,0:T(8,128)S(1)} %get-tuple-element.15.local_ref, bf16[272,256]{1,0:T(8,128)(2,1)S(1)} %first_far.1.here, bf16[272,256]{1,0:T(8,128)(2,1)S(1)} %collective-permute-done.6.partner), custom_call_target="tpu_custom_call" | custom-call | flops 1811939328 | bytes 1048576 | tf_op jit(solution)/shard_map/second_near/pallas_call | solution.py:177
  21.1 1.4 %collective-permute-done.4.after = bf16[272,256]{1,0:T(8,128)(2,1)S(1)} collective-permute-done((bf16[272,256]{1,0:T(8,128)(2,1)S(1)}, bf16[272,256]{1,0:T(8,128)(2,1)S(1)}, u32[]{:S(2)}, u32[]{:S(2)}) %collective-permute-start.4) | collective-permute-done | bytes 139296 | tf_op jit(solution)/shard_map/ppermute | solution.py:29
  22.6 0.0 copy-start.2
  22.6 3.5 %second_far.1 = (bf16[256,256]{1,0:T(8,128)(2,1)}, f32[64,384]{1,0:T(8,128)S(1)}, f32[64,256]{1,0:T(8,128)S(1)}, bf16[256,512]{1,0:T(8,128)(2,1)}) custom-call(s32[256,32]{1,0:T(8,128)S(1)} %get-tuple-element.15.local_ref, bf16[272,256]{1,0:T(8,128)(2,1)S(1)} %collective-permute-done.4.after, bf16[272,256]{1,0:T(8,128)(2,1)S(1)} %collective-permute-done.5.before, ...), custom_call_target="tpu_custom_call" | custom-call | flops 1811939328 | bytes 1048576 | tf_op jit(solution)/shard_map/second_far/pallas_call | solution.py:177
  26.1 8.0 %all-to-all-start = ((bf16[32,8,512]{2,1,0:T(8,128)(2,1)}), bf16[32,8,512]{2,1,0:T(8,128)(2,1)S(1)}, u32[]{:S(2)}, u32[]{:S(2)}) async-start(bf16[32,8,512]{2,1,0:T(8,128)(2,1)} %bitcast.6), calls=%async_computation | async-start | bytes 524288 | tf_op jit(solution)/shard_map/all_to_all | solution.py:190
  34.1 1.7 %collective-permute-start.7 = (f32[64,256]{1,0:T(8,128)S(1)}, f32[64,256]{1,0:T(8,128)S(1)}, u32[]{:S(2)}, u32[]{:S(2)}) collective-permute-start(f32[64,256]{1,0:T(8,128)S(1)} %get-tuple-element.23), channel_id=1, source_target_pairs={{0,1},{1,2},{2,3},{3,4},{4,5},{5,6},{6,7},{7,8},{8,9},{9,10},{10,1... | collective-permute-start | bytes 196616 | tf_op jit(solution)/shard_map/ppermute | solution.py:29
  35.8 2.4 %collective-permute-done.7.moved_ref = f32[64,256]{1,0:T(8,128)S(1)} collective-permute-done((f32[64,256]{1,0:T(8,128)S(1)}, f32[64,256]{1,0:T(8,128)S(1)}, u32[]{:S(2)}, u32[]{:S(2)}) %collective-permute-start.7) | collective-permute-done | bytes 65568 | tf_op jit(solution)/shard_map/ppermute | solution.py:29
  38.2 5.0 %all-to-all-done = bf16[32,8,512]{2,1,0:T(8,128)(2,1)S(1)} async-done(((bf16[32,8,512]{2,1,0:T(8,128)(2,1)}), bf16[32,8,512]{2,1,0:T(8,128)(2,1)S(1)}, u32[]{:S(2)}, u32[]{:S(2)}) %all-to-all-start) | async-done | bytes 262176 | tf_op jit(solution)/shard_map/all_to_all | solution.py:190
  43.3 14.9 %all_to_all.15 = f32[8,8,512]{2,1,0:T(8,128)S(1)} all-to-all(f32[8,8,512]{2,1,0:T(8,128)S(1)} %broadcast_in_dim.28), channel_id=1, replica_groups=mesh['y'=4,'z'=8,'x'=4,'core'=2] {'z'}, dimensions={0} | all-to-all | bytes 262144 | tf_op jit(solution)/shard_map/all_to_all | solution.py:190
  58.2 0.7 broadcast_in_dim.29
  58.9 5.7 %all-to-all-start.2 = ((bf16[32,8,512]{2,1,0:T(8,128)(2,1)}), bf16[32,8,512]{2,1,0:T(8,128)(2,1)S(1)}, u32[]{:S(2)}, u32[]{:S(2)}) async-start(bf16[32,8,512]{2,1,0:T(8,128)(2,1)} %broadcast_in_dim.29), calls=%async_computation.2 | async-start | bytes 524288 | tf_op jit(solution)/shard_map/all_to_all | solution.py:190
  64.6 0.8 %coarse.1 = bf16[64,512]{1,0:T(8,128)(2,1)} custom-call(f32[64,384]{1,0:T(8,128)S(1)} %get-tuple-element.22.own_ref, f32[64,256]{1,0:T(8,128)S(1)} %collective-permute-done.7.moved_ref, bf16[256,512]{1,0:T(8,128)(2,1)S(1)} %copy-done.2), custom_call_target="tpu_custom_call" | custom-call | bytes 1048576 | tf_op jit(solution)/shard_map/coarse/pallas_call | solution.py:177
  65.5 8.2 %all-to-all-done.2 = bf16[32,8,512]{2,1,0:T(8,128)(2,1)S(1)} async-done(((bf16[32,8,512]{2,1,0:T(8,128)(2,1)}), bf16[32,8,512]{2,1,0:T(8,128)(2,1)S(1)}, u32[]{:S(2)}, u32[]{:S(2)}) %all-to-all-start.2) | async-done | bytes 262176 | tf_op jit(solution)/shard_map/all_to_all | solution.py:190
  73.6 0.9 %bitcast_convert_fusion = f32[256,512]{1,0:T(8,128)} fusion(bf16[32,8,512]{2,1,0:T(8,128)(2,1)S(1)} %all-to-all-done.2), kind=kLoop, calls=%fused_computation.1 | loop fusion | flops 131072 | bytes 786432 | tf_op jit(solution)/shard_map/reshape | solution.py:205
  (24 shorter events, 0.1 us)
Async XLA Ops:
  0.6 8.5 %copy-start.4 = (bf16[1,64,512]{2,1,0:T(8,128)(2,1)S(1)}, bf16[1,64,512]{2,1,0:T(8,128)(2,1)}, u32[]{:S(2)}) copy-start(bf16[1,64,512]{2,1,0:T(8,128)(2,1)} %param.17) | copy-start | bytes 196612
  0.6 13.8 %copy-start.5 = (s32[1,256]{1,0:T(1,128)S(1)}, s32[1,256]{1,0:T(1,128)}, u32[]{:S(2)}) copy-start(s32[1,256]{1,0:T(1,128)} %parent_ref.3) | copy-start | bytes 3076
  0.7 13.8 %copy-start.6 = (f32[256]{0:T(256)S(1)}, f32[256]{0:T(256)}, u32[]{:S(2)}) copy-start(f32[256]{0:T(256)} %param.14) | copy-start | bytes 3076
  0.7 13.8 %copy-start = (bf16[27,256,256]{2,1,0:T(8,128)(2,1)S(1)}, bf16[27,256,256]{2,1,0:T(8,128)(2,1)}, u32[]{:S(2)}) copy-start(bf16[27,256,256]{2,1,0:T(8,128)(2,1)} %weight_ref.2) | copy-start | bytes 10616836
  0.7 4.5 %collective-permute-start = (bf16[256,256]{1,0:T(8,128)(2,1)}, bf16[256,256]{1,0:T(8,128)(2,1)S(1)}, u32[]{:S(2)}, u32[]{:S(2)}) collective-permute-start(bf16[256,256]{1,0:T(8,128)(2,1)} %bitcast.11), channel_id=1, source_target_pairs={{0,1},{1,0},{2,3},{3,2},{4,5},{5,4},{6,7},{7,6},{8,9},{9,8},{10,11... | collective-permute-start | bytes 393224 | tf_op jit(solution)/shard_map/ppermute | solution.py:34
  4.0 10.4 %collective-permute-start.2 = (bf16[256,256]{1,0:T(8,128)(2,1)}, bf16[256,256]{1,0:T(8,128)(2,1)S(1)}, u32[]{:S(2)}, u32[]{:S(2)}) collective-permute-start(bf16[256,256]{1,0:T(8,128)(2,1)} %bitcast.12), channel_id=1, source_target_pairs={{0,1},{1,2},{2,3},{3,4},{4,5},{5,6},{6,7},{7,8},{8,9},{9,10},{10,1... | collective-permute-start | bytes 393224 | tf_op jit(solution)/shard_map/ppermute | solution.py:29
  4.0 10.4 %collective-permute-start.1 = (bf16[256,256]{1,0:T(8,128)(2,1)}, bf16[256,256]{1,0:T(8,128)(2,1)S(1)}, u32[]{:S(2)}, u32[]{:S(2)}) collective-permute-start(bf16[256,256]{1,0:T(8,128)(2,1)} %bitcast.13), channel_id=1, source_target_pairs={{0,63},{1,0},{2,1},{3,2},{4,3},{5,4},{6,5},{7,6},{8,7},{9,8},{10,9... | collective-permute-start | bytes 393224 | tf_op jit(solution)/shard_map/ppermute | solution.py:29
  9.1 7.7 %collective-permute-start.3 = (bf16[64,512]{1,0:T(8,128)(2,1)S(1)}, bf16[64,512]{1,0:T(8,128)(2,1)S(1)}, u32[]{:S(2)}, u32[]{:S(2)}) collective-permute-start(bf16[64,512]{1,0:T(8,128)(2,1)S(1)} %bitcast.16), channel_id=1, source_target_pairs={{0,63},{1,0},{2,1},{3,2},{4,3},{5,4},{6,5},{7,6},{8,7},{9,8},{10,9... | collective-permute-start | bytes 196616 | tf_op jit(solution)/shard_map/ppermute | solution.py:29
  16.7 5.8 %copy-start.1 = (bf16[27,256,256]{2,1,0:T(8,128)(2,1)S(1)}, bf16[27,256,256]{2,1,0:T(8,128)(2,1)}, u32[]{:S(2)}) copy-start(bf16[27,256,256]{2,1,0:T(8,128)(2,1)} %weight_ref.3) | copy-start | bytes 10616836
  16.7 5.8 %copy-start.3 = (bf16[1,256,256]{2,1,0:T(8,128)(2,1)S(1)}, bf16[1,256,256]{2,1,0:T(8,128)(2,1)}, u32[]{:S(2)}) copy-start(bf16[1,256,256]{2,1,0:T(8,128)(2,1)} %param.9) | copy-start | bytes 393220
  16.8 5.8 %copy-start.7 = (f32[256]{0:T(256)S(1)}, f32[256]{0:T(256)}, u32[]{:S(2)}) copy-start(f32[256]{0:T(256)} %param.15) | copy-start | bytes 3076
  16.8 2.3 %collective-permute-start.6 = (bf16[272,256]{1,0:T(8,128)(2,1)S(1)}, bf16[272,256]{1,0:T(8,128)(2,1)S(1)}, u32[]{:S(2)}, u32[]{:S(2)}) collective-permute-start(bf16[272,256]{1,0:T(8,128)(2,1)S(1)} %first_far.1.here), channel_id=1, source_target_pairs={{0,1},{1,0},{2,3},{3,2},{4,5},{5,4},{6,7},{7,6},{8,9},{9,8},{10,11... | collective-permute-start | bytes 417800 | tf_op jit(solution)/shard_map/ppermute | solution.py:34
  18.1 3.1 %collective-permute-start.5 = (bf16[272,256]{1,0:T(8,128)(2,1)S(1)}, bf16[272,256]{1,0:T(8,128)(2,1)S(1)}, u32[]{:S(2)}, u32[]{:S(2)}) collective-permute-start(bf16[272,256]{1,0:T(8,128)(2,1)S(1)} %first_far.1.here), channel_id=1, source_target_pairs={{0,1},{1,2},{2,3},{3,4},{4,5},{5,6},{6,7},{7,8},{8,9},{9,10},{10,1... | collective-permute-start | bytes 417800 | tf_op jit(solution)/shard_map/ppermute | solution.py:29
  18.1 4.5 %collective-permute-start.4 = (bf16[272,256]{1,0:T(8,128)(2,1)S(1)}, bf16[272,256]{1,0:T(8,128)(2,1)S(1)}, u32[]{:S(2)}, u32[]{:S(2)}) collective-permute-start(bf16[272,256]{1,0:T(8,128)(2,1)S(1)} %first_far.1.here), channel_id=1, source_target_pairs={{0,63},{1,0},{2,1},{3,2},{4,3},{5,4},{6,5},{7,6},{8,7},{9,8},{10,9... | collective-permute-start | bytes 417800 | tf_op jit(solution)/shard_map/ppermute | solution.py:29
  22.6 42.1 %copy-start.2 = (bf16[256,512]{1,0:T(8,128)(2,1)S(1)}, bf16[256,512]{1,0:T(8,128)(2,1)}, u32[]{:S(2)}) copy-start(bf16[256,512]{1,0:T(8,128)(2,1)} %down_ref.1) | copy-start | bytes 786436
  26.1 17.2 %all-to-all-start = ((bf16[32,8,512]{2,1,0:T(8,128)(2,1)}), bf16[32,8,512]{2,1,0:T(8,128)(2,1)S(1)}, u32[]{:S(2)}, u32[]{:S(2)}) async-start(bf16[32,8,512]{2,1,0:T(8,128)(2,1)} %bitcast.6), calls=%async_computation | async-start | bytes 524288 | tf_op jit(solution)/shard_map/all_to_all | solution.py:190
  34.1 4.1 %collective-permute-start.7 = (f32[64,256]{1,0:T(8,128)S(1)}, f32[64,256]{1,0:T(8,128)S(1)}, u32[]{:S(2)}, u32[]{:S(2)}) collective-permute-start(f32[64,256]{1,0:T(8,128)S(1)} %get-tuple-element.23), channel_id=1, source_target_pairs={{0,1},{1,2},{2,3},{3,4},{4,5},{5,6},{6,7},{7,8},{8,9},{9,10},{10,1... | collective-permute-start | bytes 196616 | tf_op jit(solution)/shard_map/ppermute | solution.py:29
  58.9 14.7 %all-to-all-start.2 = ((bf16[32,8,512]{2,1,0:T(8,128)(2,1)}), bf16[32,8,512]{2,1,0:T(8,128)(2,1)S(1)}, u32[]{:S(2)}, u32[]{:S(2)}) async-start(bf16[32,8,512]{2,1,0:T(8,128)(2,1)} %broadcast_in_dim.29), calls=%async_computation.2 | async-start | bytes 524288 | tf_op jit(solution)/shard_map/all_to_all | solution.py:190

commit v8 on v7

--- a/solution.py
+++ b/solution.py
@@ -165,7 +165,8 @@
     ).astype(grad_ref.dtype)
 
 
-def coarse_kernel(own_ref, moved_ref, down_ref, coarse_ref):
+def last_kernel(own_ref, moved_ref, down_ref, gathered_ref, coarse_ref, grad_ref):
+    grad_ref[...] = gathered_ref[...].astype(grad_ref.dtype)
     chans = down_ref.shape[0]
     own = own_ref[...]
     pooled = ((own[:, :chans] + moved_ref[...]) / own[:, chans : chans + 1]).astype(jnp.bfloat16)
@@ -196,13 +197,15 @@
     return exchanged(local_grad.reshape(plane, rows // plane, cols), PLANE)
 
 
-def finished(parts, scale):
-    plane, _, cols = parts.shape
+def space_summed(parts, scale):
     part = jnp.sum(parts.astype(jnp.float32), axis=0)
     copies = jnp.broadcast_to(part[None], (lax.axis_size("z"),) + part.shape)
-    part = jnp.sum(exchanged(copies, "z"), axis=0) * scale
-    copies = jnp.broadcast_to(part.astype(jnp.bfloat16)[None], (plane,) + part.shape)
-    return exchanged(copies, PLANE).astype(jnp.float32).reshape(-1, cols)
+    return jnp.sum(exchanged(copies, "z"), axis=0) * scale
+
+
+def gathered(part):
+    copies = jnp.broadcast_to(part.astype(jnp.bfloat16)[None], (lax.axis_size(PLANE),) + part.shape)
+    return exchanged(copies, PLANE).reshape(-1, part.shape[1])
 
 
 def body(
@@ -273,12 +276,16 @@
         ),
         "second_far", select_and_picked, 2 * product,
     )
-    parts = plane_summed(local_grad)
     worlds_all = lax.axis_size(DP)
     parents_all = par_rows * lax.axis_size(SPACE)
-    moved, parts = lax.optimization_barrier((shifted(sent, 1), parts))
-    coarse = in_vmem(coarse_kernel, bf16((par_rows, out_chans)), (own, moved, down_weight), "coarse")
-    down_grad = finished(parts, 1.0 / math.sqrt(worlds_all * parents_all))
+    part = space_summed(plane_summed(local_grad), 1.0 / math.sqrt(worlds_all * parents_all))
+    sent, part = lax.optimization_barrier((sent, part))
+    coarse, down_grad = in_vmem(
+        last_kernel,
+        (bf16((par_rows, out_chans)), f32((chans, out_chans))),
+        (own, shifted(sent, 1), down_weight, gathered(part)),
+        "coarse_and_grad",
+    )
     return (fine[None], coarse[None], down_grad)
 
 

time: 74.8 us -> 73.8 us (0.987)
  blocking collectives: 14.9 us -> 31.5 us
  starting transfers between devices: 26.4 us -> 18 us
  waiting for transfers between devices: 18.2 us -> 10.3 us
  other arithmetic: 0.92 us -> 0.07 us
    all_to_all x1 -> x2, blocking collectives: 14.9 us -> 31.5 us  [exchanged(): return lax.all_to_all(pieces, axes, 0, 0, tiled=True)]
    all_to_all x2 -> x1, starting transfers between devices: 13.7 us -> 5.35 us  [exchanged(): return lax.all_to_all(pieces, axes, 0, 0, tiled=True)]
    all_to_all x2 -> x1, waiting for transfers between devices: 13.2 us -> 5.26 us  [exchanged(): return lax.all_to_all(pieces, axes, 0, 0, tiled=True)]
    reshape x1 -> x0, other arithmetic: 0.85 us -> none  [finished(): return exchanged(copies, PLANE).astype(jnp.float32).reshape(-1, cols)]
  transfers between devices with their start and end apart: 10 -> 9, of which waited for: 6 -> 5; matrix products, arithmetic and copies ran while one was open for 0% -> 0% of each run, Pallas kernels for 12% -> 11%
where the time goes in v8:
time: 73.8 us; the launch traced here: 73.6 us
  blocking collectives  31.5 us (43%)
  starting transfers between devices  18 us (24%)
  Pallas kernels  12.2 us (17%)
  waiting for transfers between devices  10.3 us (14%)
  between operations  0.8 us (1%)
  local copies, waits for them, and re-layouts  0.78 us (1%)
    all_to_all x2, blocking collectives, exchanged(): return lax.all_to_all(pieces, axes, 0, 0, tiled=True)  31.5 us
    pallas_call x5, Pallas kernels, in_vmem(): pl.pallas_call(kernel, out_shape=outs, in_specs=[vmem] * len(inputs) + [p...  12.2 us
    ppermute x6, starting transfers between devices, shifted(): lax.ppermute(array, SPACE, [(i, (i + by) % length) for i in range(length)])  8.05 us
    all_to_all x1, starting transfers between devices, exchanged(): return lax.all_to_all(pieces, axes, 0, 0, tiled=True)  5.35 us
    all_to_all x1, waiting for transfers between devices, exchanged(): return lax.all_to_all(pieces, axes, 0, 0, tiled=True)  5.26 us
    ppermute x2, starting transfers between devices, from_partner(): return lax.ppermute(array, SPACE, [(i, i ^ 1) for i in range(length)])  4.6 us
    ppermute x6, waiting for transfers between devices, shifted(): lax.ppermute(array, SPACE, [(i, (i + by) % length) for i in range(length)])  3.82 us
  transfers between devices with their start and end apart: 9, of which 5 were waited for; matrix products, arithmetic and copies ran while one was open for 0% of the time, Pallas kernels for 11%

profile of v8, /device:TPU:1, one launch (start us, length us, event | category | flops | bytes accessed | tf_op | source)
XLA Modules:
  0.0 73.6 jit_solution(6866651704581818958)
XLA Ops:
  0.7 3.3 %collective-permute-start = (bf16[256,256]{1,0:T(8,128)(2,1)}, bf16[256,256]{1,0:T(8,128)(2,1)S(1)}, u32[]{:S(2)}, u32[]{:S(2)}) collective-permute-start(bf16[256,256]{1,0:T(8,128)(2,1)} %bitcast.11), channel_id=1, source_target_pairs={{0,1},{1,0},{2,3},{3,2},{4,5},{5,4},{6,7},{7,6},{8,9},{9,8},{10,11... | collective-permute-start | bytes 393224 | tf_op jit(solution)/shard_map/ppermute | solution.py:34
  4.0 0.5 collective-permute-start.1
  4.5 0.7 collective-permute-done.partner
  5.2 3.9 %first_near.1 = (bf16[256,6912]{1,0:T(8,128)(2,1)S(1)}, s32[256,32]{1,0:T(8,128)S(1)}) custom-call(bf16[256,256]{1,0:T(8,128)(2,1)S(1)} %collective-permute-done.partner, s32[27,1,256]{2,1,0:T(1,128)} %bitcast.22, bf16[256,256]{1,0:T(8,128)(2,1)} %bitcast.14), custom_call_target="tpu_custom_call" | custom-call | flops 1811939328 | bytes 1048576 | tf_op jit(solution)/shard_map/first_near/pallas_call | solution.py:178
  9.1 5.3 %collective-permute-start.3 = (bf16[64,512]{1,0:T(8,128)(2,1)S(1)}, bf16[64,512]{1,0:T(8,128)(2,1)S(1)}, u32[]{:S(2)}, u32[]{:S(2)}) collective-permute-start(bf16[64,512]{1,0:T(8,128)(2,1)S(1)} %bitcast.16), channel_id=1, source_target_pairs={{0,63},{1,0},{2,1},{3,2},{4,3},{5,4},{6,5},{7,6},{8,7},{9,8},{10,9... | collective-permute-start | bytes 196616 | tf_op jit(solution)/shard_map/ppermute | solution.py:29
  14.4 2.3 %first_far.1.here = bf16[272,256]{1,0:T(8,128)(2,1)S(1)} custom-call(s32[256,32]{1,0:T(8,128)S(1)} %get-tuple-element.17.local_ref, bf16[256,256]{1,0:T(8,128)(2,1)S(1)} %collective-permute-done.1.after, bf16[256,256]{1,0:T(8,128)(2,1)S(1)} %collective-permute-done.2.before, bf16[256,6912]{1,0:T(8,128)(2,1)S(1)} %get-tuple-element.19.near_ref, ...), custom_call_target="tpu_custom_call" | custom-call | flops 1811939328 | bytes 1048576 | tf_op jit(solution)/shard_map/first_far/pallas_call | solution.py:178
  16.7 0.0 copy-start.1
  16.7 0.0 copy-start.3
  16.8 0.0 copy-start.7
  16.8 1.3 %collective-permute-start.6 = (bf16[272,256]{1,0:T(8,128)(2,1)S(1)}, bf16[272,256]{1,0:T(8,128)(2,1)S(1)}, u32[]{:S(2)}, u32[]{:S(2)}) collective-permute-start(bf16[272,256]{1,0:T(8,128)(2,1)S(1)} %first_far.1.here), channel_id=1, source_target_pairs={{0,1},{1,0},{2,3},{3,2},{4,5},{5,4},{6,7},{7,6},{8,9},{9,8},{10,11... | collective-permute-start | bytes 417800 | tf_op jit(solution)/shard_map/ppermute | solution.py:34
  18.1 0.5 collective-permute-start.4
  18.6 0.5 collective-permute-done.6.partner
  19.1 2.1 %second_near.1.near_ref = bf16[256,6912]{1,0:T(8,128)(2,1)S(1)} custom-call(s32[256,32]{1,0:T(8,128)S(1)} %get-tuple-element.17.local_ref, bf16[272,256]{1,0:T(8,128)(2,1)S(1)} %first_far.1.here, bf16[272,256]{1,0:T(8,128)(2,1)S(1)} %collective-permute-done.6.partner), custom_call_target="tpu_custom_call" | custom-call | flops 1811939328 | bytes 1048576 | tf_op jit(solution)/shard_map/second_near/pallas_call | solution.py:178
  21.1 1.4 %collective-permute-done.4.after = bf16[272,256]{1,0:T(8,128)(2,1)S(1)} collective-permute-done((bf16[272,256]{1,0:T(8,128)(2,1)S(1)}, bf16[272,256]{1,0:T(8,128)(2,1)S(1)}, u32[]{:S(2)}, u32[]{:S(2)}) %collective-permute-start.4) | collective-permute-done | bytes 139296 | tf_op jit(solution)/shard_map/ppermute | solution.py:29
  22.6 0.0 copy-start.2
  22.6 3.0 %second_far.1 = (bf16[256,256]{1,0:T(8,128)(2,1)}, f32[64,384]{1,0:T(8,128)S(1)}, f32[64,256]{1,0:T(8,128)S(1)}, bf16[256,512]{1,0:T(8,128)(2,1)S(1)}) custom-call(s32[256,32]{1,0:T(8,128)S(1)} %get-tuple-element.17.local_ref, bf16[272,256]{1,0:T(8,128)(2,1)S(1)} %collective-permute-done.4.after, bf16[272,256]{1,0:T(8,128)(2,1)S(1)} %collective-permute-done.5.before, ...), custom_call_target="tpu_custom_call" | custom-call | flops 1811939328 | bytes 1048576 | tf_op jit(solution)/shard_map/second_far/pallas_call | solution.py:178
  25.6 16.7 %all_to_all.15 = bf16[32,8,512]{2,1,0:T(8,128)(2,1)S(1)} all-to-all(bf16[32,8,512]{2,1,0:T(8,128)(2,1)S(1)} %bitcast.10), channel_id=1, replica_groups=mesh['y'=4,'z'=8,'x'=4,'core'=2] {'y','x','core'}, dimensions={0} | all-to-all | bytes 524288 | tf_op jit(solution)/shard_map/all_to_all | solution.py:191
  42.4 14.8 %all_to_all.16 = f32[8,8,512]{2,1,0:T(8,128)S(1)} all-to-all(f32[8,8,512]{2,1,0:T(8,128)S(1)} %broadcast_in_dim.27), channel_id=1, replica_groups=mesh['y'=4,'z'=8,'x'=4,'core'=2] {'z'}, dimensions={0} | all-to-all | bytes 262144 | tf_op jit(solution)/shard_map/all_to_all | solution.py:191
  57.2 0.7 broadcast_in_dim.28
  57.9 5.4 %all-to-all-start.2 = ((bf16[32,8,512]{2,1,0:T(8,128)(2,1)}), bf16[32,8,512]{2,1,0:T(8,128)(2,1)S(1)}, u32[]{:S(2)}, u32[]{:S(2)}) async-start(bf16[32,8,512]{2,1,0:T(8,128)(2,1)} %broadcast_in_dim.28), calls=%async_computation.2 | async-start | bytes 524288 | tf_op jit(solution)/shard_map/all_to_all | solution.py:191
  63.3 1.7 %collective-permute-start.7 = (f32[64,256]{1,0:T(8,128)S(1)}, f32[64,256]{1,0:T(8,128)S(1)}, u32[]{:S(2)}, u32[]{:S(2)}) collective-permute-start(f32[64,256]{1,0:T(8,128)S(1)} %get-tuple-element.27), channel_id=1, source_target_pairs={{0,1},{1,2},{2,3},{3,4},{4,5},{5,6},{6,7},{7,8},{8,9},{9,10},{10,1... | collective-permute-start | bytes 196616 | tf_op jit(solution)/shard_map/ppermute | solution.py:29
  65.0 2.4 %collective-permute-done.7.moved_ref = f32[64,256]{1,0:T(8,128)S(1)} collective-permute-done((f32[64,256]{1,0:T(8,128)S(1)}, f32[64,256]{1,0:T(8,128)S(1)}, u32[]{:S(2)}, u32[]{:S(2)}) %collective-permute-start.7) | collective-permute-done | bytes 65568 | tf_op jit(solution)/shard_map/ppermute | solution.py:29
  67.4 5.3 %all-to-all-done.2 = bf16[32,8,512]{2,1,0:T(8,128)(2,1)S(1)} async-done(((bf16[32,8,512]{2,1,0:T(8,128)(2,1)}), bf16[32,8,512]{2,1,0:T(8,128)(2,1)S(1)}, u32[]{:S(2)}, u32[]{:S(2)}) %all-to-all-start.2) | async-done | bytes 262176 | tf_op jit(solution)/shard_map/all_to_all | solution.py:191
  72.6 0.9 %coarse_and_grad.1 = (bf16[64,512]{1,0:T(8,128)(2,1)}, f32[256,512]{1,0:T(8,128)}) custom-call(f32[64,384]{1,0:T(8,128)S(1)} %get-tuple-element.24.own_ref, f32[64,256]{1,0:T(8,128)S(1)} %collective-permute-done.7.moved_ref, bf16[256,512]{1,0:T(8,128)(2,1)S(1)} %copy-done.2, bf16[256,512]{1,0:T(8,128)(2,1)S(1)} %bitcast.9), custom_call_target="tpu_custom_call" | custom-call | bytes 1048576 | tf_op jit(solution)/shard_map/coarse_and_grad/pallas_call | solution.py:178
  (22 shorter events, 0.1 us)
Async XLA Ops:
  0.6 8.5 %copy-start.4 = (bf16[1,64,512]{2,1,0:T(8,128)(2,1)S(1)}, bf16[1,64,512]{2,1,0:T(8,128)(2,1)}, u32[]{:S(2)}) copy-start(bf16[1,64,512]{2,1,0:T(8,128)(2,1)} %param.17) | copy-start | bytes 196612
  0.6 13.8 %copy-start.5 = (s32[1,256]{1,0:T(1,128)S(1)}, s32[1,256]{1,0:T(1,128)}, u32[]{:S(2)}) copy-start(s32[1,256]{1,0:T(1,128)} %parent_ref.3) | copy-start | bytes 3076
  0.7 13.8 %copy-start.6 = (f32[256]{0:T(256)S(1)}, f32[256]{0:T(256)}, u32[]{:S(2)}) copy-start(f32[256]{0:T(256)} %param.14) | copy-start | bytes 3076
  0.7 13.8 %copy-start = (bf16[27,256,256]{2,1,0:T(8,128)(2,1)S(1)}, bf16[27,256,256]{2,1,0:T(8,128)(2,1)}, u32[]{:S(2)}) copy-start(bf16[27,256,256]{2,1,0:T(8,128)(2,1)} %weight_ref.2) | copy-start | bytes 10616836
  0.7 4.5 %collective-permute-start = (bf16[256,256]{1,0:T(8,128)(2,1)}, bf16[256,256]{1,0:T(8,128)(2,1)S(1)}, u32[]{:S(2)}, u32[]{:S(2)}) collective-permute-start(bf16[256,256]{1,0:T(8,128)(2,1)} %bitcast.11), channel_id=1, source_target_pairs={{0,1},{1,0},{2,3},{3,2},{4,5},{5,4},{6,7},{7,6},{8,9},{9,8},{10,11... | collective-permute-start | bytes 393224 | tf_op jit(solution)/shard_map/ppermute | solution.py:34
  4.0 10.4 %collective-permute-start.2 = (bf16[256,256]{1,0:T(8,128)(2,1)}, bf16[256,256]{1,0:T(8,128)(2,1)S(1)}, u32[]{:S(2)}, u32[]{:S(2)}) collective-permute-start(bf16[256,256]{1,0:T(8,128)(2,1)} %bitcast.12), channel_id=1, source_target_pairs={{0,1},{1,2},{2,3},{3,4},{4,5},{5,6},{6,7},{7,8},{8,9},{9,10},{10,1... | collective-permute-start | bytes 393224 | tf_op jit(solution)/shard_map/ppermute | solution.py:29
  4.0 10.4 %collective-permute-start.1 = (bf16[256,256]{1,0:T(8,128)(2,1)}, bf16[256,256]{1,0:T(8,128)(2,1)S(1)}, u32[]{:S(2)}, u32[]{:S(2)}) collective-permute-start(bf16[256,256]{1,0:T(8,128)(2,1)} %bitcast.13), channel_id=1, source_target_pairs={{0,63},{1,0},{2,1},{3,2},{4,3},{5,4},{6,5},{7,6},{8,7},{9,8},{10,9... | collective-permute-start | bytes 393224 | tf_op jit(solution)/shard_map/ppermute | solution.py:29
  9.1 7.7 %collective-permute-start.3 = (bf16[64,512]{1,0:T(8,128)(2,1)S(1)}, bf16[64,512]{1,0:T(8,128)(2,1)S(1)}, u32[]{:S(2)}, u32[]{:S(2)}) collective-permute-start(bf16[64,512]{1,0:T(8,128)(2,1)S(1)} %bitcast.16), channel_id=1, source_target_pairs={{0,63},{1,0},{2,1},{3,2},{4,3},{5,4},{6,5},{7,6},{8,7},{9,8},{10,9... | collective-permute-start | bytes 196616 | tf_op jit(solution)/shard_map/ppermute | solution.py:29
  16.7 5.8 %copy-start.1 = (bf16[27,256,256]{2,1,0:T(8,128)(2,1)S(1)}, bf16[27,256,256]{2,1,0:T(8,128)(2,1)}, u32[]{:S(2)}) copy-start(bf16[27,256,256]{2,1,0:T(8,128)(2,1)} %weight_ref.3) | copy-start | bytes 10616836
  16.7 5.8 %copy-start.3 = (bf16[1,256,256]{2,1,0:T(8,128)(2,1)S(1)}, bf16[1,256,256]{2,1,0:T(8,128)(2,1)}, u32[]{:S(2)}) copy-start(bf16[1,256,256]{2,1,0:T(8,128)(2,1)} %param.9) | copy-start | bytes 393220
  16.8 5.8 %copy-start.7 = (f32[256]{0:T(256)S(1)}, f32[256]{0:T(256)}, u32[]{:S(2)}) copy-start(f32[256]{0:T(256)} %param.15) | copy-start | bytes 3076
  16.8 2.3 %collective-permute-start.6 = (bf16[272,256]{1,0:T(8,128)(2,1)S(1)}, bf16[272,256]{1,0:T(8,128)(2,1)S(1)}, u32[]{:S(2)}, u32[]{:S(2)}) collective-permute-start(bf16[272,256]{1,0:T(8,128)(2,1)S(1)} %first_far.1.here), channel_id=1, source_target_pairs={{0,1},{1,0},{2,3},{3,2},{4,5},{5,4},{6,7},{7,6},{8,9},{9,8},{10,11... | collective-permute-start | bytes 417800 | tf_op jit(solution)/shard_map/ppermute | solution.py:34
  18.1 3.1 %collective-permute-start.5 = (bf16[272,256]{1,0:T(8,128)(2,1)S(1)}, bf16[272,256]{1,0:T(8,128)(2,1)S(1)}, u32[]{:S(2)}, u32[]{:S(2)}) collective-permute-start(bf16[272,256]{1,0:T(8,128)(2,1)S(1)} %first_far.1.here), channel_id=1, source_target_pairs={{0,1},{1,2},{2,3},{3,4},{4,5},{5,6},{6,7},{7,8},{8,9},{9,10},{10,1... | collective-permute-start | bytes 417800 | tf_op jit(solution)/shard_map/ppermute | solution.py:29
  18.1 4.5 %collective-permute-start.4 = (bf16[272,256]{1,0:T(8,128)(2,1)S(1)}, bf16[272,256]{1,0:T(8,128)(2,1)S(1)}, u32[]{:S(2)}, u32[]{:S(2)}) collective-permute-start(bf16[272,256]{1,0:T(8,128)(2,1)S(1)} %first_far.1.here), channel_id=1, source_target_pairs={{0,63},{1,0},{2,1},{3,2},{4,3},{5,4},{6,5},{7,6},{8,7},{9,8},{10,9... | collective-permute-start | bytes 417800 | tf_op jit(solution)/shard_map/ppermute | solution.py:29
  22.6 50.1 %copy-start.2 = (bf16[256,512]{1,0:T(8,128)(2,1)S(1)}, bf16[256,512]{1,0:T(8,128)(2,1)}, u32[]{:S(2)}) copy-start(bf16[256,512]{1,0:T(8,128)(2,1)} %down_ref.1) | copy-start | bytes 786436
  57.9 14.7 %all-to-all-start.2 = ((bf16[32,8,512]{2,1,0:T(8,128)(2,1)}), bf16[32,8,512]{2,1,0:T(8,128)(2,1)S(1)}, u32[]{:S(2)}, u32[]{:S(2)}) async-start(bf16[32,8,512]{2,1,0:T(8,128)(2,1)} %broadcast_in_dim.28), calls=%async_computation.2 | async-start | bytes 524288 | tf_op jit(solution)/shard_map/all_to_all | solution.py:191
  63.3 4.1 %collective-permute-start.7 = (f32[64,256]{1,0:T(8,128)S(1)}, f32[64,256]{1,0:T(8,128)S(1)}, u32[]{:S(2)}, u32[]{:S(2)}) collective-permute-start(f32[64,256]{1,0:T(8,128)S(1)} %get-tuple-element.27), channel_id=1, source_target_pairs={{0,1},{1,2},{2,3},{3,4},{4,5},{5,6},{6,7},{7,8},{8,9},{9,10},{10,1... | collective-permute-start | bytes 196616 | tf_op jit(solution)/shard_map/ppermute | solution.py:29

commit v9 on v8

--- a/solution.py
+++ b/solution.py
@@ -13,6 +13,7 @@
 DP = "y"
 SPACE = ("z", "x", "core")
 PLANE = ("y", "x", "core")
+CHIPS = ("y", "x")
 GROUP = 3
 VMEM_BYTES = 32 << 20
 PAR_ROWS = 64
@@ -165,8 +166,16 @@
     ).astype(grad_ref.dtype)
 
 
-def last_kernel(own_ref, moved_ref, down_ref, gathered_ref, coarse_ref, grad_ref):
-    grad_ref[...] = gathered_ref[...].astype(grad_ref.dtype)
+def spread_kernel(scale, parts_ref, copies_ref):
+    total = jnp.sum(parts_ref[...], axis=0) * scale
+    copies_ref[...] = jnp.broadcast_to(total.astype(copies_ref.dtype)[None], copies_ref.shape)
+
+
+def last_kernel(own_ref, moved_ref, down_ref, mine_ref, other_ref, coarse_ref, grad_ref):
+    mine, other = mine_ref[...], other_ref[...]
+    upper = lax.axis_index("core") == 1
+    grad_ref[:, 0] = jnp.where(upper, other, mine).astype(grad_ref.dtype)
+    grad_ref[:, 1] = jnp.where(upper, mine, other).astype(grad_ref.dtype)
     chans = down_ref.shape[0]
     own = own_ref[...]
     pooled = ((own[:, :chans] + moved_ref[...]) / own[:, chans : chans + 1]).astype(jnp.bfloat16)
@@ -197,15 +206,9 @@
     return exchanged(local_grad.reshape(plane, rows // plane, cols), PLANE)
 
 
-def space_summed(parts, scale):
+def space_parts(parts):
     part = jnp.sum(parts.astype(jnp.float32), axis=0)
-    copies = jnp.broadcast_to(part[None], (lax.axis_size("z"),) + part.shape)
-    return jnp.sum(exchanged(copies, "z"), axis=0) * scale
-
-
-def gathered(part):
-    copies = jnp.broadcast_to(part.astype(jnp.bfloat16)[None], (lax.axis_size(PLANE),) + part.shape)
-    return exchanged(copies, PLANE).reshape(-1, part.shape[1])
+    return exchanged(jnp.broadcast_to(part[None], (lax.axis_size("z"),) + part.shape), "z")
 
 
 def body(
@@ -278,14 +281,23 @@
     )
     worlds_all = lax.axis_size(DP)
     parents_all = par_rows * lax.axis_size(SPACE)
-    part = space_summed(plane_summed(local_grad), 1.0 / math.sqrt(worlds_all * parents_all))
-    sent, part = lax.optimization_barrier((sent, part))
+    parts = space_parts(plane_summed(local_grad))
+    sent, parts = lax.optimization_barrier((sent, parts))
+    chips = lax.axis_size(CHIPS)
+    copies = in_vmem(
+        functools.partial(spread_kernel, 1.0 / math.sqrt(worlds_all * parents_all)),
+        bf16((chips,) + parts.shape[1:]),
+        (parts,),
+        "spread",
+    )
+    mine, moved = lax.optimization_barrier((exchanged(copies, CHIPS), shifted(sent, 1)))
     coarse, down_grad = in_vmem(
         last_kernel,
-        (bf16((par_rows, out_chans)), f32((chans, out_chans))),
-        (own, shifted(sent, 1), down_weight, gathered(part)),
+        (bf16((par_rows, out_chans)), f32((chips, lax.axis_size("core")) + mine.shape[1:])),
+        (own, moved, down_weight, mine, from_partner(mine)),
         "coarse_and_grad",
     )
+    down_grad = down_grad.reshape(chans, out_chans)
     return (fine[None], coarse[None], down_grad)
 
 

time: 73.8 us -> 73.7 us (level)
  waiting for transfers between devices: 10.3 us -> 7.36 us
  starting transfers between devices: 18 us -> 20.8 us
    ppermute x2 -> x3, starting transfers between devices: 4.6 us -> 7.74 us  [from_partner(): return lax.ppermute(array, SPACE, [(i, i ^ 1) for i in range(length)])]
    all_to_all x1, waiting for transfers between devices: 5.26 us -> 2.45 us  [exchanged(): return lax.all_to_all(pieces, axes, 0, 0, tiled=True)]
    all_to_all x1, starting transfers between devices: 5.35 us -> 3.71 us  [exchanged(): return lax.all_to_all(pieces, axes, 0, 0, tiled=True)]
    ppermute x6, starting transfers between devices: 8.05 us -> 9.39 us  [shifted(): lax.ppermute(array, SPACE, [(i, (i + by) % length) for i in range(length)])]
    ppermute x6, waiting for transfers between devices: 3.82 us -> 2.75 us  [shifted(): lax.ppermute(array, SPACE, [(i, (i + by) % length) for i in range(length)])]
    ppermute x2 -> x3, waiting for transfers between devices: 1.17 us -> 2.16 us  [from_partner(): return lax.ppermute(array, SPACE, [(i, i ^ 1) for i in range(length)])]
    pallas_call x5 -> x6, Pallas kernels: 12.2 us -> 12.9 us  [in_vmem(): pl.pallas_call(kernel, out_shape=outs, in_specs=[vmem] * len(inputs) + [p...]
  transfers between devices with their start and end apart: 9 -> 10, of which waited for: 5 -> 6; matrix products, arithmetic and copies ran while one was open for 0% -> 0% of each run, Pallas kernels for 11% -> 11%
where the time goes in v9:
time: 73.7 us; the launch traced here: 73.5 us
  blocking collectives  31.5 us (43%)
  starting transfers between devices  20.8 us (28%)
  Pallas kernels  12.9 us (18%)
  waiting for transfers between devices  7.36 us (10%)
  between operations  0.79 us (1%)
    all_to_all x2, blocking collectives, exchanged(): return lax.all_to_all(pieces, axes, 0, 0, tiled=True)  31.5 us
    pallas_call x6, Pallas kernels, in_vmem(): pl.pallas_call(kernel, out_shape=outs, in_specs=[vmem] * len(inputs) + [p...  12.9 us
    ppermute x6, starting transfers between devices, shifted(): lax.ppermute(array, SPACE, [(i, (i + by) % length) for i in range(length)])  9.39 us
    ppermute x3, starting transfers between devices, from_partner(): return lax.ppermute(array, SPACE, [(i, i ^ 1) for i in range(length)])  7.74 us
    all_to_all x1, starting transfers between devices, exchanged(): return lax.all_to_all(pieces, axes, 0, 0, tiled=True)  3.71 us
    ppermute x6, waiting for transfers between devices, shifted(): lax.ppermute(array, SPACE, [(i, (i + by) % length) for i in range(length)])  2.75 us
    all_to_all x1, waiting for transfers between devices, exchanged(): return lax.all_to_all(pieces, axes, 0, 0, tiled=True)  2.45 us
    ppermute x3, waiting for transfers between devices, from_partner(): return lax.ppermute(array, SPACE, [(i, i ^ 1) for i in range(length)])  2.16 us
  transfers between devices with their start and end apart: 10, of which 6 were waited for; matrix products, arithmetic and copies ran while one was open for 0% of the time, Pallas kernels for 11%

profile of v9, /device:TPU:1, one launch (start us, length us, event | category | flops | bytes accessed | tf_op | source)
XLA Modules:
  0.0 73.5 jit_solution(14562184894934772010)
XLA Ops:
  0.7 3.3 %collective-permute-start = (bf16[256,256]{1,0:T(8,128)(2,1)}, bf16[256,256]{1,0:T(8,128)(2,1)S(1)}, u32[]{:S(2)}, u32[]{:S(2)}) collective-permute-start(bf16[256,256]{1,0:T(8,128)(2,1)} %bitcast.10), channel_id=1, source_target_pairs={{0,1},{1,0},{2,3},{3,2},{4,5},{5,4},{6,7},{7,6},{8,9},{9,8},{10,11... | collective-permute-start | bytes 393224 | tf_op jit(solution)/shard_map/ppermute | solution.py:35
  4.0 0.5 collective-permute-start.1
  4.5 0.7 collective-permute-done.partner
  5.2 3.9 %first_near.1 = (bf16[256,6912]{1,0:T(8,128)(2,1)S(1)}, s32[256,32]{1,0:T(8,128)S(1)}) custom-call(bf16[256,256]{1,0:T(8,128)(2,1)S(1)} %collective-permute-done.partner, s32[27,1,256]{2,1,0:T(1,128)} %bitcast.22, bf16[256,256]{1,0:T(8,128)(2,1)} %bitcast.13), custom_call_target="tpu_custom_call" | custom-call | flops 1811939328 | bytes 1048576 | tf_op jit(solution)/shard_map/first_near/pallas_call | solution.py:187
  9.1 5.3 %collective-permute-start.3 = (bf16[64,512]{1,0:T(8,128)(2,1)S(1)}, bf16[64,512]{1,0:T(8,128)(2,1)S(1)}, u32[]{:S(2)}, u32[]{:S(2)}) collective-permute-start(bf16[64,512]{1,0:T(8,128)(2,1)S(1)} %bitcast.15), channel_id=1, source_target_pairs={{0,63},{1,0},{2,1},{3,2},{4,3},{5,4},{6,5},{7,6},{8,7},{9,8},{10,9... | collective-permute-start | bytes 196616 | tf_op jit(solution)/shard_map/ppermute | solution.py:30
  14.4 2.3 %first_far.1.here = bf16[272,256]{1,0:T(8,128)(2,1)S(1)} custom-call(s32[256,32]{1,0:T(8,128)S(1)} %get-tuple-element.19.local_ref, bf16[256,256]{1,0:T(8,128)(2,1)S(1)} %collective-permute-done.1.after, bf16[256,256]{1,0:T(8,128)(2,1)S(1)} %collective-permute-done.2.before, bf16[256,6912]{1,0:T(8,128)(2,1)S(1)} %get-tuple-element.21.near_ref, ...), custom_call_target="tpu_custom_call" | custom-call | flops 1811939328 | bytes 1048576 | tf_op jit(solution)/shard_map/first_far/pallas_call | solution.py:187
  16.7 0.0 copy-start.1
  16.8 1.3 %collective-permute-start.6 = (bf16[272,256]{1,0:T(8,128)(2,1)S(1)}, bf16[272,256]{1,0:T(8,128)(2,1)S(1)}, u32[]{:S(2)}, u32[]{:S(2)}) collective-permute-start(bf16[272,256]{1,0:T(8,128)(2,1)S(1)} %first_far.1.here), channel_id=1, source_target_pairs={{0,1},{1,0},{2,3},{3,2},{4,5},{5,4},{6,7},{7,6},{8,9},{9,8},{10,11... | collective-permute-start | bytes 417800 | tf_op jit(solution)/shard_map/ppermute | solution.py:35
  18.1 0.5 collective-permute-start.4
  18.6 0.5 collective-permute-done.6.partner
  19.1 2.1 %second_near.1.near_ref = bf16[256,6912]{1,0:T(8,128)(2,1)S(1)} custom-call(s32[256,32]{1,0:T(8,128)S(1)} %get-tuple-element.19.local_ref, bf16[272,256]{1,0:T(8,128)(2,1)S(1)} %first_far.1.here, bf16[272,256]{1,0:T(8,128)(2,1)S(1)} %collective-permute-done.6.partner), custom_call_target="tpu_custom_call" | custom-call | flops 1811939328 | bytes 1048576 | tf_op jit(solution)/shard_map/second_near/pallas_call | solution.py:187
  21.1 1.4 %collective-permute-done.4.after = bf16[272,256]{1,0:T(8,128)(2,1)S(1)} collective-permute-done((bf16[272,256]{1,0:T(8,128)(2,1)S(1)}, bf16[272,256]{1,0:T(8,128)(2,1)S(1)}, u32[]{:S(2)}, u32[]{:S(2)}) %collective-permute-start.4) | collective-permute-done | bytes 139296 | tf_op jit(solution)/shard_map/ppermute | solution.py:30
  22.6 0.0 copy-start.2
  22.6 3.0 %second_far.1 = (bf16[256,256]{1,0:T(8,128)(2,1)}, f32[64,384]{1,0:T(8,128)S(1)}, f32[64,256]{1,0:T(8,128)S(1)}, bf16[256,512]{1,0:T(8,128)(2,1)S(1)}) custom-call(s32[256,32]{1,0:T(8,128)S(1)} %get-tuple-element.19.local_ref, bf16[272,256]{1,0:T(8,128)(2,1)S(1)} %collective-permute-done.4.after, bf16[272,256]{1,0:T(8,128)(2,1)S(1)} %collective-permute-done.5.before, ...), custom_call_target="tpu_custom_call" | custom-call | flops 1811939328 | bytes 1048576 | tf_op jit(solution)/shard_map/second_far/pallas_call | solution.py:187
  25.6 16.7 %all_to_all.15 = bf16[32,8,512]{2,1,0:T(8,128)(2,1)S(1)} all-to-all(bf16[32,8,512]{2,1,0:T(8,128)(2,1)S(1)} %bitcast.9), channel_id=1, replica_groups=mesh['y'=4,'z'=8,'x'=4,'core'=2] {'y','x','core'}, dimensions={0} | all-to-all | bytes 524288 | tf_op jit(solution)/shard_map/all_to_all | solution.py:200
  42.4 14.8 %all_to_all.16.parts_ref = f32[8,8,512]{2,1,0:T(8,128)S(1)} all-to-all(f32[8,8,512]{2,1,0:T(8,128)S(1)} %broadcast_in_dim.21), channel_id=1, replica_groups=mesh['y'=4,'z'=8,'x'=4,'core'=2] {'z'}, dimensions={0} | all-to-all | bytes 262144 | tf_op jit(solution)/shard_map/all_to_all | solution.py:200
  57.2 0.7 spread.1
  57.8 3.7 %all-to-all-start.2 = ((bf16[16,8,512]{2,1,0:T(8,128)(2,1)}), bf16[16,8,512]{2,1,0:T(8,128)(2,1)S(1)}, u32[]{:S(2)}, u32[]{:S(2)}) async-start(bf16[16,8,512]{2,1,0:T(8,128)(2,1)} %spread.1), calls=%async_computation.2 | async-start | bytes 262144 | tf_op jit(solution)/shard_map/all_to_all | solution.py:200
  61.6 3.1 %collective-permute-start.7 = (f32[64,256]{1,0:T(8,128)S(1)}, f32[64,256]{1,0:T(8,128)S(1)}, u32[]{:S(2)}, u32[]{:S(2)}) collective-permute-start(f32[64,256]{1,0:T(8,128)S(1)} %get-tuple-element.30), channel_id=1, source_target_pairs={{0,1},{1,2},{2,3},{3,4},{4,5},{5,6},{6,7},{7,8},{8,9},{9,10},{10,1... | collective-permute-start | bytes 196616 | tf_op jit(solution)/shard_map/ppermute | solution.py:30
  64.6 1.3 %collective-permute-done.7.moved_ref = f32[64,256]{1,0:T(8,128)S(1)} collective-permute-done((f32[64,256]{1,0:T(8,128)S(1)}, f32[64,256]{1,0:T(8,128)S(1)}, u32[]{:S(2)}, u32[]{:S(2)}) %collective-permute-start.7) | collective-permute-done | bytes 65568 | tf_op jit(solution)/shard_map/ppermute | solution.py:30
  65.9 2.5 %all-to-all-done.2.mine_ref = bf16[16,8,512]{2,1,0:T(8,128)(2,1)S(1)} async-done(((bf16[16,8,512]{2,1,0:T(8,128)(2,1)}), bf16[16,8,512]{2,1,0:T(8,128)(2,1)S(1)}, u32[]{:S(2)}, u32[]{:S(2)}) %all-to-all-start.2) | async-done | bytes 131104 | tf_op jit(solution)/shard_map/all_to_all | solution.py:200
  68.4 3.1 %collective-permute-start.8 = (bf16[16,8,512]{2,1,0:T(8,128)(2,1)S(1)}, bf16[16,8,512]{2,1,0:T(8,128)(2,1)S(1)}, u32[]{:S(2)}, u32[]{:S(2)}) collective-permute-start(bf16[16,8,512]{2,1,0:T(8,128)(2,1)S(1)} %all-to-all-done.2.mine_ref), channel_id=1, source_target_pairs={{0,1},{1,0},{2,3},{3,2},{4,5},{5,4},{6,7},{7,6},{8,9},{9,8},{10,11... | collective-permute-start | bytes 393224 | tf_op jit(solution)/shard_map/ppermute | solution.py:35
  71.5 1.0 %collective-permute-done.8.other_ref = bf16[16,8,512]{2,1,0:T(8,128)(2,1)S(1)} collective-permute-done((bf16[16,8,512]{2,1,0:T(8,128)(2,1)S(1)}, bf16[16,8,512]{2,1,0:T(8,128)(2,1)S(1)}, u32[]{:S(2)}, u32[]{:S(2)}) %collective-permute-start.8) | collective-permute-done | bytes 131104 | tf_op jit(solution)/shard_map/ppermute | solution.py:35
  72.5 0.9 %coarse_and_grad.1 = (bf16[64,512]{1,0:T(8,128)(2,1)}, f32[16,2,8,512]{3,2,1,0:T(8,128)}) custom-call(f32[64,384]{1,0:T(8,128)S(1)} %get-tuple-element.26.own_ref, f32[64,256]{1,0:T(8,128)S(1)} %collective-permute-done.7.moved_ref, bf16[256,512]{1,0:T(8,128)(2,1)S(1)} %copy-done.2, bf16[16,8,512]{2,1,0:T(8,128)(2,1)S(1)} %all-to-all-done.2.mine_ref, ...), custom_call_target="tpu_custom_call" | custom-call | bytes 1048576 | tf_op jit(solution)/shard_map/coarse_and_grad/pallas_call | solution.py:187
  (22 shorter events, 0.1 us)
Async XLA Ops:
  0.6 8.5 %copy-start.4 = (bf16[1,64,512]{2,1,0:T(8,128)(2,1)S(1)}, bf16[1,64,512]{2,1,0:T(8,128)(2,1)}, u32[]{:S(2)}) copy-start(bf16[1,64,512]{2,1,0:T(8,128)(2,1)} %param.17) | copy-start | bytes 196612
  0.6 13.8 %copy-start.5 = (s32[1,256]{1,0:T(1,128)S(1)}, s32[1,256]{1,0:T(1,128)}, u32[]{:S(2)}) copy-start(s32[1,256]{1,0:T(1,128)} %parent_ref.3) | copy-start | bytes 3076
  0.7 13.8 %copy-start.6 = (f32[256]{0:T(256)S(1)}, f32[256]{0:T(256)}, u32[]{:S(2)}) copy-start(f32[256]{0:T(256)} %param.14) | copy-start | bytes 3076
  0.7 13.8 %copy-start = (bf16[27,256,256]{2,1,0:T(8,128)(2,1)S(1)}, bf16[27,256,256]{2,1,0:T(8,128)(2,1)}, u32[]{:S(2)}) copy-start(bf16[27,256,256]{2,1,0:T(8,128)(2,1)} %weight_ref.2) | copy-start | bytes 10616836
  0.7 4.5 %collective-permute-start = (bf16[256,256]{1,0:T(8,128)(2,1)}, bf16[256,256]{1,0:T(8,128)(2,1)S(1)}, u32[]{:S(2)}, u32[]{:S(2)}) collective-permute-start(bf16[256,256]{1,0:T(8,128)(2,1)} %bitcast.10), channel_id=1, source_target_pairs={{0,1},{1,0},{2,3},{3,2},{4,5},{5,4},{6,7},{7,6},{8,9},{9,8},{10,11... | collective-permute-start | bytes 393224 | tf_op jit(solution)/shard_map/ppermute | solution.py:35
  4.0 10.4 %collective-permute-start.2 = (bf16[256,256]{1,0:T(8,128)(2,1)}, bf16[256,256]{1,0:T(8,128)(2,1)S(1)}, u32[]{:S(2)}, u32[]{:S(2)}) collective-permute-start(bf16[256,256]{1,0:T(8,128)(2,1)} %bitcast.11), channel_id=1, source_target_pairs={{0,1},{1,2},{2,3},{3,4},{4,5},{5,6},{6,7},{7,8},{8,9},{9,10},{10,1... | collective-permute-start | bytes 393224 | tf_op jit(solution)/shard_map/ppermute | solution.py:30
  4.0 10.4 %collective-permute-start.1 = (bf16[256,256]{1,0:T(8,128)(2,1)}, bf16[256,256]{1,0:T(8,128)(2,1)S(1)}, u32[]{:S(2)}, u32[]{:S(2)}) collective-permute-start(bf16[256,256]{1,0:T(8,128)(2,1)} %bitcast.12), channel_id=1, source_target_pairs={{0,63},{1,0},{2,1},{3,2},{4,3},{5,4},{6,5},{7,6},{8,7},{9,8},{10,9... | collective-permute-start | bytes 393224 | tf_op jit(solution)/shard_map/ppermute | solution.py:30
  9.1 7.7 %collective-permute-start.3 = (bf16[64,512]{1,0:T(8,128)(2,1)S(1)}, bf16[64,512]{1,0:T(8,128)(2,1)S(1)}, u32[]{:S(2)}, u32[]{:S(2)}) collective-permute-start(bf16[64,512]{1,0:T(8,128)(2,1)S(1)} %bitcast.15), channel_id=1, source_target_pairs={{0,63},{1,0},{2,1},{3,2},{4,3},{5,4},{6,5},{7,6},{8,7},{9,8},{10,9... | collective-permute-start | bytes 196616 | tf_op jit(solution)/shard_map/ppermute | solution.py:30
  16.7 5.8 %copy-start.1 = (bf16[27,256,256]{2,1,0:T(8,128)(2,1)S(1)}, bf16[27,256,256]{2,1,0:T(8,128)(2,1)}, u32[]{:S(2)}) copy-start(bf16[27,256,256]{2,1,0:T(8,128)(2,1)} %weight_ref.3) | copy-start | bytes 10616836
  16.7 5.8 %copy-start.3 = (bf16[1,256,256]{2,1,0:T(8,128)(2,1)S(1)}, bf16[1,256,256]{2,1,0:T(8,128)(2,1)}, u32[]{:S(2)}) copy-start(bf16[1,256,256]{2,1,0:T(8,128)(2,1)} %param.9) | copy-start | bytes 393220
  16.8 5.8 %copy-start.7 = (f32[256]{0:T(256)S(1)}, f32[256]{0:T(256)}, u32[]{:S(2)}) copy-start(f32[256]{0:T(256)} %param.15) | copy-start | bytes 3076
  16.8 2.3 %collective-permute-start.6 = (bf16[272,256]{1,0:T(8,128)(2,1)S(1)}, bf16[272,256]{1,0:T(8,128)(2,1)S(1)}, u32[]{:S(2)}, u32[]{:S(2)}) collective-permute-start(bf16[272,256]{1,0:T(8,128)(2,1)S(1)} %first_far.1.here), channel_id=1, source_target_pairs={{0,1},{1,0},{2,3},{3,2},{4,5},{5,4},{6,7},{7,6},{8,9},{9,8},{10,11... | collective-permute-start | bytes 417800 | tf_op jit(solution)/shard_map/ppermute | solution.py:35
  18.1 3.1 %collective-permute-start.5 = (bf16[272,256]{1,0:T(8,128)(2,1)S(1)}, bf16[272,256]{1,0:T(8,128)(2,1)S(1)}, u32[]{:S(2)}, u32[]{:S(2)}) collective-permute-start(bf16[272,256]{1,0:T(8,128)(2,1)S(1)} %first_far.1.here), channel_id=1, source_target_pairs={{0,1},{1,2},{2,3},{3,4},{4,5},{5,6},{6,7},{7,8},{8,9},{9,10},{10,1... | collective-permute-start | bytes 417800 | tf_op jit(solution)/shard_map/ppermute | solution.py:30
  18.1 4.5 %collective-permute-start.4 = (bf16[272,256]{1,0:T(8,128)(2,1)S(1)}, bf16[272,256]{1,0:T(8,128)(2,1)S(1)}, u32[]{:S(2)}, u32[]{:S(2)}) collective-permute-start(bf16[272,256]{1,0:T(8,128)(2,1)S(1)} %first_far.1.here), channel_id=1, source_target_pairs={{0,63},{1,0},{2,1},{3,2},{4,3},{5,4},{6,5},{7,6},{8,7},{9,8},{10,9... | collective-permute-start | bytes 417800 | tf_op jit(solution)/shard_map/ppermute | solution.py:30
  22.6 50.0 %copy-start.2 = (bf16[256,512]{1,0:T(8,128)(2,1)S(1)}, bf16[256,512]{1,0:T(8,128)(2,1)}, u32[]{:S(2)}) copy-start(bf16[256,512]{1,0:T(8,128)(2,1)} %down_ref.1) | copy-start | bytes 786436
  57.8 10.6 %all-to-all-start.2 = ((bf16[16,8,512]{2,1,0:T(8,128)(2,1)}), bf16[16,8,512]{2,1,0:T(8,128)(2,1)S(1)}, u32[]{:S(2)}, u32[]{:S(2)}) async-start(bf16[16,8,512]{2,1,0:T(8,128)(2,1)} %spread.1), calls=%async_computation.2 | async-start | bytes 262144 | tf_op jit(solution)/shard_map/all_to_all | solution.py:200
  61.6 4.4 %collective-permute-start.7 = (f32[64,256]{1,0:T(8,128)S(1)}, f32[64,256]{1,0:T(8,128)S(1)}, u32[]{:S(2)}, u32[]{:S(2)}) collective-permute-start(f32[64,256]{1,0:T(8,128)S(1)} %get-tuple-element.30), channel_id=1, source_target_pairs={{0,1},{1,2},{2,3},{3,4},{4,5},{5,6},{6,7},{7,8},{8,9},{9,10},{10,1... | collective-permute-start | bytes 196616 | tf_op jit(solution)/shard_map/ppermute | solution.py:30
  68.4 4.1 %collective-permute-start.8 = (bf16[16,8,512]{2,1,0:T(8,128)(2,1)S(1)}, bf16[16,8,512]{2,1,0:T(8,128)(2,1)S(1)}, u32[]{:S(2)}, u32[]{:S(2)}) collective-permute-start(bf16[16,8,512]{2,1,0:T(8,128)(2,1)S(1)} %all-to-all-done.2.mine_ref), channel_id=1, source_target_pairs={{0,1},{1,0},{2,3},{3,2},{4,5},{5,4},{6,7},{7,6},{8,9},{9,8},{10,11... | collective-permute-start | bytes 393224 | tf_op jit(solution)/shard_map/ppermute | solution.py:35

commit v10 on v8

--- a/solution.py
+++ b/solution.py
@@ -48,25 +48,27 @@
     return jnp.concatenate([local, jnp.full((-taps % 8, rows), -1, jnp.int32)], axis=0).T
 
 
-def pick(local, taps, blocks, select_ref, put, wait=None):
+def select(local, taps, starts, select_ref):
     rows = local.shape[0]
     places = lax.broadcasted_iota(jnp.int16, (rows, rows), 1)
     one, zero = jnp.ones((), jnp.bfloat16), jnp.zeros((), jnp.bfloat16)
     for tap in range(taps):
         column = jnp.broadcast_to(local[:, tap : tap + 1], (rows, 128))
-        for b, (_, start) in enumerate(blocks):
+        for b, start in enumerate(starts):
             wanted = (column - start).astype(jnp.int16)
             wanted = jnp.concatenate([wanted] * (rows // 128), axis=1)
             select_ref[tap * rows : (tap + 1) * rows, b * rows : (b + 1) * rows] = jnp.where(
                 wanted == places, one, zero
             )
-    if wait is not None:
-        wait()
+
+
+def pick(taps, blocks, select_ref, put):
+    rows = blocks[0].shape[0]
     for first in range(0, taps, GROUP):
         part = select_ref[first * rows : (first + GROUP) * rows]
         picked = sum(
             jnp.dot(part[:, b * rows : (b + 1) * rows], block[...], preferred_element_type=jnp.float32)
-            for b, (block, _) in enumerate(blocks)
+            for b, block in enumerate(blocks)
         ).astype(jnp.bfloat16)
         for j in range(GROUP):
             put(first + j, picked[j * rows : (j + 1) * rows])
@@ -74,16 +76,19 @@
 
 def pick_near(local, here, partner, select_ref, near_ref, wait=None):
     rows, chans = here.shape
-    blocks = ((here, rows), (partner, 2 * rows * (1 - lax.axis_index("core"))))
+    taps = near_ref.shape[1] // chans
+    select(local, taps, (rows, 2 * rows * (1 - lax.axis_index("core"))), select_ref)
 
     def put(tap, picked):
         near_ref[:, tap * chans : (tap + 1) * chans] = picked
 
-    pick(local, near_ref.shape[1] // chans, blocks, select_ref, put, wait)
-
-
-def convolved(local, before, after, near_ref, weight_ref, select_ref, picked_ref):
-    rows, chans = before.shape
+    if wait is not None:
+        wait()
+    pick(taps, (here, partner), select_ref, put)
+
+
+def convolved(select_ref, before, after, near_ref, weight_ref, picked_ref):
+    chans = before.shape[1]
     across = jnp.where(lax.axis_index("core") == 1, after, before)
     taps = weight_ref.shape[0]
 
@@ -91,7 +96,7 @@
         columns = slice(tap * chans, (tap + 1) * chans)
         picked_ref[:, columns] = near_ref[:, columns] + picked
 
-    pick(local, taps, ((across, 2 * rows * lax.axis_index("core")),), select_ref, put)
+    pick(taps, (across,), select_ref, put)
     return jnp.dot(
         picked_ref[...],
         weight_ref[...].reshape(taps * chans, weight_ref.shape[2]),
@@ -100,7 +105,7 @@
 
 
 def first_near_kernel(
-    partner, taps_hbm, here_hbm, near_ref, local_ref, select_ref, taps_ref, here, taps_sem, here_sem
+    partner, taps_hbm, here_hbm, near_ref, local_ref, far_ref, select_ref, taps_ref, here, taps_sem, here_sem
 ):
     taps_copy = pltpu.make_async_copy(taps_hbm, taps_ref, taps_sem)
     here_copy = pltpu.make_async_copy(here_hbm, here, here_sem)
@@ -110,13 +115,14 @@
     local = local_table(taps_ref)
     local_ref[...] = local
     pick_near(local, here, partner, select_ref, near_ref, here_copy.wait)
+    rows = here.shape[0]
+    select(local, taps_ref.shape[0], (2 * rows * lax.axis_index("core"),), far_ref)
 
 
 def first_far_kernel(
-    local_ref, after, before, near_ref, weight_ref, gain_ref, parent_ref,
-    middle_ref, select_ref, picked_ref,
+    select_ref, after, before, near_ref, weight_ref, gain_ref, parent_ref, middle_ref, picked_ref
 ):
-    total = convolved(local_ref[...], before[...], after[...], near_ref, weight_ref, select_ref, picked_ref)
+    total = convolved(select_ref, before[...], after[...], near_ref, weight_ref, picked_ref)
     rows = total.shape[0]
     middle_ref[:rows] = settled(total, gain_ref[...]).astype(middle_ref.dtype)
     ids = parent_ref[...] - lax.axis_index(SPACE) * PAR_ROWS
@@ -134,12 +140,12 @@
 
 
 def second_far_kernel(
-    local_ref, after, before, near_ref, weight_ref, gain_ref, feature_ref, parent_ref,
+    select_ref, after, before, near_ref, weight_ref, gain_ref, feature_ref, parent_ref,
     cotangent_ref, next_ref,
-    fine_ref, own_ref, sent_ref, grad_ref, select_ref, picked_ref,
+    fine_ref, own_ref, sent_ref, grad_ref, picked_ref,
 ):
     rows, chans = feature_ref.shape
-    total = convolved(local_ref[...], before[:rows], after[:rows], near_ref, weight_ref, select_ref, picked_ref)
+    total = convolved(select_ref, before[:rows], after[:rows], near_ref, weight_ref, picked_ref)
     fine = feature_ref[...].astype(jnp.float32) + settled(total, gain_ref[...])
     fine = fine.astype(fine_ref.dtype)
     fine_ref[...] = fine
@@ -227,18 +233,19 @@
     f32 = functools.partial(jax.ShapeDtypeStruct, dtype=jnp.float32)
     product = 2 * taps * rows * chans * rows
     near_shape = bf16((rows, taps * chans))
-    select = [pltpu.VMEM((taps * rows, 2 * rows), jnp.bfloat16)]
-    select_and_picked = [
-        pltpu.VMEM((taps * rows, rows), jnp.bfloat16),
-        pltpu.VMEM((rows, taps * chans), jnp.bfloat16),
-    ]
+    chosen = [pltpu.VMEM((taps * rows, 2 * rows), jnp.bfloat16)]
+    all_picked = [pltpu.VMEM((rows, taps * chans), jnp.bfloat16)]
     after, before = shifted(field, -1), shifted(field, 1)
-    near, local = in_vmem(
+    near, local, far = in_vmem(
         first_near_kernel,
-        (near_shape, jax.ShapeDtypeStruct((rows, taps + -taps % 8), jnp.int32)),
+        (
+            near_shape,
+            jax.ShapeDtypeStruct((rows, taps + -taps % 8), jnp.int32),
+            bf16((taps * rows, rows)),
+        ),
         (from_partner(field),),
         "first_near",
-        select
+        chosen
         + [
             pltpu.VMEM((taps, 1, rows), jnp.int32),
             pltpu.VMEM((rows, chans), jnp.bfloat16),
@@ -253,14 +260,14 @@
     middle = in_vmem(
         first_far_kernel,
         bf16((rows + 16, chans)),
-        (local, after, before, near, conv_first, gain_first[None], parents),
-        "first_far", select_and_picked, 2 * product,
+        (far, after, before, near, conv_first, gain_first[None], parents),
+        "first_far", all_picked, 2 * product,
     )
     middle, next_grad = lax.optimization_barrier((middle, next_grad))
     after, before = shifted(middle, -1), shifted(middle, 1)
     partner = from_partner(middle)
     near = in_vmem(
-        second_near_kernel, near_shape, (local, middle, partner), "second_near", select, 2 * product
+        second_near_kernel, near_shape, (local, middle, partner), "second_near", chosen, 2 * product
     )
     fine, own, sent, local_grad = in_vmem(
         second_far_kernel,
@@ -271,10 +278,10 @@
             bf16((chans, out_chans)),
         ),
         (
-            local, after, before, near, conv_second, gain_second[None], field, parents,
+            far, after, before, near, conv_second, gain_second[None], field, parents,
             grad_in, next_grad,
         ),
-        "second_far", select_and_picked, 2 * product,
+        "second_far", all_picked, 2 * product,
     )
     worlds_all = lax.axis_size(DP)
     parents_all = par_rows * lax.axis_size(SPACE)

time: 73.8 us -> 74.2 us (level)
  transfers between devices with their start and end apart: 9 -> 9, of which waited for: 5 -> 5; matrix products, arithmetic and copies ran while one was open for 0% -> 0% of each run, Pallas kernels for 11% -> 12%
where the time goes in v10:
time: 74.2 us; the launch traced here: 74 us
  blocking collectives  31.5 us (42%)
  starting transfers between devices  18 us (24%)
  Pallas kernels  12.5 us (17%)
  waiting for transfers between devices  10.3 us (14%)
  between operations  0.8 us (1%)
  local copies, waits for them, and re-layouts  0.78 us (1%)
    all_to_all x2, blocking collectives, exchanged(): return lax.all_to_all(pieces, axes, 0, 0, tiled=True)  31.5 us
    pallas_call x5, Pallas kernels, in_vmem(): pl.pallas_call(kernel, out_shape=outs, in_specs=[vmem] * len(inputs) + [p...  12.5 us
    ppermute x6, starting transfers between devices, shifted(): lax.ppermute(array, SPACE, [(i, (i + by) % length) for i in range(length)])  8.05 us
    all_to_all x1, starting transfers between devices, exchanged(): return lax.all_to_all(pieces, axes, 0, 0, tiled=True)  5.35 us
    all_to_all x1, waiting for transfers between devices, exchanged(): return lax.all_to_all(pieces, axes, 0, 0, tiled=True)  5.26 us
    ppermute x2, starting transfers between devices, from_partner(): return lax.ppermute(array, SPACE, [(i, i ^ 1) for i in range(length)])  4.6 us
    ppermute x6, waiting for transfers between devices, shifted(): lax.ppermute(array, SPACE, [(i, (i + by) % length) for i in range(length)])  3.83 us
  transfers between devices with their start and end apart: 9, of which 5 were waited for; matrix products, arithmetic and copies ran while one was open for 0% of the time, Pallas kernels for 12%

profile of v10, /device:TPU:1, one launch (start us, length us, event | category | flops | bytes accessed | tf_op | source)
XLA Modules:
  0.0 74.0 jit_solution(394982906928749141)
XLA Ops:
  0.7 3.3 %collective-permute-start = (bf16[256,256]{1,0:T(8,128)(2,1)}, bf16[256,256]{1,0:T(8,128)(2,1)S(1)}, u32[]{:S(2)}, u32[]{:S(2)}) collective-permute-start(bf16[256,256]{1,0:T(8,128)(2,1)} %bitcast.11), channel_id=1, source_target_pairs={{0,1},{1,0},{2,3},{3,2},{4,5},{5,4},{6,7},{7,6},{8,9},{9,8},{10,11... | collective-permute-start | bytes 393224 | tf_op jit(solution)/shard_map/ppermute | solution.py:34
  4.0 0.5 collective-permute-start.1
  4.5 0.7 collective-permute-done.partner
  5.2 4.2 %first_near.1 = (bf16[256,6912]{1,0:T(8,128)(2,1)S(1)}, s32[256,32]{1,0:T(8,128)S(1)}, bf16[6912,256]{1,0:T(8,128)(2,1)S(1)}) custom-call(bf16[256,256]{1,0:T(8,128)(2,1)S(1)} %collective-permute-done.partner, s32[27,1,256]{2,1,0:T(1,128)} %bitcast.22, bf16[256,256]{1,0:T(8,128)(2,1)} %bitcast.14), custom_call_target="tpu_custom_call" | custom-call | flops 1811939328 | bytes 1048576 | tf_op jit(solution)/shard_map/first_near/pallas_call | solution.py:184
  9.4 5.3 %collective-permute-start.3 = (bf16[64,512]{1,0:T(8,128)(2,1)S(1)}, bf16[64,512]{1,0:T(8,128)(2,1)S(1)}, u32[]{:S(2)}, u32[]{:S(2)}) collective-permute-start(bf16[64,512]{1,0:T(8,128)(2,1)S(1)} %bitcast.16), channel_id=1, source_target_pairs={{0,63},{1,0},{2,1},{3,2},{4,3},{5,4},{6,5},{7,6},{8,7},{9,8},{10,9... | collective-permute-start | bytes 196616 | tf_op jit(solution)/shard_map/ppermute | solution.py:29
  14.8 2.3 %first_far.1.here = bf16[272,256]{1,0:T(8,128)(2,1)S(1)} custom-call(bf16[6912,256]{1,0:T(8,128)(2,1)S(1)} %get-tuple-element.18.select_ref, bf16[256,256]{1,0:T(8,128)(2,1)S(1)} %collective-permute-done.1.after, bf16[256,256]{1,0:T(8,128)(2,1)S(1)} %collective-permute-done.2.before, bf16[256,6912]{1,0:T(8,128)(2,1)S(1)} %get-tuple-element.20.near_ref, ...), custom_call_target="tpu_custom_call" | custom-call | flops 1811939328 | bytes 1048576 | tf_op jit(solution)/shard_map/first_far/pallas_call | solution.py:184
  17.1 0.0 copy-start
  17.1 0.0 copy-start.3
  17.1 0.0 copy-start.6
  17.2 1.3 %collective-permute-start.6 = (bf16[272,256]{1,0:T(8,128)(2,1)S(1)}, bf16[272,256]{1,0:T(8,128)(2,1)S(1)}, u32[]{:S(2)}, u32[]{:S(2)}) collective-permute-start(bf16[272,256]{1,0:T(8,128)(2,1)S(1)} %first_far.1.here), channel_id=1, source_target_pairs={{0,1},{1,0},{2,3},{3,2},{4,5},{5,4},{6,7},{7,6},{8,9},{9,8},{10,11... | collective-permute-start | bytes 417800 | tf_op jit(solution)/shard_map/ppermute | solution.py:34
  18.4 0.5 collective-permute-start.4
  18.9 0.5 collective-permute-done.6.partner
  19.4 2.1 %second_near.1.near_ref = bf16[256,6912]{1,0:T(8,128)(2,1)S(1)} custom-call(s32[256,32]{1,0:T(8,128)S(1)} %get-tuple-element.23.local_ref, bf16[272,256]{1,0:T(8,128)(2,1)S(1)} %first_far.1.here, bf16[272,256]{1,0:T(8,128)(2,1)S(1)} %collective-permute-done.6.partner), custom_call_target="tpu_custom_call" | custom-call | flops 1811939328 | bytes 1048576 | tf_op jit(solution)/shard_map/second_near/pallas_call | solution.py:184
  21.5 1.4 %collective-permute-done.4.after = bf16[272,256]{1,0:T(8,128)(2,1)S(1)} collective-permute-done((bf16[272,256]{1,0:T(8,128)(2,1)S(1)}, bf16[272,256]{1,0:T(8,128)(2,1)S(1)}, u32[]{:S(2)}, u32[]{:S(2)}) %collective-permute-start.4) | collective-permute-done | bytes 139296 | tf_op jit(solution)/shard_map/ppermute | solution.py:29
  22.9 0.0 copy-start.2
  22.9 3.0 %second_far.1 = (bf16[256,256]{1,0:T(8,128)(2,1)}, f32[64,384]{1,0:T(8,128)S(1)}, f32[64,256]{1,0:T(8,128)S(1)}, bf16[256,512]{1,0:T(8,128)(2,1)S(1)}) custom-call(bf16[6912,256]{1,0:T(8,128)(2,1)S(1)} %get-tuple-element.18.select_ref, bf16[272,256]{1,0:T(8,128)(2,1)S(1)} %collective-permute-done.4.after, ...), custom_call_target="tpu_custom_call" | custom-call | flops 1811939328 | bytes 1048576 | tf_op jit(solution)/shard_map/second_far/pallas_call | solution.py:184
  26.0 16.7 %all_to_all.15 = bf16[32,8,512]{2,1,0:T(8,128)(2,1)S(1)} all-to-all(bf16[32,8,512]{2,1,0:T(8,128)(2,1)S(1)} %bitcast.10), channel_id=1, replica_groups=mesh['y'=4,'z'=8,'x'=4,'core'=2] {'y','x','core'}, dimensions={0} | all-to-all | bytes 524288 | tf_op jit(solution)/shard_map/all_to_all | solution.py:197
  42.8 14.8 %all_to_all.16 = f32[8,8,512]{2,1,0:T(8,128)S(1)} all-to-all(f32[8,8,512]{2,1,0:T(8,128)S(1)} %broadcast_in_dim.27), channel_id=1, replica_groups=mesh['y'=4,'z'=8,'x'=4,'core'=2] {'z'}, dimensions={0} | all-to-all | bytes 262144 | tf_op jit(solution)/shard_map/all_to_all | solution.py:197
  57.6 0.7 broadcast_in_dim.28
  58.3 5.4 %all-to-all-start.2 = ((bf16[32,8,512]{2,1,0:T(8,128)(2,1)}), bf16[32,8,512]{2,1,0:T(8,128)(2,1)S(1)}, u32[]{:S(2)}, u32[]{:S(2)}) async-start(bf16[32,8,512]{2,1,0:T(8,128)(2,1)} %broadcast_in_dim.28), calls=%async_computation.2 | async-start | bytes 524288 | tf_op jit(solution)/shard_map/all_to_all | solution.py:197
  63.6 1.7 %collective-permute-start.7 = (f32[64,256]{1,0:T(8,128)S(1)}, f32[64,256]{1,0:T(8,128)S(1)}, u32[]{:S(2)}, u32[]{:S(2)}) collective-permute-start(f32[64,256]{1,0:T(8,128)S(1)} %get-tuple-element.29), channel_id=1, source_target_pairs={{0,1},{1,2},{2,3},{3,4},{4,5},{5,6},{6,7},{7,8},{8,9},{9,10},{10,1... | collective-permute-start | bytes 196616 | tf_op jit(solution)/shard_map/ppermute | solution.py:29
  65.4 2.4 %collective-permute-done.7.moved_ref = f32[64,256]{1,0:T(8,128)S(1)} collective-permute-done((f32[64,256]{1,0:T(8,128)S(1)}, f32[64,256]{1,0:T(8,128)S(1)}, u32[]{:S(2)}, u32[]{:S(2)}) %collective-permute-start.7) | collective-permute-done | bytes 65568 | tf_op jit(solution)/shard_map/ppermute | solution.py:29
  67.8 5.3 %all-to-all-done.2 = bf16[32,8,512]{2,1,0:T(8,128)(2,1)S(1)} async-done(((bf16[32,8,512]{2,1,0:T(8,128)(2,1)}), bf16[32,8,512]{2,1,0:T(8,128)(2,1)S(1)}, u32[]{:S(2)}, u32[]{:S(2)}) %all-to-all-start.2) | async-done | bytes 262176 | tf_op jit(solution)/shard_map/all_to_all | solution.py:197
  73.0 0.9 %coarse_and_grad.1 = (bf16[64,512]{1,0:T(8,128)(2,1)}, f32[256,512]{1,0:T(8,128)}) custom-call(f32[64,384]{1,0:T(8,128)S(1)} %get-tuple-element.26.own_ref, f32[64,256]{1,0:T(8,128)S(1)} %collective-permute-done.7.moved_ref, bf16[256,512]{1,0:T(8,128)(2,1)S(1)} %copy-done.2, bf16[256,512]{1,0:T(8,128)(2,1)S(1)} %bitcast.9), custom_call_target="tpu_custom_call" | custom-call | bytes 1048576 | tf_op jit(solution)/shard_map/coarse_and_grad/pallas_call | solution.py:184
  (22 shorter events, 0.1 us)
Async XLA Ops:
  0.6 8.8 %copy-start.4 = (bf16[1,64,512]{2,1,0:T(8,128)(2,1)S(1)}, bf16[1,64,512]{2,1,0:T(8,128)(2,1)}, u32[]{:S(2)}) copy-start(bf16[1,64,512]{2,1,0:T(8,128)(2,1)} %param.17) | copy-start | bytes 196612
  0.6 14.1 %copy-start.5 = (s32[1,256]{1,0:T(1,128)S(1)}, s32[1,256]{1,0:T(1,128)}, u32[]{:S(2)}) copy-start(s32[1,256]{1,0:T(1,128)} %parent_ref.3) | copy-start | bytes 3076
  0.7 14.1 %copy-start.7 = (f32[256]{0:T(256)S(1)}, f32[256]{0:T(256)}, u32[]{:S(2)}) copy-start(f32[256]{0:T(256)} %param.14) | copy-start | bytes 3076
  0.7 14.1 %copy-start.1 = (bf16[27,256,256]{2,1,0:T(8,128)(2,1)S(1)}, bf16[27,256,256]{2,1,0:T(8,128)(2,1)}, u32[]{:S(2)}) copy-start(bf16[27,256,256]{2,1,0:T(8,128)(2,1)} %weight_ref.2) | copy-start | bytes 10616836
  0.7 4.5 %collective-permute-start = (bf16[256,256]{1,0:T(8,128)(2,1)}, bf16[256,256]{1,0:T(8,128)(2,1)S(1)}, u32[]{:S(2)}, u32[]{:S(2)}) collective-permute-start(bf16[256,256]{1,0:T(8,128)(2,1)} %bitcast.11), channel_id=1, source_target_pairs={{0,1},{1,0},{2,3},{3,2},{4,5},{5,4},{6,7},{7,6},{8,9},{9,8},{10,11... | collective-permute-start | bytes 393224 | tf_op jit(solution)/shard_map/ppermute | solution.py:34
  4.0 10.8 %collective-permute-start.2 = (bf16[256,256]{1,0:T(8,128)(2,1)}, bf16[256,256]{1,0:T(8,128)(2,1)S(1)}, u32[]{:S(2)}, u32[]{:S(2)}) collective-permute-start(bf16[256,256]{1,0:T(8,128)(2,1)} %bitcast.12), channel_id=1, source_target_pairs={{0,1},{1,2},{2,3},{3,4},{4,5},{5,6},{6,7},{7,8},{8,9},{9,10},{10,1... | collective-permute-start | bytes 393224 | tf_op jit(solution)/shard_map/ppermute | solution.py:29
  4.0 10.8 %collective-permute-start.1 = (bf16[256,256]{1,0:T(8,128)(2,1)}, bf16[256,256]{1,0:T(8,128)(2,1)S(1)}, u32[]{:S(2)}, u32[]{:S(2)}) collective-permute-start(bf16[256,256]{1,0:T(8,128)(2,1)} %bitcast.13), channel_id=1, source_target_pairs={{0,63},{1,0},{2,1},{3,2},{4,3},{5,4},{6,5},{7,6},{8,7},{9,8},{10,9... | collective-permute-start | bytes 393224 | tf_op jit(solution)/shard_map/ppermute | solution.py:29
  9.4 7.7 %collective-permute-start.3 = (bf16[64,512]{1,0:T(8,128)(2,1)S(1)}, bf16[64,512]{1,0:T(8,128)(2,1)S(1)}, u32[]{:S(2)}, u32[]{:S(2)}) collective-permute-start(bf16[64,512]{1,0:T(8,128)(2,1)S(1)} %bitcast.16), channel_id=1, source_target_pairs={{0,63},{1,0},{2,1},{3,2},{4,3},{5,4},{6,5},{7,6},{8,7},{9,8},{10,9... | collective-permute-start | bytes 196616 | tf_op jit(solution)/shard_map/ppermute | solution.py:29
  17.1 5.8 %copy-start = (bf16[27,256,256]{2,1,0:T(8,128)(2,1)S(1)}, bf16[27,256,256]{2,1,0:T(8,128)(2,1)}, u32[]{:S(2)}) copy-start(bf16[27,256,256]{2,1,0:T(8,128)(2,1)} %weight_ref.3) | copy-start | bytes 10616836
  17.1 5.8 %copy-start.3 = (bf16[1,256,256]{2,1,0:T(8,128)(2,1)S(1)}, bf16[1,256,256]{2,1,0:T(8,128)(2,1)}, u32[]{:S(2)}) copy-start(bf16[1,256,256]{2,1,0:T(8,128)(2,1)} %param.9) | copy-start | bytes 393220
  17.1 5.8 %copy-start.6 = (f32[256]{0:T(256)S(1)}, f32[256]{0:T(256)}, u32[]{:S(2)}) copy-start(f32[256]{0:T(256)} %param.15) | copy-start | bytes 3076
  17.2 2.3 %collective-permute-start.6 = (bf16[272,256]{1,0:T(8,128)(2,1)S(1)}, bf16[272,256]{1,0:T(8,128)(2,1)S(1)}, u32[]{:S(2)}, u32[]{:S(2)}) collective-permute-start(bf16[272,256]{1,0:T(8,128)(2,1)S(1)} %first_far.1.here), channel_id=1, source_target_pairs={{0,1},{1,0},{2,3},{3,2},{4,5},{5,4},{6,7},{7,6},{8,9},{9,8},{10,11... | collective-permute-start | bytes 417800 | tf_op jit(solution)/shard_map/ppermute | solution.py:34
  18.4 3.1 %collective-permute-start.5 = (bf16[272,256]{1,0:T(8,128)(2,1)S(1)}, bf16[272,256]{1,0:T(8,128)(2,1)S(1)}, u32[]{:S(2)}, u32[]{:S(2)}) collective-permute-start(bf16[272,256]{1,0:T(8,128)(2,1)S(1)} %first_far.1.here), channel_id=1, source_target_pairs={{0,1},{1,2},{2,3},{3,4},{4,5},{5,6},{6,7},{7,8},{8,9},{9,10},{10,1... | collective-permute-start | bytes 417800 | tf_op jit(solution)/shard_map/ppermute | solution.py:29
  18.4 4.5 %collective-permute-start.4 = (bf16[272,256]{1,0:T(8,128)(2,1)S(1)}, bf16[272,256]{1,0:T(8,128)(2,1)S(1)}, u32[]{:S(2)}, u32[]{:S(2)}) collective-permute-start(bf16[272,256]{1,0:T(8,128)(2,1)S(1)} %first_far.1.here), channel_id=1, source_target_pairs={{0,63},{1,0},{2,1},{3,2},{4,3},{5,4},{6,5},{7,6},{8,7},{9,8},{10,9... | collective-permute-start | bytes 417800 | tf_op jit(solution)/shard_map/ppermute | solution.py:29
  22.9 50.1 %copy-start.2 = (bf16[256,512]{1,0:T(8,128)(2,1)S(1)}, bf16[256,512]{1,0:T(8,128)(2,1)}, u32[]{:S(2)}) copy-start(bf16[256,512]{1,0:T(8,128)(2,1)} %down_ref.1) | copy-start | bytes 786436
  58.3 14.7 %all-to-all-start.2 = ((bf16[32,8,512]{2,1,0:T(8,128)(2,1)}), bf16[32,8,512]{2,1,0:T(8,128)(2,1)S(1)}, u32[]{:S(2)}, u32[]{:S(2)}) async-start(bf16[32,8,512]{2,1,0:T(8,128)(2,1)} %broadcast_in_dim.28), calls=%async_computation.2 | async-start | bytes 524288 | tf_op jit(solution)/shard_map/all_to_all | solution.py:197
  63.6 4.1 %collective-permute-start.7 = (f32[64,256]{1,0:T(8,128)S(1)}, f32[64,256]{1,0:T(8,128)S(1)}, u32[]{:S(2)}, u32[]{:S(2)}) collective-permute-start(f32[64,256]{1,0:T(8,128)S(1)} %get-tuple-element.29), channel_id=1, source_target_pairs={{0,1},{1,2},{2,3},{3,4},{4,5},{5,6},{6,7},{7,8},{8,9},{9,10},{10,1... | collective-permute-start | bytes 196616 | tf_op jit(solution)/shard_map/ppermute | solution.py:29

commit v11 on v8

--- a/solution.py
+++ b/solution.py
@@ -113,7 +113,7 @@
 
 
 def first_far_kernel(
-    local_ref, after, before, near_ref, weight_ref, gain_ref, parent_ref,
+    local_ref, before, after, near_ref, weight_ref, gain_ref, parent_ref,
     middle_ref, select_ref, picked_ref,
 ):
     total = convolved(local_ref[...], before[...], after[...], near_ref, weight_ref, select_ref, picked_ref)
@@ -134,16 +134,15 @@
 
 
 def second_far_kernel(
-    local_ref, after, before, near_ref, weight_ref, gain_ref, feature_ref, parent_ref,
-    cotangent_ref, next_ref,
-    fine_ref, own_ref, sent_ref, grad_ref, select_ref, picked_ref,
+    local_ref, before, after, near_ref, weight_ref, gain_ref, feature_ref, parent_ref,
+    fine_ref, own_ref, sent_ref, share_ref, select_ref, picked_ref,
 ):
     rows, chans = feature_ref.shape
     total = convolved(local_ref[...], before[:rows], after[:rows], near_ref, weight_ref, select_ref, picked_ref)
     fine = feature_ref[...].astype(jnp.float32) + settled(total, gain_ref[...])
     fine = fine.astype(fine_ref.dtype)
     fine_ref[...] = fine
-    half = cotangent_ref.shape[0]
+    half = own_ref.shape[0]
     member = membership(parent_ref[...] - lax.axis_index(SPACE) * half, 2 * half)
     sums = jnp.dot(member.astype(jnp.bfloat16), fine, preferred_element_type=jnp.float32)
 
@@ -159,9 +158,13 @@
     own_ref[:, chans:] = jnp.broadcast_to(count_own, (half, own_ref.shape[1] - chans))
     sent_ref[...] = sums[half:]
     shares = sums / jnp.concatenate([count_own, count_after], axis=0)
+    share_ref[...] = shares.astype(share_ref.dtype)
+
+
+def gradient_kernel(share_ref, cotangent_ref, next_ref, grad_ref):
     grads_in = jnp.concatenate([cotangent_ref[...], next_ref[...]], axis=0)
     grad_ref[...] = lax.dot_general(
-        shares.astype(jnp.bfloat16), grads_in, (((0,), (0,)), ((), ())), preferred_element_type=jnp.float32
+        share_ref[...], grads_in, (((0,), (0,)), ((), ())), preferred_element_type=jnp.float32
     ).astype(grad_ref.dtype)
 
 
@@ -253,28 +256,29 @@
     middle = in_vmem(
         first_far_kernel,
         bf16((rows + 16, chans)),
-        (local, after, before, near, conv_first, gain_first[None], parents),
+        (local, before, after, near, conv_first, gain_first[None], parents),
         "first_far", select_and_picked, 2 * product,
     )
-    middle, next_grad = lax.optimization_barrier((middle, next_grad))
     after, before = shifted(middle, -1), shifted(middle, 1)
     partner = from_partner(middle)
     near = in_vmem(
         second_near_kernel, near_shape, (local, middle, partner), "second_near", select, 2 * product
     )
-    fine, own, sent, local_grad = in_vmem(
+    fine, own, sent, shares = in_vmem(
         second_far_kernel,
         (
             bf16((rows, chans)),
             f32((par_rows, chans + 128)),
             f32((par_rows, chans)),
-            bf16((chans, out_chans)),
+            bf16((2 * par_rows, chans)),
         ),
         (
-            local, after, before, near, conv_second, gain_second[None], field, parents,
-            grad_in, next_grad,
+            local, before, after, near, conv_second, gain_second[None], field, parents,
         ),
         "second_far", select_and_picked, 2 * product,
+    )
+    local_grad = in_vmem(
+        gradient_kernel, bf16((chans, out_chans)), (shares, grad_in, next_grad), "gradient"
     )
     worlds_all = lax.axis_size(DP)
     parents_all = par_rows * lax.axis_size(SPACE)

time: 73.8 us -> 73.6 us (level)
  starting transfers between devices: 18 us -> 21.4 us
  blocking collectives: 31.5 us -> 29.5 us
  waiting for transfers between devices: 10.3 us -> 8.36 us
    ppermute x2, starting transfers between devices: 4.6 us -> 8.65 us  [from_partner(): return lax.ppermute(array, SPACE, [(i, i ^ 1) for i in range(length)])]
    all_to_all x2, blocking collectives: 31.5 us -> 29.5 us  [exchanged(): return lax.all_to_all(pieces, axes, 0, 0, tiled=True)]
    ppermute x6, waiting for transfers between devices: 3.82 us -> 2.41 us  [shifted(): lax.ppermute(array, SPACE, [(i, (i + by) % length) for i in range(length)])]
    pallas_call x5 -> x6, Pallas kernels: 12.2 us -> 12.4 us  [in_vmem(): pl.pallas_call(kernel, out_shape=outs, in_specs=[vmem] * len(inputs) + [p...]
  transfers between devices with their start and end apart: 9 -> 9, of which waited for: 5 -> 3; matrix products, arithmetic and copies ran while one was open for 0% -> 0% of each run, Pallas kernels for 11% -> 12%
where the time goes in v11:
time: 73.6 us; the launch traced here: 73.3 us
  blocking collectives  29.5 us (40%)
  starting transfers between devices  21.4 us (29%)
  Pallas kernels  12.4 us (17%)
  waiting for transfers between devices  8.36 us (11%)
  between operations  0.84 us (1%)
  local copies, waits for them, and re-layouts  0.78 us (1%)
    all_to_all x2, blocking collectives, exchanged(): return lax.all_to_all(pieces, axes, 0, 0, tiled=True)  29.5 us
    pallas_call x6, Pallas kernels, in_vmem(): pl.pallas_call(kernel, out_shape=outs, in_specs=[vmem] * len(inputs) + [p...  12.4 us
    ppermute x2, starting transfers between devices, from_partner(): return lax.ppermute(array, SPACE, [(i, i ^ 1) for i in range(length)])  8.65 us
    ppermute x6, starting transfers between devices, shifted(): lax.ppermute(array, SPACE, [(i, (i + by) % length) for i in range(length)])  7.38 us
    all_to_all x1, starting transfers between devices, exchanged(): return lax.all_to_all(pieces, axes, 0, 0, tiled=True)  5.35 us
    all_to_all x1, waiting for transfers between devices, exchanged(): return lax.all_to_all(pieces, axes, 0, 0, tiled=True)  5.26 us
    ppermute x6, waiting for transfers between devices, shifted(): lax.ppermute(array, SPACE, [(i, (i + by) % length) for i in range(length)])  2.41 us
  transfers between devices with their start and end apart: 9, of which 3 were waited for; matrix products, arithmetic and copies ran while one was open for 0% of the time, Pallas kernels for 12%

profile of v11, /device:TPU:1, one launch (start us, length us, event | category | flops | bytes accessed | tf_op | source)
XLA Modules:
  0.0 73.3 jit_solution(15392741896560828087)
XLA Ops:
  0.7 3.3 %collective-permute-start = (bf16[256,256]{1,0:T(8,128)(2,1)}, bf16[256,256]{1,0:T(8,128)(2,1)S(1)}, u32[]{:S(2)}, u32[]{:S(2)}) collective-permute-start(bf16[256,256]{1,0:T(8,128)(2,1)} %bitcast.11), channel_id=1, source_target_pairs={{0,1},{1,0},{2,3},{3,2},{4,5},{5,4},{6,7},{7,6},{8,9},{9,8},{10,11... | collective-permute-start | bytes 393224 | tf_op jit(solution)/shard_map/ppermute | solution.py:34
  4.0 0.5 collective-permute-start.2
  4.5 0.7 collective-permute-done.partner
  5.2 3.9 %first_near.1 = (bf16[256,6912]{1,0:T(8,128)(2,1)S(1)}, s32[256,32]{1,0:T(8,128)S(1)}) custom-call(bf16[256,256]{1,0:T(8,128)(2,1)S(1)} %collective-permute-done.partner, s32[27,1,256]{2,1,0:T(1,128)} %bitcast.22, bf16[256,256]{1,0:T(8,128)(2,1)} %bitcast.14), custom_call_target="tpu_custom_call" | custom-call | flops 1811939328 | bytes 1048576 | tf_op jit(solution)/shard_map/first_near/pallas_call | solution.py:181
  9.1 0.0 copy-start.4
  9.1 2.3 %first_far.1.here = bf16[272,256]{1,0:T(8,128)(2,1)S(1)} custom-call(s32[256,32]{1,0:T(8,128)S(1)} %get-tuple-element.15.local_ref, bf16[256,256]{1,0:T(8,128)(2,1)S(1)} %collective-permute-done.1.before, bf16[256,256]{1,0:T(8,128)(2,1)S(1)} %collective-permute-done.2.after, bf16[256,6912]{1,0:T(8,128)(2,1)S(1)} %get-tuple-element.17.near_ref, ...), custom_call_target="tpu_custom_call" | custom-call | flops 1811939328 | bytes 1048576 | tf_op jit(solution)/shard_map/first_far/pallas_call | solution.py:181
  11.4 0.0 copy-start.1
  11.4 0.0 copy-start.3
  11.5 0.0 copy-start.7
  11.5 5.3 %collective-permute-start.5 = (bf16[272,256]{1,0:T(8,128)(2,1)S(1)}, bf16[272,256]{1,0:T(8,128)(2,1)S(1)}, u32[]{:S(2)}, u32[]{:S(2)}) collective-permute-start(bf16[272,256]{1,0:T(8,128)(2,1)S(1)} %first_far.1.here), channel_id=1, source_target_pairs={{0,1},{1,0},{2,3},{3,2},{4,5},{5,4},{6,7},{7,6},{8,9},{9,8},{10,11... | collective-permute-start | bytes 417800 | tf_op jit(solution)/shard_map/ppermute | solution.py:34
  16.8 0.5 collective-permute-start.4
  17.3 4.6 %collective-permute-start.6 = (bf16[64,512]{1,0:T(8,128)(2,1)S(1)}, bf16[64,512]{1,0:T(8,128)(2,1)S(1)}, u32[]{:S(2)}, u32[]{:S(2)}) collective-permute-start(bf16[64,512]{1,0:T(8,128)(2,1)S(1)} %bitcast.16), channel_id=1, source_target_pairs={{0,63},{1,0},{2,1},{3,2},{4,3},{5,4},{6,5},{7,6},{8,7},{9,8},{10,9... | collective-permute-start | bytes 196616 | tf_op jit(solution)/shard_map/ppermute | solution.py:29
  22.0 2.1 %second_near.1.near_ref = bf16[256,6912]{1,0:T(8,128)(2,1)S(1)} custom-call(s32[256,32]{1,0:T(8,128)S(1)} %get-tuple-element.15.local_ref, bf16[272,256]{1,0:T(8,128)(2,1)S(1)} %first_far.1.here, bf16[272,256]{1,0:T(8,128)(2,1)S(1)} %collective-permute-done.5.partner), custom_call_target="tpu_custom_call" | custom-call | flops 1811939328 | bytes 1048576 | tf_op jit(solution)/shard_map/second_near/pallas_call | solution.py:181
  24.1 0.0 copy-start.2
  24.1 3.0 %second_far.1 = (bf16[256,256]{1,0:T(8,128)(2,1)}, f32[64,384]{1,0:T(8,128)S(1)}, f32[64,256]{1,0:T(8,128)S(1)}, bf16[128,256]{1,0:T(8,128)(2,1)S(1)}) custom-call(s32[256,32]{1,0:T(8,128)S(1)} %get-tuple-element.15.local_ref, bf16[272,256]{1,0:T(8,128)(2,1)S(1)} %collective-permute-done.3.before, bf16[272,256]{1,0:T(8,128)(2,1)S(1)} %collective-permute-done.4.after, ...), custom_call_target="tpu_custom_call" | custom-call | flops 1811939328 | bytes 1048576 | tf_op jit(solution)/shard_map/second_far/pallas_call | solution.py:181
  27.1 0.2 gradient.1
  27.3 13.9 %all_to_all.15 = bf16[32,8,512]{2,1,0:T(8,128)(2,1)S(1)} all-to-all(bf16[32,8,512]{2,1,0:T(8,128)(2,1)S(1)} %bitcast.9), channel_id=1, replica_groups=mesh['y'=4,'z'=8,'x'=4,'core'=2] {'y','x','core'}, dimensions={0} | all-to-all | bytes 524288 | tf_op jit(solution)/shard_map/all_to_all | solution.py:194
  41.4 15.5 %all_to_all.16 = f32[8,8,512]{2,1,0:T(8,128)S(1)} all-to-all(f32[8,8,512]{2,1,0:T(8,128)S(1)} %broadcast_in_dim.27), channel_id=1, replica_groups=mesh['y'=4,'z'=8,'x'=4,'core'=2] {'z'}, dimensions={0} | all-to-all | bytes 262144 | tf_op jit(solution)/shard_map/all_to_all | solution.py:194
  56.9 0.7 broadcast_in_dim.28
  57.6 5.4 %all-to-all-start.2 = ((bf16[32,8,512]{2,1,0:T(8,128)(2,1)}), bf16[32,8,512]{2,1,0:T(8,128)(2,1)S(1)}, u32[]{:S(2)}, u32[]{:S(2)}) async-start(bf16[32,8,512]{2,1,0:T(8,128)(2,1)} %broadcast_in_dim.28), calls=%async_computation.2 | async-start | bytes 524288 | tf_op jit(solution)/shard_map/all_to_all | solution.py:194
  63.0 1.7 %collective-permute-start.7 = (f32[64,256]{1,0:T(8,128)S(1)}, f32[64,256]{1,0:T(8,128)S(1)}, u32[]{:S(2)}, u32[]{:S(2)}) collective-permute-start(f32[64,256]{1,0:T(8,128)S(1)} %get-tuple-element.23), channel_id=1, source_target_pairs={{0,1},{1,2},{2,3},{3,4},{4,5},{5,6},{6,7},{7,8},{8,9},{9,10},{10,1... | collective-permute-start | bytes 196616 | tf_op jit(solution)/shard_map/ppermute | solution.py:29
  64.7 2.4 %collective-permute-done.7.moved_ref = f32[64,256]{1,0:T(8,128)S(1)} collective-permute-done((f32[64,256]{1,0:T(8,128)S(1)}, f32[64,256]{1,0:T(8,128)S(1)}, u32[]{:S(2)}, u32[]{:S(2)}) %collective-permute-start.7) | collective-permute-done | bytes 65568 | tf_op jit(solution)/shard_map/ppermute | solution.py:29
  67.1 5.3 %all-to-all-done.2 = bf16[32,8,512]{2,1,0:T(8,128)(2,1)S(1)} async-done(((bf16[32,8,512]{2,1,0:T(8,128)(2,1)}), bf16[32,8,512]{2,1,0:T(8,128)(2,1)S(1)}, u32[]{:S(2)}, u32[]{:S(2)}) %all-to-all-start.2) | async-done | bytes 262176 | tf_op jit(solution)/shard_map/all_to_all | solution.py:194
  72.4 0.9 %coarse_and_grad.1 = (bf16[64,512]{1,0:T(8,128)(2,1)}, f32[256,512]{1,0:T(8,128)}) custom-call(f32[64,384]{1,0:T(8,128)S(1)} %get-tuple-element.19.own_ref, f32[64,256]{1,0:T(8,128)S(1)} %collective-permute-done.7.moved_ref, bf16[256,512]{1,0:T(8,128)(2,1)S(1)} %copy-done.2, bf16[256,512]{1,0:T(8,128)(2,1)S(1)} %bitcast.10), custom_call_target="tpu_custom_call" | custom-call | bytes 1048576 | tf_op jit(solution)/shard_map/coarse_and_grad/pallas_call | solution.py:181
  (23 shorter events, 0.1 us)
Async XLA Ops:
  0.6 8.5 %copy-start.6 = (f32[256]{0:T(256)S(1)}, f32[256]{0:T(256)}, u32[]{:S(2)}) copy-start(f32[256]{0:T(256)} %param.14) | copy-start | bytes 3076
  0.6 8.5 %copy-start.5 = (s32[1,256]{1,0:T(1,128)S(1)}, s32[1,256]{1,0:T(1,128)}, u32[]{:S(2)}) copy-start(s32[1,256]{1,0:T(1,128)} %parent_ref.3) | copy-start | bytes 3076
  0.7 8.5 %copy-start = (bf16[27,256,256]{2,1,0:T(8,128)(2,1)S(1)}, bf16[27,256,256]{2,1,0:T(8,128)(2,1)}, u32[]{:S(2)}) copy-start(bf16[27,256,256]{2,1,0:T(8,128)(2,1)} %weight_ref.2) | copy-start | bytes 10616836
  0.7 4.5 %collective-permute-start = (bf16[256,256]{1,0:T(8,128)(2,1)}, bf16[256,256]{1,0:T(8,128)(2,1)S(1)}, u32[]{:S(2)}, u32[]{:S(2)}) collective-permute-start(bf16[256,256]{1,0:T(8,128)(2,1)} %bitcast.11), channel_id=1, source_target_pairs={{0,1},{1,0},{2,3},{3,2},{4,5},{5,4},{6,7},{7,6},{8,9},{9,8},{10,11... | collective-permute-start | bytes 393224 | tf_op jit(solution)/shard_map/ppermute | solution.py:34
  4.0 5.1 %collective-permute-start.1 = (bf16[256,256]{1,0:T(8,128)(2,1)}, bf16[256,256]{1,0:T(8,128)(2,1)S(1)}, u32[]{:S(2)}, u32[]{:S(2)}) collective-permute-start(bf16[256,256]{1,0:T(8,128)(2,1)} %bitcast.12), channel_id=1, source_target_pairs={{0,1},{1,2},{2,3},{3,4},{4,5},{5,6},{6,7},{7,8},{8,9},{9,10},{10,1... | collective-permute-start | bytes 393224 | tf_op jit(solution)/shard_map/ppermute | solution.py:29
  4.0 5.1 %collective-permute-start.2 = (bf16[256,256]{1,0:T(8,128)(2,1)}, bf16[256,256]{1,0:T(8,128)(2,1)S(1)}, u32[]{:S(2)}, u32[]{:S(2)}) collective-permute-start(bf16[256,256]{1,0:T(8,128)(2,1)} %bitcast.13), channel_id=1, source_target_pairs={{0,63},{1,0},{2,1},{3,2},{4,3},{5,4},{6,5},{7,6},{8,7},{9,8},{10,9... | collective-permute-start | bytes 393224 | tf_op jit(solution)/shard_map/ppermute | solution.py:29
  9.1 8.2 %copy-start.4 = (bf16[1,64,512]{2,1,0:T(8,128)(2,1)S(1)}, bf16[1,64,512]{2,1,0:T(8,128)(2,1)}, u32[]{:S(2)}) copy-start(bf16[1,64,512]{2,1,0:T(8,128)(2,1)} %param.17) | copy-start | bytes 196612
  11.4 12.6 %copy-start.1 = (bf16[27,256,256]{2,1,0:T(8,128)(2,1)S(1)}, bf16[27,256,256]{2,1,0:T(8,128)(2,1)}, u32[]{:S(2)}) copy-start(bf16[27,256,256]{2,1,0:T(8,128)(2,1)} %weight_ref.3) | copy-start | bytes 10616836
  11.4 12.6 %copy-start.3 = (bf16[1,256,256]{2,1,0:T(8,128)(2,1)S(1)}, bf16[1,256,256]{2,1,0:T(8,128)(2,1)}, u32[]{:S(2)}) copy-start(bf16[1,256,256]{2,1,0:T(8,128)(2,1)} %param.9) | copy-start | bytes 393220
  11.5 12.6 %copy-start.7 = (f32[256]{0:T(256)S(1)}, f32[256]{0:T(256)}, u32[]{:S(2)}) copy-start(f32[256]{0:T(256)} %param.15) | copy-start | bytes 3076
  11.5 10.5 %collective-permute-start.5 = (bf16[272,256]{1,0:T(8,128)(2,1)S(1)}, bf16[272,256]{1,0:T(8,128)(2,1)S(1)}, u32[]{:S(2)}, u32[]{:S(2)}) collective-permute-start(bf16[272,256]{1,0:T(8,128)(2,1)S(1)} %first_far.1.here), channel_id=1, source_target_pairs={{0,1},{1,0},{2,3},{3,2},{4,5},{5,4},{6,7},{7,6},{8,9},{9,8},{10,11... | collective-permute-start | bytes 417800 | tf_op jit(solution)/shard_map/ppermute | solution.py:34
  16.8 7.2 %collective-permute-start.3 = (bf16[272,256]{1,0:T(8,128)(2,1)S(1)}, bf16[272,256]{1,0:T(8,128)(2,1)S(1)}, u32[]{:S(2)}, u32[]{:S(2)}) collective-permute-start(bf16[272,256]{1,0:T(8,128)(2,1)S(1)} %first_far.1.here), channel_id=1, source_target_pairs={{0,1},{1,2},{2,3},{3,4},{4,5},{5,6},{6,7},{7,8},{8,9},{9,10},{10,1... | collective-permute-start | bytes 417800 | tf_op jit(solution)/shard_map/ppermute | solution.py:29
  16.8 7.2 %collective-permute-start.4 = (bf16[272,256]{1,0:T(8,128)(2,1)S(1)}, bf16[272,256]{1,0:T(8,128)(2,1)S(1)}, u32[]{:S(2)}, u32[]{:S(2)}) collective-permute-start(bf16[272,256]{1,0:T(8,128)(2,1)S(1)} %first_far.1.here), channel_id=1, source_target_pairs={{0,63},{1,0},{2,1},{3,2},{4,3},{5,4},{6,5},{7,6},{8,7},{9,8},{10,9... | collective-permute-start | bytes 417800 | tf_op jit(solution)/shard_map/ppermute | solution.py:29
  17.3 9.8 %collective-permute-start.6 = (bf16[64,512]{1,0:T(8,128)(2,1)S(1)}, bf16[64,512]{1,0:T(8,128)(2,1)S(1)}, u32[]{:S(2)}, u32[]{:S(2)}) collective-permute-start(bf16[64,512]{1,0:T(8,128)(2,1)S(1)} %bitcast.16), channel_id=1, source_target_pairs={{0,63},{1,0},{2,1},{3,2},{4,3},{5,4},{6,5},{7,6},{8,7},{9,8},{10,9... | collective-permute-start | bytes 196616 | tf_op jit(solution)/shard_map/ppermute | solution.py:29
  24.1 48.3 %copy-start.2 = (bf16[256,512]{1,0:T(8,128)(2,1)S(1)}, bf16[256,512]{1,0:T(8,128)(2,1)}, u32[]{:S(2)}) copy-start(bf16[256,512]{1,0:T(8,128)(2,1)} %down_ref.1) | copy-start | bytes 786436
  57.6 14.7 %all-to-all-start.2 = ((bf16[32,8,512]{2,1,0:T(8,128)(2,1)}), bf16[32,8,512]{2,1,0:T(8,128)(2,1)S(1)}, u32[]{:S(2)}, u32[]{:S(2)}) async-start(bf16[32,8,512]{2,1,0:T(8,128)(2,1)} %broadcast_in_dim.28), calls=%async_computation.2 | async-start | bytes 524288 | tf_op jit(solution)/shard_map/all_to_all | solution.py:194
  63.0 4.1 %collective-permute-start.7 = (f32[64,256]{1,0:T(8,128)S(1)}, f32[64,256]{1,0:T(8,128)S(1)}, u32[]{:S(2)}, u32[]{:S(2)}) collective-permute-start(f32[64,256]{1,0:T(8,128)S(1)} %get-tuple-element.23), channel_id=1, source_target_pairs={{0,1},{1,2},{2,3},{3,4},{4,5},{5,6},{6,7},{7,8},{8,9},{9,10},{10,1... | collective-permute-start | bytes 196616 | tf_op jit(solution)/shard_map/ppermute | solution.py:29

commit v12 on v11

--- a/solution.py
+++ b/solution.py
@@ -13,7 +13,7 @@
 DP = "y"
 SPACE = ("z", "x", "core")
 PLANE = ("y", "x", "core")
-GROUP = 3
+GROUP = 9
 VMEM_BYTES = 32 << 20
 PAR_ROWS = 64
 COST_BYTES = 1 << 20

time: 73.6 us -> 73.6 us (level)
  no operation moved by 1% of the time
where the time goes in v12:
time: 73.6 us; the launch traced here: 73.3 us
  blocking collectives  29.5 us (40%)
  starting transfers between devices  21.4 us (29%)
  Pallas kernels  12.4 us (17%)
  waiting for transfers between devices  8.36 us (11%)
  between operations  0.83 us (1%)
  local copies, waits for them, and re-layouts  0.78 us (1%)
    all_to_all x2, blocking collectives, exchanged(): return lax.all_to_all(pieces, axes, 0, 0, tiled=True)  29.5 us
    pallas_call x6, Pallas kernels, in_vmem(): pl.pallas_call(kernel, out_shape=outs, in_specs=[vmem] * len(inputs) + [p...  12.4 us
    ppermute x2, starting transfers between devices, from_partner(): return lax.ppermute(array, SPACE, [(i, i ^ 1) for i in range(length)])  8.64 us
    ppermute x6, starting transfers between devices, shifted(): lax.ppermute(array, SPACE, [(i, (i + by) % length) for i in range(length)])  7.38 us
    all_to_all x1, starting transfers between devices, exchanged(): return lax.all_to_all(pieces, axes, 0, 0, tiled=True)  5.35 us
    all_to_all x1, waiting for transfers between devices, exchanged(): return lax.all_to_all(pieces, axes, 0, 0, tiled=True)  5.26 us
    ppermute x6, waiting for transfers between devices, shifted(): lax.ppermute(array, SPACE, [(i, (i + by) % length) for i in range(length)])  2.41 us
  transfers between devices with their start and end apart: 9, of which 3 were waited for; matrix products, arithmetic and copies ran while one was open for 0% of the time, Pallas kernels for 12%

profile of v12, /device:TPU:1, one launch (start us, length us, event | category | flops | bytes accessed | tf_op | source)
XLA Modules:
  0.0 73.3 jit_solution(14815778542966292910)
XLA Ops:
  0.7 3.3 %collective-permute-start = (bf16[256,256]{1,0:T(8,128)(2,1)}, bf16[256,256]{1,0:T(8,128)(2,1)S(1)}, u32[]{:S(2)}, u32[]{:S(2)}) collective-permute-start(bf16[256,256]{1,0:T(8,128)(2,1)} %bitcast.11), channel_id=1, source_target_pairs={{0,1},{1,0},{2,3},{3,2},{4,5},{5,4},{6,7},{7,6},{8,9},{9,8},{10,11... | collective-permute-start | bytes 393224 | tf_op jit(solution)/shard_map/ppermute | solution.py:34
  4.0 0.5 collective-permute-start.2
  4.5 0.7 collective-permute-done.partner
  5.2 3.9 %first_near.1 = (bf16[256,6912]{1,0:T(8,128)(2,1)S(1)}, s32[256,32]{1,0:T(8,128)S(1)}) custom-call(bf16[256,256]{1,0:T(8,128)(2,1)S(1)} %collective-permute-done.partner, s32[27,1,256]{2,1,0:T(1,128)} %bitcast.22, bf16[256,256]{1,0:T(8,128)(2,1)} %bitcast.14), custom_call_target="tpu_custom_call" | custom-call | flops 1811939328 | bytes 1048576 | tf_op jit(solution)/shard_map/first_near/pallas_call | solution.py:181
  9.1 0.0 copy-start.4
  9.1 2.3 %first_far.1.here = bf16[272,256]{1,0:T(8,128)(2,1)S(1)} custom-call(s32[256,32]{1,0:T(8,128)S(1)} %get-tuple-element.15.local_ref, bf16[256,256]{1,0:T(8,128)(2,1)S(1)} %collective-permute-done.1.before, bf16[256,256]{1,0:T(8,128)(2,1)S(1)} %collective-permute-done.2.after, bf16[256,6912]{1,0:T(8,128)(2,1)S(1)} %get-tuple-element.17.near_ref, ...), custom_call_target="tpu_custom_call" | custom-call | flops 1811939328 | bytes 1048576 | tf_op jit(solution)/shard_map/first_far/pallas_call | solution.py:181
  11.4 0.0 copy-start.1
  11.4 0.0 copy-start.3
  11.5 0.0 copy-start.7
  11.5 5.3 %collective-permute-start.5 = (bf16[272,256]{1,0:T(8,128)(2,1)S(1)}, bf16[272,256]{1,0:T(8,128)(2,1)S(1)}, u32[]{:S(2)}, u32[]{:S(2)}) collective-permute-start(bf16[272,256]{1,0:T(8,128)(2,1)S(1)} %first_far.1.here), channel_id=1, source_target_pairs={{0,1},{1,0},{2,3},{3,2},{4,5},{5,4},{6,7},{7,6},{8,9},{9,8},{10,11... | collective-permute-start | bytes 417800 | tf_op jit(solution)/shard_map/ppermute | solution.py:34
  16.8 0.5 collective-permute-start.4
  17.3 4.6 %collective-permute-start.6 = (bf16[64,512]{1,0:T(8,128)(2,1)S(1)}, bf16[64,512]{1,0:T(8,128)(2,1)S(1)}, u32[]{:S(2)}, u32[]{:S(2)}) collective-permute-start(bf16[64,512]{1,0:T(8,128)(2,1)S(1)} %bitcast.16), channel_id=1, source_target_pairs={{0,63},{1,0},{2,1},{3,2},{4,3},{5,4},{6,5},{7,6},{8,7},{9,8},{10,9... | collective-permute-start | bytes 196616 | tf_op jit(solution)/shard_map/ppermute | solution.py:29
  22.0 2.1 %second_near.1.near_ref = bf16[256,6912]{1,0:T(8,128)(2,1)S(1)} custom-call(s32[256,32]{1,0:T(8,128)S(1)} %get-tuple-element.15.local_ref, bf16[272,256]{1,0:T(8,128)(2,1)S(1)} %first_far.1.here, bf16[272,256]{1,0:T(8,128)(2,1)S(1)} %collective-permute-done.5.partner), custom_call_target="tpu_custom_call" | custom-call | flops 1811939328 | bytes 1048576 | tf_op jit(solution)/shard_map/second_near/pallas_call | solution.py:181
  24.1 0.0 copy-start.2
  24.1 3.0 %second_far.1 = (bf16[256,256]{1,0:T(8,128)(2,1)}, f32[64,384]{1,0:T(8,128)S(1)}, f32[64,256]{1,0:T(8,128)S(1)}, bf16[128,256]{1,0:T(8,128)(2,1)S(1)}) custom-call(s32[256,32]{1,0:T(8,128)S(1)} %get-tuple-element.15.local_ref, bf16[272,256]{1,0:T(8,128)(2,1)S(1)} %collective-permute-done.3.before, bf16[272,256]{1,0:T(8,128)(2,1)S(1)} %collective-permute-done.4.after, ...), custom_call_target="tpu_custom_call" | custom-call | flops 1811939328 | bytes 1048576 | tf_op jit(solution)/shard_map/second_far/pallas_call | solution.py:181
  27.1 0.2 gradient.1
  27.3 13.9 %all_to_all.15 = bf16[32,8,512]{2,1,0:T(8,128)(2,1)S(1)} all-to-all(bf16[32,8,512]{2,1,0:T(8,128)(2,1)S(1)} %bitcast.9), channel_id=1, replica_groups=mesh['y'=4,'z'=8,'x'=4,'core'=2] {'y','x','core'}, dimensions={0} | all-to-all | bytes 524288 | tf_op jit(solution)/shard_map/all_to_all | solution.py:194
  41.4 15.5 %all_to_all.16 = f32[8,8,512]{2,1,0:T(8,128)S(1)} all-to-all(f32[8,8,512]{2,1,0:T(8,128)S(1)} %broadcast_in_dim.27), channel_id=1, replica_groups=mesh['y'=4,'z'=8,'x'=4,'core'=2] {'z'}, dimensions={0} | all-to-all | bytes 262144 | tf_op jit(solution)/shard_map/all_to_all | solution.py:194
  56.9 0.7 broadcast_in_dim.28
  57.7 5.4 %all-to-all-start.2 = ((bf16[32,8,512]{2,1,0:T(8,128)(2,1)}), bf16[32,8,512]{2,1,0:T(8,128)(2,1)S(1)}, u32[]{:S(2)}, u32[]{:S(2)}) async-start(bf16[32,8,512]{2,1,0:T(8,128)(2,1)} %broadcast_in_dim.28), calls=%async_computation.2 | async-start | bytes 524288 | tf_op jit(solution)/shard_map/all_to_all | solution.py:194
  63.0 1.7 %collective-permute-start.7 = (f32[64,256]{1,0:T(8,128)S(1)}, f32[64,256]{1,0:T(8,128)S(1)}, u32[]{:S(2)}, u32[]{:S(2)}) collective-permute-start(f32[64,256]{1,0:T(8,128)S(1)} %get-tuple-element.23), channel_id=1, source_target_pairs={{0,1},{1,2},{2,3},{3,4},{4,5},{5,6},{6,7},{7,8},{8,9},{9,10},{10,1... | collective-permute-start | bytes 196616 | tf_op jit(solution)/shard_map/ppermute | solution.py:29
  64.7 2.4 %collective-permute-done.7.moved_ref = f32[64,256]{1,0:T(8,128)S(1)} collective-permute-done((f32[64,256]{1,0:T(8,128)S(1)}, f32[64,256]{1,0:T(8,128)S(1)}, u32[]{:S(2)}, u32[]{:S(2)}) %collective-permute-start.7) | collective-permute-done | bytes 65568 | tf_op jit(solution)/shard_map/ppermute | solution.py:29
  67.1 5.3 %all-to-all-done.2 = bf16[32,8,512]{2,1,0:T(8,128)(2,1)S(1)} async-done(((bf16[32,8,512]{2,1,0:T(8,128)(2,1)}), bf16[32,8,512]{2,1,0:T(8,128)(2,1)S(1)}, u32[]{:S(2)}, u32[]{:S(2)}) %all-to-all-start.2) | async-done | bytes 262176 | tf_op jit(solution)/shard_map/all_to_all | solution.py:194
  72.4 0.9 %coarse_and_grad.1 = (bf16[64,512]{1,0:T(8,128)(2,1)}, f32[256,512]{1,0:T(8,128)}) custom-call(f32[64,384]{1,0:T(8,128)S(1)} %get-tuple-element.19.own_ref, f32[64,256]{1,0:T(8,128)S(1)} %collective-permute-done.7.moved_ref, bf16[256,512]{1,0:T(8,128)(2,1)S(1)} %copy-done.2, bf16[256,512]{1,0:T(8,128)(2,1)S(1)} %bitcast.10), custom_call_target="tpu_custom_call" | custom-call | bytes 1048576 | tf_op jit(solution)/shard_map/coarse_and_grad/pallas_call | solution.py:181
  (23 shorter events, 0.1 us)
Async XLA Ops:
  0.6 8.5 %copy-start.6 = (f32[256]{0:T(256)S(1)}, f32[256]{0:T(256)}, u32[]{:S(2)}) copy-start(f32[256]{0:T(256)} %param.14) | copy-start | bytes 3076
  0.6 8.5 %copy-start.5 = (s32[1,256]{1,0:T(1,128)S(1)}, s32[1,256]{1,0:T(1,128)}, u32[]{:S(2)}) copy-start(s32[1,256]{1,0:T(1,128)} %parent_ref.3) | copy-start | bytes 3076
  0.7 8.5 %copy-start = (bf16[27,256,256]{2,1,0:T(8,128)(2,1)S(1)}, bf16[27,256,256]{2,1,0:T(8,128)(2,1)}, u32[]{:S(2)}) copy-start(bf16[27,256,256]{2,1,0:T(8,128)(2,1)} %weight_ref.2) | copy-start | bytes 10616836
  0.7 4.5 %collective-permute-start = (bf16[256,256]{1,0:T(8,128)(2,1)}, bf16[256,256]{1,0:T(8,128)(2,1)S(1)}, u32[]{:S(2)}, u32[]{:S(2)}) collective-permute-start(bf16[256,256]{1,0:T(8,128)(2,1)} %bitcast.11), channel_id=1, source_target_pairs={{0,1},{1,0},{2,3},{3,2},{4,5},{5,4},{6,7},{7,6},{8,9},{9,8},{10,11... | collective-permute-start | bytes 393224 | tf_op jit(solution)/shard_map/ppermute | solution.py:34
  4.0 5.1 %collective-permute-start.1 = (bf16[256,256]{1,0:T(8,128)(2,1)}, bf16[256,256]{1,0:T(8,128)(2,1)S(1)}, u32[]{:S(2)}, u32[]{:S(2)}) collective-permute-start(bf16[256,256]{1,0:T(8,128)(2,1)} %bitcast.12), channel_id=1, source_target_pairs={{0,1},{1,2},{2,3},{3,4},{4,5},{5,6},{6,7},{7,8},{8,9},{9,10},{10,1... | collective-permute-start | bytes 393224 | tf_op jit(solution)/shard_map/ppermute | solution.py:29
  4.0 5.1 %collective-permute-start.2 = (bf16[256,256]{1,0:T(8,128)(2,1)}, bf16[256,256]{1,0:T(8,128)(2,1)S(1)}, u32[]{:S(2)}, u32[]{:S(2)}) collective-permute-start(bf16[256,256]{1,0:T(8,128)(2,1)} %bitcast.13), channel_id=1, source_target_pairs={{0,63},{1,0},{2,1},{3,2},{4,3},{5,4},{6,5},{7,6},{8,7},{9,8},{10,9... | collective-permute-start | bytes 393224 | tf_op jit(solution)/shard_map/ppermute | solution.py:29
  9.1 8.2 %copy-start.4 = (bf16[1,64,512]{2,1,0:T(8,128)(2,1)S(1)}, bf16[1,64,512]{2,1,0:T(8,128)(2,1)}, u32[]{:S(2)}) copy-start(bf16[1,64,512]{2,1,0:T(8,128)(2,1)} %param.17) | copy-start | bytes 196612
  11.4 12.6 %copy-start.1 = (bf16[27,256,256]{2,1,0:T(8,128)(2,1)S(1)}, bf16[27,256,256]{2,1,0:T(8,128)(2,1)}, u32[]{:S(2)}) copy-start(bf16[27,256,256]{2,1,0:T(8,128)(2,1)} %weight_ref.3) | copy-start | bytes 10616836
  11.4 12.6 %copy-start.3 = (bf16[1,256,256]{2,1,0:T(8,128)(2,1)S(1)}, bf16[1,256,256]{2,1,0:T(8,128)(2,1)}, u32[]{:S(2)}) copy-start(bf16[1,256,256]{2,1,0:T(8,128)(2,1)} %param.9) | copy-start | bytes 393220
  11.5 12.6 %copy-start.7 = (f32[256]{0:T(256)S(1)}, f32[256]{0:T(256)}, u32[]{:S(2)}) copy-start(f32[256]{0:T(256)} %param.15) | copy-start | bytes 3076
  11.5 10.5 %collective-permute-start.5 = (bf16[272,256]{1,0:T(8,128)(2,1)S(1)}, bf16[272,256]{1,0:T(8,128)(2,1)S(1)}, u32[]{:S(2)}, u32[]{:S(2)}) collective-permute-start(bf16[272,256]{1,0:T(8,128)(2,1)S(1)} %first_far.1.here), channel_id=1, source_target_pairs={{0,1},{1,0},{2,3},{3,2},{4,5},{5,4},{6,7},{7,6},{8,9},{9,8},{10,11... | collective-permute-start | bytes 417800 | tf_op jit(solution)/shard_map/ppermute | solution.py:34
  16.8 7.2 %collective-permute-start.3 = (bf16[272,256]{1,0:T(8,128)(2,1)S(1)}, bf16[272,256]{1,0:T(8,128)(2,1)S(1)}, u32[]{:S(2)}, u32[]{:S(2)}) collective-permute-start(bf16[272,256]{1,0:T(8,128)(2,1)S(1)} %first_far.1.here), channel_id=1, source_target_pairs={{0,1},{1,2},{2,3},{3,4},{4,5},{5,6},{6,7},{7,8},{8,9},{9,10},{10,1... | collective-permute-start | bytes 417800 | tf_op jit(solution)/shard_map/ppermute | solution.py:29
  16.8 7.3 %collective-permute-start.4 = (bf16[272,256]{1,0:T(8,128)(2,1)S(1)}, bf16[272,256]{1,0:T(8,128)(2,1)S(1)}, u32[]{:S(2)}, u32[]{:S(2)}) collective-permute-start(bf16[272,256]{1,0:T(8,128)(2,1)S(1)} %first_far.1.here), channel_id=1, source_target_pairs={{0,63},{1,0},{2,1},{3,2},{4,3},{5,4},{6,5},{7,6},{8,7},{9,8},{10,9... | collective-permute-start | bytes 417800 | tf_op jit(solution)/shard_map/ppermute | solution.py:29
  17.3 9.8 %collective-permute-start.6 = (bf16[64,512]{1,0:T(8,128)(2,1)S(1)}, bf16[64,512]{1,0:T(8,128)(2,1)S(1)}, u32[]{:S(2)}, u32[]{:S(2)}) collective-permute-start(bf16[64,512]{1,0:T(8,128)(2,1)S(1)} %bitcast.16), channel_id=1, source_target_pairs={{0,63},{1,0},{2,1},{3,2},{4,3},{5,4},{6,5},{7,6},{8,7},{9,8},{10,9... | collective-permute-start | bytes 196616 | tf_op jit(solution)/shard_map/ppermute | solution.py:29
  24.1 48.3 %copy-start.2 = (bf16[256,512]{1,0:T(8,128)(2,1)S(1)}, bf16[256,512]{1,0:T(8,128)(2,1)}, u32[]{:S(2)}) copy-start(bf16[256,512]{1,0:T(8,128)(2,1)} %down_ref.1) | copy-start | bytes 786436
  57.7 14.7 %all-to-all-start.2 = ((bf16[32,8,512]{2,1,0:T(8,128)(2,1)}), bf16[32,8,512]{2,1,0:T(8,128)(2,1)S(1)}, u32[]{:S(2)}, u32[]{:S(2)}) async-start(bf16[32,8,512]{2,1,0:T(8,128)(2,1)} %broadcast_in_dim.28), calls=%async_computation.2 | async-start | bytes 524288 | tf_op jit(solution)/shard_map/all_to_all | solution.py:194
  63.0 4.1 %collective-permute-start.7 = (f32[64,256]{1,0:T(8,128)S(1)}, f32[64,256]{1,0:T(8,128)S(1)}, u32[]{:S(2)}, u32[]{:S(2)}) collective-permute-start(f32[64,256]{1,0:T(8,128)S(1)} %get-tuple-element.23), channel_id=1, source_target_pairs={{0,1},{1,2},{2,3},{3,4},{4,5},{5,6},{6,7},{7,8},{8,9},{9,10},{10,1... | collective-permute-start | bytes 196616 | tf_op jit(solution)/shard_map/ppermute | solution.py:29

commit v13 on v12

--- a/solution.py
+++ b/solution.py
@@ -135,13 +135,15 @@
 
 def second_far_kernel(
     local_ref, before, after, near_ref, weight_ref, gain_ref, feature_ref, parent_ref,
-    fine_ref, own_ref, sent_ref, share_ref, select_ref, picked_ref,
+    fine_hbm, own_ref, sent_ref, share_ref, select_ref, picked_ref, fine_ref, fine_sem,
 ):
     rows, chans = feature_ref.shape
     total = convolved(local_ref[...], before[:rows], after[:rows], near_ref, weight_ref, select_ref, picked_ref)
     fine = feature_ref[...].astype(jnp.float32) + settled(total, gain_ref[...])
     fine = fine.astype(fine_ref.dtype)
     fine_ref[...] = fine
+    copy = pltpu.make_async_copy(fine_ref, fine_hbm, fine_sem)
+    copy.start()
     half = own_ref.shape[0]
     member = membership(parent_ref[...] - lax.axis_index(SPACE) * half, 2 * half)
     sums = jnp.dot(member.astype(jnp.bfloat16), fine, preferred_element_type=jnp.float32)
@@ -159,6 +161,7 @@
     sent_ref[...] = sums[half:]
     shares = sums / jnp.concatenate([count_own, count_after], axis=0)
     share_ref[...] = shares.astype(share_ref.dtype)
+    copy.wait()
 
 
 def gradient_kernel(share_ref, cotangent_ref, next_ref, grad_ref):
@@ -176,13 +179,15 @@
     coarse_ref[...] = jnp.dot(pooled, down_ref[...], preferred_element_type=jnp.float32).astype(coarse_ref.dtype)
 
 
-def in_vmem(kernel, outs, inputs, name, scratch=(), flops=0, from_hbm=()):
+def in_vmem(kernel, outs, inputs, name, scratch=(), flops=0, from_hbm=(), to_hbm=0):
     vmem = pl.BlockSpec(memory_space=pltpu.VMEM)
     return pl.pallas_call(
         kernel,
         out_shape=outs,
         in_specs=[vmem] * len(inputs) + [pl.BlockSpec(memory_space=pltpu.HBM)] * len(from_hbm),
-        out_specs=jax.tree.map(lambda _: vmem, outs),
+        out_specs=([pl.BlockSpec(memory_space=pl.ANY)] * to_hbm + [vmem] * (len(outs) - to_hbm))
+        if isinstance(outs, tuple)
+        else vmem,
         scratch_shapes=scratch,
         compiler_params=pltpu.CompilerParams(vmem_limit_bytes=VMEM_BYTES),
         cost_estimate=pl.CostEstimate(flops=flops, bytes_accessed=COST_BYTES, transcendentals=0),
@@ -275,7 +280,10 @@
         (
             local, before, after, near, conv_second, gain_second[None], field, parents,
         ),
-        "second_far", select_and_picked, 2 * product,
+        "second_far",
+        select_and_picked + [pltpu.VMEM((rows, chans), jnp.bfloat16), pltpu.SemaphoreType.DMA],
+        2 * product,
+        to_hbm=1,
     )
     local_grad = in_vmem(
         gradient_kernel, bf16((chans, out_chans)), (shares, grad_in, next_grad), "gradient"

time: 73.6 us -> 73.6 us (level)
  no operation moved by 1% of the time
where the time goes in v13:
time: 73.6 us; the launch traced here: 73.3 us
  blocking collectives  29.5 us (40%)
  starting transfers between devices  21.4 us (29%)
  Pallas kernels  12.4 us (17%)
  waiting for transfers between devices  8.36 us (11%)
  between operations  0.85 us (1%)
  local copies, waits for them, and re-layouts  0.78 us (1%)
    all_to_all x2, blocking collectives, exchanged(): return lax.all_to_all(pieces, axes, 0, 0, tiled=True)  29.5 us
    pallas_call x6, Pallas kernels, in_vmem(): pl.pallas_call(kernel, out_shape=outs, in_specs=[vmem] * len(inputs) + [p...  12.4 us
    ppermute x2, starting transfers between devices, from_partner(): return lax.ppermute(array, SPACE, [(i, i ^ 1) for i in range(length)])  8.64 us
    ppermute x6, starting transfers between devices, shifted(): lax.ppermute(array, SPACE, [(i, (i + by) % length) for i in range(length)])  7.38 us
    all_to_all x1, starting transfers between devices, exchanged(): return lax.all_to_all(pieces, axes, 0, 0, tiled=True)  5.35 us
    all_to_all x1, waiting for transfers between devices, exchanged(): return lax.all_to_all(pieces, axes, 0, 0, tiled=True)  5.26 us
    ppermute x6, waiting for transfers between devices, shifted(): lax.ppermute(array, SPACE, [(i, (i + by) % length) for i in range(length)])  2.41 us
  transfers between devices with their start and end apart: 9, of which 3 were waited for; matrix products, arithmetic and copies ran while one was open for 0% of the time, Pallas kernels for 12%

profile of v13, /device:TPU:1, one launch (start us, length us, event | category | flops | bytes accessed | tf_op | source)
XLA Modules:
  0.0 73.3 jit_solution(2926975186671830361)
XLA Ops:
  0.7 3.3 %collective-permute-start = (bf16[256,256]{1,0:T(8,128)(2,1)}, bf16[256,256]{1,0:T(8,128)(2,1)S(1)}, u32[]{:S(2)}, u32[]{:S(2)}) collective-permute-start(bf16[256,256]{1,0:T(8,128)(2,1)} %bitcast.11), channel_id=1, source_target_pairs={{0,1},{1,0},{2,3},{3,2},{4,5},{5,4},{6,7},{7,6},{8,9},{9,8},{10,11... | collective-permute-start | bytes 393224 | tf_op jit(solution)/shard_map/ppermute | solution.py:34
  4.0 0.5 collective-permute-start.2
  4.5 0.7 collective-permute-done.partner
  5.2 3.9 %first_near.1 = (bf16[256,6912]{1,0:T(8,128)(2,1)S(1)}, s32[256,32]{1,0:T(8,128)S(1)}) custom-call(bf16[256,256]{1,0:T(8,128)(2,1)S(1)} %collective-permute-done.partner, s32[27,1,256]{2,1,0:T(1,128)} %bitcast.22, bf16[256,256]{1,0:T(8,128)(2,1)} %bitcast.14), custom_call_target="tpu_custom_call" | custom-call | flops 1811939328 | bytes 1048576 | tf_op jit(solution)/shard_map/first_near/pallas_call | solution.py:184
  9.1 0.0 copy-start.4
  9.1 2.3 %first_far.1.here = bf16[272,256]{1,0:T(8,128)(2,1)S(1)} custom-call(s32[256,32]{1,0:T(8,128)S(1)} %get-tuple-element.15.local_ref, bf16[256,256]{1,0:T(8,128)(2,1)S(1)} %collective-permute-done.1.before, bf16[256,256]{1,0:T(8,128)(2,1)S(1)} %collective-permute-done.2.after, bf16[256,6912]{1,0:T(8,128)(2,1)S(1)} %get-tuple-element.17.near_ref, ...), custom_call_target="tpu_custom_call" | custom-call | flops 1811939328 | bytes 1048576 | tf_op jit(solution)/shard_map/first_far/pallas_call | solution.py:184
  11.4 0.0 copy-start.1
  11.4 0.0 copy-start.3
  11.5 0.0 copy-start.7
  11.5 5.3 %collective-permute-start.5 = (bf16[272,256]{1,0:T(8,128)(2,1)S(1)}, bf16[272,256]{1,0:T(8,128)(2,1)S(1)}, u32[]{:S(2)}, u32[]{:S(2)}) collective-permute-start(bf16[272,256]{1,0:T(8,128)(2,1)S(1)} %first_far.1.here), channel_id=1, source_target_pairs={{0,1},{1,0},{2,3},{3,2},{4,5},{5,4},{6,7},{7,6},{8,9},{9,8},{10,11... | collective-permute-start | bytes 417800 | tf_op jit(solution)/shard_map/ppermute | solution.py:34
  16.8 0.5 collective-permute-start.4
  17.3 4.6 %collective-permute-start.6 = (bf16[64,512]{1,0:T(8,128)(2,1)S(1)}, bf16[64,512]{1,0:T(8,128)(2,1)S(1)}, u32[]{:S(2)}, u32[]{:S(2)}) collective-permute-start(bf16[64,512]{1,0:T(8,128)(2,1)S(1)} %bitcast.16), channel_id=1, source_target_pairs={{0,63},{1,0},{2,1},{3,2},{4,3},{5,4},{6,5},{7,6},{8,7},{9,8},{10,9... | collective-permute-start | bytes 196616 | tf_op jit(solution)/shard_map/ppermute | solution.py:29
  22.0 2.1 %second_near.1.near_ref = bf16[256,6912]{1,0:T(8,128)(2,1)S(1)} custom-call(s32[256,32]{1,0:T(8,128)S(1)} %get-tuple-element.15.local_ref, bf16[272,256]{1,0:T(8,128)(2,1)S(1)} %first_far.1.here, bf16[272,256]{1,0:T(8,128)(2,1)S(1)} %collective-permute-done.5.partner), custom_call_target="tpu_custom_call" | custom-call | flops 1811939328 | bytes 1048576 | tf_op jit(solution)/shard_map/second_near/pallas_call | solution.py:184
  24.1 0.0 copy-start.2
  24.1 3.0 %second_far.1 = (bf16[256,256]{1,0:T(8,128)(2,1)}, f32[64,384]{1,0:T(8,128)S(1)}, f32[64,256]{1,0:T(8,128)S(1)}, bf16[128,256]{1,0:T(8,128)(2,1)S(1)}) custom-call(s32[256,32]{1,0:T(8,128)S(1)} %get-tuple-element.15.local_ref, bf16[272,256]{1,0:T(8,128)(2,1)S(1)} %collective-permute-done.3.before, bf16[272,256]{1,0:T(8,128)(2,1)S(1)} %collective-permute-done.4.after, ...), custom_call_target="tpu_custom_call" | custom-call | flops 1811939328 | bytes 1048576 | tf_op jit(solution)/shard_map/second_far/pallas_call | solution.py:184
  27.1 0.2 gradient.1
  27.4 13.9 %all_to_all.15 = bf16[32,8,512]{2,1,0:T(8,128)(2,1)S(1)} all-to-all(bf16[32,8,512]{2,1,0:T(8,128)(2,1)S(1)} %bitcast.9), channel_id=1, replica_groups=mesh['y'=4,'z'=8,'x'=4,'core'=2] {'y','x','core'}, dimensions={0} | all-to-all | bytes 524288 | tf_op jit(solution)/shard_map/all_to_all | solution.py:199
  41.4 15.5 %all_to_all.16 = f32[8,8,512]{2,1,0:T(8,128)S(1)} all-to-all(f32[8,8,512]{2,1,0:T(8,128)S(1)} %broadcast_in_dim.27), channel_id=1, replica_groups=mesh['y'=4,'z'=8,'x'=4,'core'=2] {'z'}, dimensions={0} | all-to-all | bytes 262144 | tf_op jit(solution)/shard_map/all_to_all | solution.py:199
  57.0 0.7 broadcast_in_dim.28
  57.7 5.4 %all-to-all-start.2 = ((bf16[32,8,512]{2,1,0:T(8,128)(2,1)}), bf16[32,8,512]{2,1,0:T(8,128)(2,1)S(1)}, u32[]{:S(2)}, u32[]{:S(2)}) async-start(bf16[32,8,512]{2,1,0:T(8,128)(2,1)} %broadcast_in_dim.28), calls=%async_computation.2 | async-start | bytes 524288 | tf_op jit(solution)/shard_map/all_to_all | solution.py:199
  63.0 1.7 %collective-permute-start.7 = (f32[64,256]{1,0:T(8,128)S(1)}, f32[64,256]{1,0:T(8,128)S(1)}, u32[]{:S(2)}, u32[]{:S(2)}) collective-permute-start(f32[64,256]{1,0:T(8,128)S(1)} %get-tuple-element.23), channel_id=1, source_target_pairs={{0,1},{1,2},{2,3},{3,4},{4,5},{5,6},{6,7},{7,8},{8,9},{9,10},{10,1... | collective-permute-start | bytes 196616 | tf_op jit(solution)/shard_map/ppermute | solution.py:29
  64.7 2.4 %collective-permute-done.7.moved_ref = f32[64,256]{1,0:T(8,128)S(1)} collective-permute-done((f32[64,256]{1,0:T(8,128)S(1)}, f32[64,256]{1,0:T(8,128)S(1)}, u32[]{:S(2)}, u32[]{:S(2)}) %collective-permute-start.7) | collective-permute-done | bytes 65568 | tf_op jit(solution)/shard_map/ppermute | solution.py:29
  67.2 5.3 %all-to-all-done.2 = bf16[32,8,512]{2,1,0:T(8,128)(2,1)S(1)} async-done(((bf16[32,8,512]{2,1,0:T(8,128)(2,1)}), bf16[32,8,512]{2,1,0:T(8,128)(2,1)S(1)}, u32[]{:S(2)}, u32[]{:S(2)}) %all-to-all-start.2) | async-done | bytes 262176 | tf_op jit(solution)/shard_map/all_to_all | solution.py:199
  72.4 0.9 %coarse_and_grad.1 = (bf16[64,512]{1,0:T(8,128)(2,1)}, f32[256,512]{1,0:T(8,128)}) custom-call(f32[64,384]{1,0:T(8,128)S(1)} %get-tuple-element.19.own_ref, f32[64,256]{1,0:T(8,128)S(1)} %collective-permute-done.7.moved_ref, bf16[256,512]{1,0:T(8,128)(2,1)S(1)} %copy-done.2, bf16[256,512]{1,0:T(8,128)(2,1)S(1)} %bitcast.10), custom_call_target="tpu_custom_call" | custom-call | bytes 1048576 | tf_op jit(solution)/shard_map/coarse_and_grad/pallas_call | solution.py:184
  (23 shorter events, 0.1 us)
Async XLA Ops:
  0.6 8.5 %copy-start.6 = (f32[256]{0:T(256)S(1)}, f32[256]{0:T(256)}, u32[]{:S(2)}) copy-start(f32[256]{0:T(256)} %param.14) | copy-start | bytes 3076
  0.6 8.5 %copy-start.5 = (s32[1,256]{1,0:T(1,128)S(1)}, s32[1,256]{1,0:T(1,128)}, u32[]{:S(2)}) copy-start(s32[1,256]{1,0:T(1,128)} %parent_ref.3) | copy-start | bytes 3076
  0.7 8.5 %copy-start = (bf16[27,256,256]{2,1,0:T(8,128)(2,1)S(1)}, bf16[27,256,256]{2,1,0:T(8,128)(2,1)}, u32[]{:S(2)}) copy-start(bf16[27,256,256]{2,1,0:T(8,128)(2,1)} %weight_ref.2) | copy-start | bytes 10616836
  0.7 4.5 %collective-permute-start = (bf16[256,256]{1,0:T(8,128)(2,1)}, bf16[256,256]{1,0:T(8,128)(2,1)S(1)}, u32[]{:S(2)}, u32[]{:S(2)}) collective-permute-start(bf16[256,256]{1,0:T(8,128)(2,1)} %bitcast.11), channel_id=1, source_target_pairs={{0,1},{1,0},{2,3},{3,2},{4,5},{5,4},{6,7},{7,6},{8,9},{9,8},{10,11... | collective-permute-start | bytes 393224 | tf_op jit(solution)/shard_map/ppermute | solution.py:34
  4.0 5.1 %collective-permute-start.1 = (bf16[256,256]{1,0:T(8,128)(2,1)}, bf16[256,256]{1,0:T(8,128)(2,1)S(1)}, u32[]{:S(2)}, u32[]{:S(2)}) collective-permute-start(bf16[256,256]{1,0:T(8,128)(2,1)} %bitcast.12), channel_id=1, source_target_pairs={{0,1},{1,2},{2,3},{3,4},{4,5},{5,6},{6,7},{7,8},{8,9},{9,10},{10,1... | collective-permute-start | bytes 393224 | tf_op jit(solution)/shard_map/ppermute | solution.py:29
  4.0 5.1 %collective-permute-start.2 = (bf16[256,256]{1,0:T(8,128)(2,1)}, bf16[256,256]{1,0:T(8,128)(2,1)S(1)}, u32[]{:S(2)}, u32[]{:S(2)}) collective-permute-start(bf16[256,256]{1,0:T(8,128)(2,1)} %bitcast.13), channel_id=1, source_target_pairs={{0,63},{1,0},{2,1},{3,2},{4,3},{5,4},{6,5},{7,6},{8,7},{9,8},{10,9... | collective-permute-start | bytes 393224 | tf_op jit(solution)/shard_map/ppermute | solution.py:29
  9.1 8.2 %copy-start.4 = (bf16[1,64,512]{2,1,0:T(8,128)(2,1)S(1)}, bf16[1,64,512]{2,1,0:T(8,128)(2,1)}, u32[]{:S(2)}) copy-start(bf16[1,64,512]{2,1,0:T(8,128)(2,1)} %param.17) | copy-start | bytes 196612
  11.4 12.6 %copy-start.1 = (bf16[27,256,256]{2,1,0:T(8,128)(2,1)S(1)}, bf16[27,256,256]{2,1,0:T(8,128)(2,1)}, u32[]{:S(2)}) copy-start(bf16[27,256,256]{2,1,0:T(8,128)(2,1)} %weight_ref.3) | copy-start | bytes 10616836
  11.4 12.6 %copy-start.3 = (bf16[1,256,256]{2,1,0:T(8,128)(2,1)S(1)}, bf16[1,256,256]{2,1,0:T(8,128)(2,1)}, u32[]{:S(2)}) copy-start(bf16[1,256,256]{2,1,0:T(8,128)(2,1)} %param.9) | copy-start | bytes 393220
  11.5 12.6 %copy-start.7 = (f32[256]{0:T(256)S(1)}, f32[256]{0:T(256)}, u32[]{:S(2)}) copy-start(f32[256]{0:T(256)} %param.15) | copy-start | bytes 3076
  11.5 10.5 %collective-permute-start.5 = (bf16[272,256]{1,0:T(8,128)(2,1)S(1)}, bf16[272,256]{1,0:T(8,128)(2,1)S(1)}, u32[]{:S(2)}, u32[]{:S(2)}) collective-permute-start(bf16[272,256]{1,0:T(8,128)(2,1)S(1)} %first_far.1.here), channel_id=1, source_target_pairs={{0,1},{1,0},{2,3},{3,2},{4,5},{5,4},{6,7},{7,6},{8,9},{9,8},{10,11... | collective-permute-start | bytes 417800 | tf_op jit(solution)/shard_map/ppermute | solution.py:34
  16.8 7.2 %collective-permute-start.3 = (bf16[272,256]{1,0:T(8,128)(2,1)S(1)}, bf16[272,256]{1,0:T(8,128)(2,1)S(1)}, u32[]{:S(2)}, u32[]{:S(2)}) collective-permute-start(bf16[272,256]{1,0:T(8,128)(2,1)S(1)} %first_far.1.here), channel_id=1, source_target_pairs={{0,1},{1,2},{2,3},{3,4},{4,5},{5,6},{6,7},{7,8},{8,9},{9,10},{10,1... | collective-permute-start | bytes 417800 | tf_op jit(solution)/shard_map/ppermute | solution.py:29
  16.8 7.3 %collective-permute-start.4 = (bf16[272,256]{1,0:T(8,128)(2,1)S(1)}, bf16[272,256]{1,0:T(8,128)(2,1)S(1)}, u32[]{:S(2)}, u32[]{:S(2)}) collective-permute-start(bf16[272,256]{1,0:T(8,128)(2,1)S(1)} %first_far.1.here), channel_id=1, source_target_pairs={{0,63},{1,0},{2,1},{3,2},{4,3},{5,4},{6,5},{7,6},{8,7},{9,8},{10,9... | collective-permute-start | bytes 417800 | tf_op jit(solution)/shard_map/ppermute | solution.py:29
  17.3 9.8 %collective-permute-start.6 = (bf16[64,512]{1,0:T(8,128)(2,1)S(1)}, bf16[64,512]{1,0:T(8,128)(2,1)S(1)}, u32[]{:S(2)}, u32[]{:S(2)}) collective-permute-start(bf16[64,512]{1,0:T(8,128)(2,1)S(1)} %bitcast.16), channel_id=1, source_target_pairs={{0,63},{1,0},{2,1},{3,2},{4,3},{5,4},{6,5},{7,6},{8,7},{9,8},{10,9... | collective-permute-start | bytes 196616 | tf_op jit(solution)/shard_map/ppermute | solution.py:29
  24.1 48.3 %copy-start.2 = (bf16[256,512]{1,0:T(8,128)(2,1)S(1)}, bf16[256,512]{1,0:T(8,128)(2,1)}, u32[]{:S(2)}) copy-start(bf16[256,512]{1,0:T(8,128)(2,1)} %down_ref.1) | copy-start | bytes 786436
  57.7 14.7 %all-to-all-start.2 = ((bf16[32,8,512]{2,1,0:T(8,128)(2,1)}), bf16[32,8,512]{2,1,0:T(8,128)(2,1)S(1)}, u32[]{:S(2)}, u32[]{:S(2)}) async-start(bf16[32,8,512]{2,1,0:T(8,128)(2,1)} %broadcast_in_dim.28), calls=%async_computation.2 | async-start | bytes 524288 | tf_op jit(solution)/shard_map/all_to_all | solution.py:199
  63.0 4.1 %collective-permute-start.7 = (f32[64,256]{1,0:T(8,128)S(1)}, f32[64,256]{1,0:T(8,128)S(1)}, u32[]{:S(2)}, u32[]{:S(2)}) collective-permute-start(f32[64,256]{1,0:T(8,128)S(1)} %get-tuple-element.23), channel_id=1, source_target_pairs={{0,1},{1,2},{2,3},{3,4},{4,5},{5,6},{6,7},{7,8},{8,9},{9,10},{10,1... | collective-permute-start | bytes 196616 | tf_op jit(solution)/shard_map/ppermute | solution.py:29

commit v14 on v12

--- a/solution.py
+++ b/solution.py
@@ -156,7 +156,7 @@
     count_after = jnp.maximum(tally_own[half:] + tally_after, 1.0)
     own_ref[:, :chans] = sums[:half]
     own_ref[:, chans:] = jnp.broadcast_to(count_own, (half, own_ref.shape[1] - chans))
-    sent_ref[...] = sums[half:]
+    sent_ref[...] = sums[half:].astype(sent_ref.dtype)
     shares = sums / jnp.concatenate([count_own, count_after], axis=0)
     share_ref[...] = shares.astype(share_ref.dtype)
 
@@ -172,7 +172,7 @@
     grad_ref[...] = gathered_ref[...].astype(grad_ref.dtype)
     chans = down_ref.shape[0]
     own = own_ref[...]
-    pooled = ((own[:, :chans] + moved_ref[...]) / own[:, chans : chans + 1]).astype(jnp.bfloat16)
+    pooled = ((own[:, :chans] + moved_ref[...].astype(jnp.float32)) / own[:, chans : chans + 1]).astype(jnp.bfloat16)
     coarse_ref[...] = jnp.dot(pooled, down_ref[...], preferred_element_type=jnp.float32).astype(coarse_ref.dtype)
 
 
@@ -269,7 +269,7 @@
         (
             bf16((rows, chans)),
             f32((par_rows, chans + 128)),
-            f32((par_rows, chans)),
+            bf16((par_rows, chans)),
             bf16((2 * par_rows, chans)),
         ),
         (

time: 73.6 us -> 73.5 us (level)
  no operation moved by 1% of the time
where the time goes in v14:
time: 73.5 us; the launch traced here: 73.2 us
  blocking collectives  29.5 us (40%)
  starting transfers between devices  21.4 us (29%)
  Pallas kernels  12.4 us (17%)
  waiting for transfers between devices  8.26 us (11%)
  between operations  0.83 us (1%)
  local copies, waits for them, and re-layouts  0.78 us (1%)
    all_to_all x2, blocking collectives, exchanged(): return lax.all_to_all(pieces, axes, 0, 0, tiled=True)  29.5 us
    pallas_call x6, Pallas kernels, in_vmem(): pl.pallas_call(kernel, out_shape=outs, in_specs=[vmem] * len(inputs) + [p...  12.4 us
    ppermute x2, starting transfers between devices, from_partner(): return lax.ppermute(array, SPACE, [(i, i ^ 1) for i in range(length)])  8.64 us
    ppermute x6, starting transfers between devices, shifted(): lax.ppermute(array, SPACE, [(i, (i + by) % length) for i in range(length)])  7.38 us
    all_to_all x1, waiting for transfers between devices, exchanged(): return lax.all_to_all(pieces, axes, 0, 0, tiled=True)  5.47 us
    all_to_all x1, starting transfers between devices, exchanged(): return lax.all_to_all(pieces, axes, 0, 0, tiled=True)  5.35 us
    ppermute x6, waiting for transfers between devices, shifted(): lax.ppermute(array, SPACE, [(i, (i + by) % length) for i in range(length)])  2.1 us
  transfers between devices with their start and end apart: 9, of which 3 were waited for; matrix products, arithmetic and copies ran while one was open for 0% of the time, Pallas kernels for 12%

profile of v14, /device:TPU:1, one launch (start us, length us, event | category | flops | bytes accessed | tf_op | source)
XLA Modules:
  0.0 73.2 jit_solution(1752647785078512077)
XLA Ops:
  0.7 3.3 %collective-permute-start = (bf16[256,256]{1,0:T(8,128)(2,1)}, bf16[256,256]{1,0:T(8,128)(2,1)S(1)}, u32[]{:S(2)}, u32[]{:S(2)}) collective-permute-start(bf16[256,256]{1,0:T(8,128)(2,1)} %bitcast.11), channel_id=1, source_target_pairs={{0,1},{1,0},{2,3},{3,2},{4,5},{5,4},{6,7},{7,6},{8,9},{9,8},{10,11... | collective-permute-start | bytes 393224 | tf_op jit(solution)/shard_map/ppermute | solution.py:34
  4.0 0.5 collective-permute-start.2
  4.5 0.7 collective-permute-done.partner
  5.2 3.9 %first_near.1 = (bf16[256,6912]{1,0:T(8,128)(2,1)S(1)}, s32[256,32]{1,0:T(8,128)S(1)}) custom-call(bf16[256,256]{1,0:T(8,128)(2,1)S(1)} %collective-permute-done.partner, s32[27,1,256]{2,1,0:T(1,128)} %bitcast.22, bf16[256,256]{1,0:T(8,128)(2,1)} %bitcast.14), custom_call_target="tpu_custom_call" | custom-call | flops 1811939328 | bytes 1048576 | tf_op jit(solution)/shard_map/first_near/pallas_call | solution.py:181
  9.1 0.0 copy-start.4
  9.1 2.3 %first_far.1.here = bf16[272,256]{1,0:T(8,128)(2,1)S(1)} custom-call(s32[256,32]{1,0:T(8,128)S(1)} %get-tuple-element.15.local_ref, bf16[256,256]{1,0:T(8,128)(2,1)S(1)} %collective-permute-done.1.before, bf16[256,256]{1,0:T(8,128)(2,1)S(1)} %collective-permute-done.2.after, bf16[256,6912]{1,0:T(8,128)(2,1)S(1)} %get-tuple-element.17.near_ref, ...), custom_call_target="tpu_custom_call" | custom-call | flops 1811939328 | bytes 1048576 | tf_op jit(solution)/shard_map/first_far/pallas_call | solution.py:181
  11.4 0.0 copy-start.1
  11.4 0.0 copy-start.3
  11.5 0.0 copy-start.7
  11.5 5.3 %collective-permute-start.5 = (bf16[272,256]{1,0:T(8,128)(2,1)S(1)}, bf16[272,256]{1,0:T(8,128)(2,1)S(1)}, u32[]{:S(2)}, u32[]{:S(2)}) collective-permute-start(bf16[272,256]{1,0:T(8,128)(2,1)S(1)} %first_far.1.here), channel_id=1, source_target_pairs={{0,1},{1,0},{2,3},{3,2},{4,5},{5,4},{6,7},{7,6},{8,9},{9,8},{10,11... | collective-permute-start | bytes 417800 | tf_op jit(solution)/shard_map/ppermute | solution.py:34
  16.8 0.5 collective-permute-start.4
  17.3 4.6 %collective-permute-start.6 = (bf16[64,512]{1,0:T(8,128)(2,1)S(1)}, bf16[64,512]{1,0:T(8,128)(2,1)S(1)}, u32[]{:S(2)}, u32[]{:S(2)}) collective-permute-start(bf16[64,512]{1,0:T(8,128)(2,1)S(1)} %bitcast.16), channel_id=1, source_target_pairs={{0,63},{1,0},{2,1},{3,2},{4,3},{5,4},{6,5},{7,6},{8,7},{9,8},{10,9... | collective-permute-start | bytes 196616 | tf_op jit(solution)/shard_map/ppermute | solution.py:29
  22.0 2.1 %second_near.1.near_ref = bf16[256,6912]{1,0:T(8,128)(2,1)S(1)} custom-call(s32[256,32]{1,0:T(8,128)S(1)} %get-tuple-element.15.local_ref, bf16[272,256]{1,0:T(8,128)(2,1)S(1)} %first_far.1.here, bf16[272,256]{1,0:T(8,128)(2,1)S(1)} %collective-permute-done.5.partner), custom_call_target="tpu_custom_call" | custom-call | flops 1811939328 | bytes 1048576 | tf_op jit(solution)/shard_map/second_near/pallas_call | solution.py:181
  24.1 0.0 copy-start.2
  24.1 3.0 %second_far.1 = (bf16[256,256]{1,0:T(8,128)(2,1)}, f32[64,384]{1,0:T(8,128)S(1)}, bf16[64,256]{1,0:T(8,128)(2,1)S(1)}, bf16[128,256]{1,0:T(8,128)(2,1)S(1)}) custom-call(s32[256,32]{1,0:T(8,128)S(1)} %get-tuple-element.15.local_ref, bf16[272,256]{1,0:T(8,128)(2,1)S(1)} %collective-permute-done.3.before, bf16[272,256]{1,0:T(8,128)(2,1)S(1)} %collective-permute-done.4.after, ...), custom_call_target="tpu_custom_call" | custom-call | flops 1811939328 | bytes 1048576 | tf_op jit(solution)/shard_map/second_far/pallas_call | solution.py:181
  27.1 0.2 gradient.1
  27.3 13.9 %all_to_all.15 = bf16[32,8,512]{2,1,0:T(8,128)(2,1)S(1)} all-to-all(bf16[32,8,512]{2,1,0:T(8,128)(2,1)S(1)} %bitcast.9), channel_id=1, replica_groups=mesh['y'=4,'z'=8,'x'=4,'core'=2] {'y','x','core'}, dimensions={0} | all-to-all | bytes 524288 | tf_op jit(solution)/shard_map/all_to_all | solution.py:194
  41.4 15.5 %all_to_all.16 = f32[8,8,512]{2,1,0:T(8,128)S(1)} all-to-all(f32[8,8,512]{2,1,0:T(8,128)S(1)} %broadcast_in_dim.27), channel_id=1, replica_groups=mesh['y'=4,'z'=8,'x'=4,'core'=2] {'z'}, dimensions={0} | all-to-all | bytes 262144 | tf_op jit(solution)/shard_map/all_to_all | solution.py:194
  56.9 0.7 broadcast_in_dim.28
  57.7 5.4 %all-to-all-start.2 = ((bf16[32,8,512]{2,1,0:T(8,128)(2,1)}), bf16[32,8,512]{2,1,0:T(8,128)(2,1)S(1)}, u32[]{:S(2)}, u32[]{:S(2)}) async-start(bf16[32,8,512]{2,1,0:T(8,128)(2,1)} %broadcast_in_dim.28), calls=%async_computation.2 | async-start | bytes 524288 | tf_op jit(solution)/shard_map/all_to_all | solution.py:194
  63.0 1.7 %collective-permute-start.7 = (bf16[64,256]{1,0:T(8,128)(2,1)S(1)}, bf16[64,256]{1,0:T(8,128)(2,1)S(1)}, u32[]{:S(2)}, u32[]{:S(2)}) collective-permute-start(bf16[64,256]{1,0:T(8,128)(2,1)S(1)} %get-tuple-element.23), channel_id=1, source_target_pairs={{0,1},{1,2},{2,3},{3,4},{4,5},{5,6},{6,7},{7,8},{8,9},{9,10},{10,1... | collective-permute-start | bytes 98312 | tf_op jit(solution)/shard_map/ppermute | solution.py:29
  64.7 2.1 %collective-permute-done.7.moved_ref = bf16[64,256]{1,0:T(8,128)(2,1)S(1)} collective-permute-done((bf16[64,256]{1,0:T(8,128)(2,1)S(1)}, bf16[64,256]{1,0:T(8,128)(2,1)S(1)}, u32[]{:S(2)}, u32[]{:S(2)}) %collective-permute-start.7) | collective-permute-done | bytes 32800 | tf_op jit(solution)/shard_map/ppermute | solution.py:29
  66.8 5.5 %all-to-all-done.2 = bf16[32,8,512]{2,1,0:T(8,128)(2,1)S(1)} async-done(((bf16[32,8,512]{2,1,0:T(8,128)(2,1)}), bf16[32,8,512]{2,1,0:T(8,128)(2,1)S(1)}, u32[]{:S(2)}, u32[]{:S(2)}) %all-to-all-start.2) | async-done | bytes 262176 | tf_op jit(solution)/shard_map/all_to_all | solution.py:194
  72.3 0.9 %coarse_and_grad.1 = (bf16[64,512]{1,0:T(8,128)(2,1)}, f32[256,512]{1,0:T(8,128)}) custom-call(f32[64,384]{1,0:T(8,128)S(1)} %get-tuple-element.19.own_ref, bf16[64,256]{1,0:T(8,128)(2,1)S(1)} %collective-permute-done.7.moved_ref, bf16[256,512]{1,0:T(8,128)(2,1)S(1)} %copy-done.2, bf16[256,512]{1,0:T(8,128)(2,1)S(1)} %bitcast.10), custom_call_target="tpu_custom_call" | custom-call | bytes 1048576 | tf_op jit(solution)/shard_map/coarse_and_grad/pallas_call | solution.py:181
  (23 shorter events, 0.1 us)
Async XLA Ops:
  0.6 8.5 %copy-start.6 = (f32[256]{0:T(256)S(1)}, f32[256]{0:T(256)}, u32[]{:S(2)}) copy-start(f32[256]{0:T(256)} %param.14) | copy-start | bytes 3076
  0.6 8.5 %copy-start.5 = (s32[1,256]{1,0:T(1,128)S(1)}, s32[1,256]{1,0:T(1,128)}, u32[]{:S(2)}) copy-start(s32[1,256]{1,0:T(1,128)} %parent_ref.3) | copy-start | bytes 3076
  0.7 8.5 %copy-start = (bf16[27,256,256]{2,1,0:T(8,128)(2,1)S(1)}, bf16[27,256,256]{2,1,0:T(8,128)(2,1)}, u32[]{:S(2)}) copy-start(bf16[27,256,256]{2,1,0:T(8,128)(2,1)} %weight_ref.2) | copy-start | bytes 10616836
  0.7 4.5 %collective-permute-start = (bf16[256,256]{1,0:T(8,128)(2,1)}, bf16[256,256]{1,0:T(8,128)(2,1)S(1)}, u32[]{:S(2)}, u32[]{:S(2)}) collective-permute-start(bf16[256,256]{1,0:T(8,128)(2,1)} %bitcast.11), channel_id=1, source_target_pairs={{0,1},{1,0},{2,3},{3,2},{4,5},{5,4},{6,7},{7,6},{8,9},{9,8},{10,11... | collective-permute-start | bytes 393224 | tf_op jit(solution)/shard_map/ppermute | solution.py:34
  4.0 5.1 %collective-permute-start.1 = (bf16[256,256]{1,0:T(8,128)(2,1)}, bf16[256,256]{1,0:T(8,128)(2,1)S(1)}, u32[]{:S(2)}, u32[]{:S(2)}) collective-permute-start(bf16[256,256]{1,0:T(8,128)(2,1)} %bitcast.12), channel_id=1, source_target_pairs={{0,1},{1,2},{2,3},{3,4},{4,5},{5,6},{6,7},{7,8},{8,9},{9,10},{10,1... | collective-permute-start | bytes 393224 | tf_op jit(solution)/shard_map/ppermute | solution.py:29
  4.0 5.1 %collective-permute-start.2 = (bf16[256,256]{1,0:T(8,128)(2,1)}, bf16[256,256]{1,0:T(8,128)(2,1)S(1)}, u32[]{:S(2)}, u32[]{:S(2)}) collective-permute-start(bf16[256,256]{1,0:T(8,128)(2,1)} %bitcast.13), channel_id=1, source_target_pairs={{0,63},{1,0},{2,1},{3,2},{4,3},{5,4},{6,5},{7,6},{8,7},{9,8},{10,9... | collective-permute-start | bytes 393224 | tf_op jit(solution)/shard_map/ppermute | solution.py:29
  9.1 8.2 %copy-start.4 = (bf16[1,64,512]{2,1,0:T(8,128)(2,1)S(1)}, bf16[1,64,512]{2,1,0:T(8,128)(2,1)}, u32[]{:S(2)}) copy-start(bf16[1,64,512]{2,1,0:T(8,128)(2,1)} %param.17) | copy-start | bytes 196612
  11.4 12.6 %copy-start.1 = (bf16[27,256,256]{2,1,0:T(8,128)(2,1)S(1)}, bf16[27,256,256]{2,1,0:T(8,128)(2,1)}, u32[]{:S(2)}) copy-start(bf16[27,256,256]{2,1,0:T(8,128)(2,1)} %weight_ref.3) | copy-start | bytes 10616836
  11.4 12.6 %copy-start.3 = (bf16[1,256,256]{2,1,0:T(8,128)(2,1)S(1)}, bf16[1,256,256]{2,1,0:T(8,128)(2,1)}, u32[]{:S(2)}) copy-start(bf16[1,256,256]{2,1,0:T(8,128)(2,1)} %param.9) | copy-start | bytes 393220
  11.5 12.6 %copy-start.7 = (f32[256]{0:T(256)S(1)}, f32[256]{0:T(256)}, u32[]{:S(2)}) copy-start(f32[256]{0:T(256)} %param.15) | copy-start | bytes 3076
  11.5 10.5 %collective-permute-start.5 = (bf16[272,256]{1,0:T(8,128)(2,1)S(1)}, bf16[272,256]{1,0:T(8,128)(2,1)S(1)}, u32[]{:S(2)}, u32[]{:S(2)}) collective-permute-start(bf16[272,256]{1,0:T(8,128)(2,1)S(1)} %first_far.1.here), channel_id=1, source_target_pairs={{0,1},{1,0},{2,3},{3,2},{4,5},{5,4},{6,7},{7,6},{8,9},{9,8},{10,11... | collective-permute-start | bytes 417800 | tf_op jit(solution)/shard_map/ppermute | solution.py:34
  16.8 7.2 %collective-permute-start.3 = (bf16[272,256]{1,0:T(8,128)(2,1)S(1)}, bf16[272,256]{1,0:T(8,128)(2,1)S(1)}, u32[]{:S(2)}, u32[]{:S(2)}) collective-permute-start(bf16[272,256]{1,0:T(8,128)(2,1)S(1)} %first_far.1.here), channel_id=1, source_target_pairs={{0,1},{1,2},{2,3},{3,4},{4,5},{5,6},{6,7},{7,8},{8,9},{9,10},{10,1... | collective-permute-start | bytes 417800 | tf_op jit(solution)/shard_map/ppermute | solution.py:29
  16.8 7.3 %collective-permute-start.4 = (bf16[272,256]{1,0:T(8,128)(2,1)S(1)}, bf16[272,256]{1,0:T(8,128)(2,1)S(1)}, u32[]{:S(2)}, u32[]{:S(2)}) collective-permute-start(bf16[272,256]{1,0:T(8,128)(2,1)S(1)} %first_far.1.here), channel_id=1, source_target_pairs={{0,63},{1,0},{2,1},{3,2},{4,3},{5,4},{6,5},{7,6},{8,7},{9,8},{10,9... | collective-permute-start | bytes 417800 | tf_op jit(solution)/shard_map/ppermute | solution.py:29
  17.3 9.8 %collective-permute-start.6 = (bf16[64,512]{1,0:T(8,128)(2,1)S(1)}, bf16[64,512]{1,0:T(8,128)(2,1)S(1)}, u32[]{:S(2)}, u32[]{:S(2)}) collective-permute-start(bf16[64,512]{1,0:T(8,128)(2,1)S(1)} %bitcast.16), channel_id=1, source_target_pairs={{0,63},{1,0},{2,1},{3,2},{4,3},{5,4},{6,5},{7,6},{8,7},{9,8},{10,9... | collective-permute-start | bytes 196616 | tf_op jit(solution)/shard_map/ppermute | solution.py:29
  24.1 48.2 %copy-start.2 = (bf16[256,512]{1,0:T(8,128)(2,1)S(1)}, bf16[256,512]{1,0:T(8,128)(2,1)}, u32[]{:S(2)}) copy-start(bf16[256,512]{1,0:T(8,128)(2,1)} %down_ref.1) | copy-start | bytes 786436
  57.7 14.6 %all-to-all-start.2 = ((bf16[32,8,512]{2,1,0:T(8,128)(2,1)}), bf16[32,8,512]{2,1,0:T(8,128)(2,1)S(1)}, u32[]{:S(2)}, u32[]{:S(2)}) async-start(bf16[32,8,512]{2,1,0:T(8,128)(2,1)} %broadcast_in_dim.28), calls=%async_computation.2 | async-start | bytes 524288 | tf_op jit(solution)/shard_map/all_to_all | solution.py:194
  63.0 3.8 %collective-permute-start.7 = (bf16[64,256]{1,0:T(8,128)(2,1)S(1)}, bf16[64,256]{1,0:T(8,128)(2,1)S(1)}, u32[]{:S(2)}, u32[]{:S(2)}) collective-permute-start(bf16[64,256]{1,0:T(8,128)(2,1)S(1)} %get-tuple-element.23), channel_id=1, source_target_pairs={{0,1},{1,2},{2,3},{3,4},{4,5},{5,6},{6,7},{7,8},{8,9},{9,10},{10,1... | collective-permute-start | bytes 98312 | tf_op jit(solution)/shard_map/ppermute | solution.py:29
